TPU v7x, 32 devices: a whole 2x2x4 slice. The times are simulated.
32 devices in a mesh: group: 2 (over y), ctx: 16 (over z, x, core).
Axes of the slice: x: 2, y: 2, z: 4, core: 2. Of those that a mesh axis runs over, the one named last changes fastest.
Arguments:
- queries: bfloat16 [4096, 8192], P(('group', 'ctx')), parts along dimension 0, may hold values from -5 to 5
- keys: bfloat16 [4096, 512], P(('group', 'ctx')), parts along dimension 0, may hold values from -5 to 5
- values: bfloat16 [4096, 512], P(('group', 'ctx')), parts along dimension 0, may hold values from -6 to 6
- outputs: bfloat16 [4096, 8192], P(('group', 'ctx')), parts along dimension 0, may hold values from -6 to 6
- d_out: bfloat16 [4096, 8192], P(('group', 'ctx')), parts along dimension 0, may hold values from -6 to 6
- lengths: int32 [16], P('group'), parts along dimension 0, may hold values from 1 to 512, 2048 in all
Outputs:
- d_queries: bfloat16 [4096, 8192], P(('group', 'ctx')), parts along dimension 0
- d_keys: bfloat16 [4096, 512], P(('group', 'ctx')), parts along dimension 0
- d_values: bfloat16 [4096, 512], P(('group', 'ctx')), parts along dimension 0
There are 2 independent parts, one for each index of `group`. A program takes and returns all parts, laid end to end along the dimension named above; each array names one. Nothing has to cross between parts.
Inputs may be any that keep to these rules, and one draw needn't show every extreme that they name: Each document is at most 512 tokens long, and one document in every draw is exactly that long; the lengths sum to 2048.
All inputs are finite; a program needn't handle non-finite values.
Results may differ from a plain program's by a relative error of at most 0.0049.
Values may be sent and summed in bfloat16 or wider, within the bound.
No kernel may reach another device: no remote copies, remote signals or barrier semaphores. Data moves between devices by JAX's collectives and lax.ppermute only.
A program may use at most 128 MiB of HBM per device.

v0:
```python
import math

import jax
import jax.numpy as jnp
from jax import lax
from jax.sharding import PartitionSpec as P

HQ = 64
HK = 4
HD = 128
SPAN = 4


def shifted(x, axis, by):
    size = lax.axis_size(axis)
    pairs = [(i, i + by) for i in range(size) if 0 <= i + by < size]
    return lax.ppermute(x, axis, pairs)


def doc_index(ends, positions):
    return jnp.sum((ends[None, :] <= positions[:, None]).astype(jnp.int32), axis=1)


def on_device(queries, keys, values, outputs, d_out, lengths):
    rows = queries.shape[0]
    per_kv = HQ // HK
    factor = 1.0 / math.sqrt(HD)
    place = lax.axis_index("ctx")
    ends = jnp.cumsum(lengths)
    local_rows = jnp.arange(rows, dtype=jnp.int32)
    query_pos = place * rows + local_rows
    query_doc = doc_index(ends, query_pos)
    query_four = queries.reshape(rows, HK, per_kv, HD)
    grad_four = d_out.reshape(rows, HK, per_kv, HD)
    output_four = outputs.reshape(rows, HK, per_kv, HD)
    key_three = keys.reshape(rows, HK, HD)
    value_three = values.reshape(rows, HK, HD)
    delta = jnp.einsum("tkgd,tkgd->kgt", grad_four, output_four, preferred_element_type=jnp.float32)

    def visibility(distance):
        key_pos = (place - distance) * rows + local_rows
        visible = (key_pos[None, :] <= query_pos[:, None]) & (key_pos[None, :] >= 0)
        return visible & (query_doc[:, None] == doc_index(ends, key_pos)[None, :])

    def tile_scores(key_block):
        return (
            jnp.einsum("tkgd,ukd->kgtu", query_four, key_block, preferred_element_type=jnp.float32)
            * factor
        )

    def stats_step(state, key_block, distance):
        visible = visibility(distance)
        row_top, total = state
        scores = jnp.where(visible, tile_scores(key_block), -jnp.inf)
        new_top = jnp.maximum(row_top, jnp.max(scores, axis=-1))
        total = total * jnp.exp(row_top - new_top) + jnp.sum(
            jnp.exp(scores - new_top[..., None]), axis=-1
        )
        return (new_top, total)

    start_top = jnp.full((HK, per_kv, rows), -jnp.inf, jnp.float32)
    start_total = jnp.zeros((HK, per_kv, rows), jnp.float32)
    state = stats_step((start_top, start_total), key_three, 0)
    stored_keys = jnp.zeros((SPAN, rows, HK, HD), keys.dtype)
    stored_values = jnp.zeros((SPAN, rows, HK, HD), values.dtype)

    def relay_keys(distance, carry):
        current, cur_values, inner, kept, kept_values = carry
        current = shifted(current, "ctx", 1)
        cur_values = shifted(cur_values, "ctx", 1)
        kept = lax.dynamic_update_index_in_dim(kept, current, distance - 1, 0)
        kept_values = lax.dynamic_update_index_in_dim(kept_values, cur_values, distance - 1, 0)
        return (current, cur_values, stats_step(inner, current, distance), kept, kept_values)

    _, _, state, stored_keys, stored_values = lax.fori_loop(
        1, SPAN + 1, relay_keys, (key_three, value_three, state, stored_keys, stored_values)
    )
    log_total = state[0] + jnp.log(state[1])
    zero_pair = jnp.zeros((rows, HK, HD), jnp.float32)

    def grad_tile(key_block, value_block, distance):
        visible = visibility(distance)
        scores = tile_scores(key_block)
        probs = jnp.where(
            visible, jnp.exp(jnp.where(visible, scores - log_total[..., None], 0.0)), 0.0
        )
        grad_probs = jnp.einsum(
            "tkgd,ukd->kgtu", grad_four, value_block, preferred_element_type=jnp.float32
        )
        grad_scores = (factor * probs * (grad_probs - delta[..., None])).astype(jnp.bfloat16)
        part_query = jnp.einsum(
            "kgtu,ukd->tkgd", grad_scores, key_block, preferred_element_type=jnp.float32
        )
        part_key = jnp.einsum(
            "kgtu,tkgd->ukd", grad_scores, query_four, preferred_element_type=jnp.float32
        )
        part_value = jnp.einsum(
            "kgtu,tkgd->ukd",
            probs.astype(jnp.bfloat16),
            grad_four,
            preferred_element_type=jnp.float32,
        )
        return (part_query, part_key, part_value)

    grad_query, grad_key, grad_value = grad_tile(key_three, value_three, 0)

    def relay_grads(step, carry):
        sum_keys, sum_values, query_sum = carry
        distance = SPAN - step
        key_block = lax.dynamic_index_in_dim(stored_keys, distance - 1, 0, keepdims=False)
        value_block = lax.dynamic_index_in_dim(stored_values, distance - 1, 0, keepdims=False)
        part_query, part_key, part_value = grad_tile(key_block, value_block, distance)
        sum_keys, sum_values = shifted((sum_keys + part_key, sum_values + part_value), "ctx", -1)
        return (sum_keys, sum_values, query_sum + part_query)

    carried = lax.fori_loop(0, SPAN, relay_grads, (zero_pair, zero_pair, grad_query))
    grad_query = carried[2]
    grad_key = grad_key + carried[0]
    grad_value = grad_value + carried[1]
    d_queries = grad_query.astype(jnp.bfloat16).reshape(rows, HQ * HD)
    d_keys = grad_key.astype(jnp.bfloat16).reshape(rows, HK * HD)
    d_values = grad_value.astype(jnp.bfloat16).reshape(rows, HK * HD)
    return (d_queries, d_keys, d_values)


def solution(mesh):
    placed = (
        P(("group", "ctx"), None),
        P(("group", "ctx"), None),
        P(("group", "ctx"), None),
        P(("group", "ctx"), None),
        P(("group", "ctx"), None),
        P("group"),
    )
    return jax.shard_map(
        on_device,
        mesh=mesh,
        in_specs=placed,
        out_specs=(P(("group", "ctx"), None), P(("group", "ctx"), None), P(("group", "ctx"), None)),
        check_vma=False,
    )
```

profile of v0, /device:TPU:25, one launch (start us, length us, event | category | flops | bytes accessed | tf_op | source)
XLA Modules:
  0.0 192.0 jit_solution(11426296946453427224)
XLA Ops:
  6.3 3.2 %copy.59 = bf16[128,8192]{0,1:T(8,128)(2,1)S(1)} copy(bf16[128,8192]{1,0:T(8,128)(2,1)} %param.14) | data formatting | bytes 4194304 | tf_op args[4]
  9.5 2.7 %copy.67 = bf16[128,4,16,128]{3,0,2,1:T(8,128)(2,1)} copy(bf16[128,4,16,128]{0,3,2,1:T(8,128)(2,1)S(1)} %bitcast.206) | data formatting | bytes 4194304
  12.2 4.1 %copy.53 = bf16[128,8192]{0,1:T(8,128)(2,1)} copy(bf16[128,8192]{1,0:T(8,128)(2,1)} %param.10) | data formatting | bytes 4194304 | tf_op args[0]
  16.3 3.0 %copy.58 = bf16[128,4,16,128]{3,0,2,1:T(8,128)(2,1)S(1)} copy(bf16[128,4,16,128]{0,3,2,1:T(8,128)(2,1)} %bitcast.203) | data formatting | bytes 4194304
  19.3 3.5 %copy.110 = bf16[16,8,64,128]{3,2,1,0:T(8,128)(2,1)} copy(bf16[16,8,64,128]{3,1,2,0:T(8,128)(2,1)} %bitcast.215) | data formatting | bytes 4194304
  22.9 4.9 %copy.91 = f32[4,16,128,128]{3,1,0,2:T(8,128)} copy(bf16[4,16,128,128]{2,3,1,0:T(8,128)(2,1)} %bitcast.207) | data formatting | bytes 6291456
  27.8 4.1 %multiply_reduce_fusion = f32[4,16,128]{1,0,2:T(4,128)S(1)} fusion(f32[4,16,128,128]{3,1,0,2:T(8,128)} %copy.91, bf16[128,4,16,128]{3,2,1,0:T(8,128)(2,1)} %bitcast.210), kind=kLoop, calls=%fused_computation.56 | loop fusion | flops 3137536 | bytes 6324224
  38.1 43.6 %while.50 = (s32[]{:T(128)}, bf16[128,4,128]{2,0,1:T(8,128)(2,1)S(1)}, bf16[128,4,128]{2,1,0:T(4,128)(2,1)S(1)}, f32[4,16,128]{2,1,0:T(8,128)S(1)}, f32[4,16,128...) while((s32[]{:T(128)}, ...), condition=%wide.region_8.9_spmd.clone, body=%wide.region_4.0_spmd.clone.sunk | while | flops 275860864 | bytes 13193769 | solution.py:75
  38.1 3.7 %collective-permute-start.1 = (bf16[128,4,128]{2,1,0:T(4,128)(2,1)S(1)}, bf16[128,4,128]{2,1,0:T(4,128)(2,1)S(1)}, u32[]{:S(2)}, u32[]{:S(2)}) collective-permute-start(bf16[128,4,128]{2,1,0:T(4,128)(2,1)S(1)} %get-tuple-element.1264), channel_id=1, source_target_pairs={{0,1},{1,2},{2,3},{3,4},{4,5},{5,6},{6,7},{7,8},{8,9},{9,10},{10,1... | collective-permute-start | bytes 393224 | tf_op jit(solution)/shard_map/while/body/eval_jaxpr/ppermute | solution.py:17
  48.4 4.4 %collective-permute-start.1 = (bf16[128,4,128]{2,1,0:T(4,128)(2,1)S(1)}, bf16[128,4,128]{2,1,0:T(4,128)(2,1)S(1)}, u32[]{:S(2)}, u32[]{:S(2)}) collective-permute-start(bf16[128,4,128]{2,1,0:T(4,128)(2,1)S(1)} %get-tuple-element.1264), channel_id=1, source_target_pairs={{0,1},{1,2},{2,3},{3,4},{4,5},{5,6},{6,7},{7,8},{8,9},{9,10},{10,1... | collective-permute-start | bytes 393224 | tf_op jit(solution)/shard_map/while/body/eval_jaxpr/ppermute | solution.py:17
  59.3 4.3 %collective-permute-start.1 = (bf16[128,4,128]{2,1,0:T(4,128)(2,1)S(1)}, bf16[128,4,128]{2,1,0:T(4,128)(2,1)S(1)}, u32[]{:S(2)}, u32[]{:S(2)}) collective-permute-start(bf16[128,4,128]{2,1,0:T(4,128)(2,1)S(1)} %get-tuple-element.1264), channel_id=1, source_target_pairs={{0,1},{1,2},{2,3},{3,4},{4,5},{5,6},{6,7},{7,8},{8,9},{9,10},{10,1... | collective-permute-start | bytes 393224 | tf_op jit(solution)/shard_map/while/body/eval_jaxpr/ppermute | solution.py:17
  70.3 4.4 %collective-permute-start.1 = (bf16[128,4,128]{2,1,0:T(4,128)(2,1)S(1)}, bf16[128,4,128]{2,1,0:T(4,128)(2,1)S(1)}, u32[]{:S(2)}, u32[]{:S(2)}) collective-permute-start(bf16[128,4,128]{2,1,0:T(4,128)(2,1)S(1)} %get-tuple-element.1264), channel_id=1, source_target_pairs={{0,1},{1,2},{2,3},{3,4},{4,5},{5,6},{6,7},{7,8},{8,9},{9,10},{10,1... | collective-permute-start | bytes 393224 | tf_op jit(solution)/shard_map/while/body/eval_jaxpr/ppermute | solution.py:17
  81.8 4.5 %fusion.37 = bf16[4,16,128,128]{2,3,1,0:T(8,128)(2,1)S(1)} fusion(f32[4,128,128,16]{2,1,3,0:T(8,128)} %copy-done.3, bf16[128,4,16,128]{0,3,2,1:T(8,128)(2,1)} %bitcast.208, f32[4,16,128]{2,1,0:T(8,128)} %copy.92, f32[4,16,128]{2,1,0:T(8,128)S(1)} %log_add_fusion, pred[128,128]{0,1:T(8,128)(4,1)S(1)} %compare_and_fusion.2, ...), kind=kOutput, calls=%fused_computation.50 | convolution fusion | flops 276824064 | bytes 8601600 | tf_op jit(solution)/shard_map/tkgd,ukd->kgtu/dot_general | solution.py:87
  87.6 2.9 %convolution_bitcast_fusion.1 = f32[128,4,16,128]{3,0,2,1:T(8,128)} fusion(bf16[4,16,128,128]{2,3,1,0:T(8,128)(2,1)S(1)} %fusion.37, bf16[128,4,128,1]{0,2,3,1:T(8,128)(2,1)S(1)} %bitcast.214), kind=kOutput, calls=%fused_computation.60 | convolution fusion | flops 268435456 | bytes 6422528 | tf_op jit(solution)/shard_map/kgtu,ukd->tkgd/dot_general | solution.py:91
  90.4 5.4 %copy.64 = f32[128,4,16,128]{0,3,2,1:T(8,128)} copy(f32[128,4,16,128]{3,0,2,1:T(8,128)} %convolution_bitcast_fusion.1) | data formatting | bytes 8388608
  95.9 79.8 %while.51 = (s32[]{:T(128)}, f32[128,4,128]{2,0,1:T(8,128)S(1)}, f32[128,4,128]{2,0,1:T(8,128)S(1)}, f32[128,4,16,128]{0,3,2,1:T(8,128)}, s32[]{:T(128)}, /*inde...) while((s32[]{:T(128)}, f32[128,4,128]{2,0,1:T(8,128)S(1)}, ...), condition=%wide.region_11.12_spmd.clone, body=%wide.region_9.11_spmd.clone.sunk | while | flops 1357057408 | bytes 56382152 | solution.py:116
  99.4 2.4 %fusion.102 = bf16[4,16,128,128]{2,3,1,0:T(8,128)(2,1)S(1)} fusion(f32[4,128,128,16]{2,1,3,0:T(8,128)S(1)} %fusion.101, bf16[128,4,16,128]{3,0,2,1:T(8,128)(2,1)S(1)} %copy-done.5, f32[4,16,128]{2,1,0:T(8,128)} %get-tuple-element.1342, f32[4,16,128]{2,1,0:T(8,128)S(1)} %get-tuple-element.1339, pred[128,128]{0,1:T(8,128)(4,1)S(1)} %compare_and_fusion.6, ...), kind=kOutput, calls=%fused_computation.20.clone.1 | convolution fusion | flops 276824064 | bytes 8601600 | tf_op jit(solution)/shard_map/while/body/eval_jaxpr/tkgd,ukd->kgtu/dot_general | solution.py:87
  102.5 6.3 %collective-permute-start.2 = (f32[128,4,128]{2,0,1:T(8,128)S(1)}, f32[128,4,128]{2,0,1:T(8,128)S(1)}, u32[]{:S(2)}, u32[]{:S(2)}) collective-permute-start(f32[128,4,128]{2,0,1:T(8,128)S(1)} %fusion.103), channel_id=1, source_target_pairs={{1,0},{2,1},{3,2},{4,3},{5,4},{6,5},{7,6},{8,7},{9,8},{10,9},{11,1... | collective-permute-start | bytes 786440 | tf_op jit(solution)/shard_map/while/body/eval_jaxpr/ppermute | solution.py:17
  112.5 5.6 %bitcast_add_fusion.2 = f32[128,4,16,128]{0,3,2,1:T(8,128)} fusion(f32[128,4,16,128]{0,3,2,1:T(8,128)} %get-tuple-element.1313, bf16[4,16,128,128]{2,3,1,0:T(8,128)(2,1)} %copy-done, bf16[4,128,4,128]{3,1,2,0:T(8,128)(2,1)S(1)} %get-tuple-element.1337, s32[]{:T(128)S(6)} %select_n.161), kind=kOutput, calls=%fused_computation.17.clone.1 | convolution fusion | flops 269484032 | bytes 10616836 | tf_op jit(solution)/shard_map/while/body/eval_jaxpr/kgtu,ukd->tkgd/dot_general | solution.py:91
  121.8 2.4 %fusion.102 = bf16[4,16,128,128]{2,3,1,0:T(8,128)(2,1)S(1)} fusion(f32[4,128,128,16]{2,1,3,0:T(8,128)S(1)} %fusion.101, bf16[128,4,16,128]{3,0,2,1:T(8,128)(2,1)S(1)} %copy-done.5, f32[4,16,128]{2,1,0:T(8,128)} %get-tuple-element.1342, f32[4,16,128]{2,1,0:T(8,128)S(1)} %get-tuple-element.1339, pred[128,128]{0,1:T(8,128)(4,1)S(1)} %compare_and_fusion.6, ...), kind=kOutput, calls=%fused_computation.20.clone.1 | convolution fusion | flops 276824064 | bytes 8601600 | tf_op jit(solution)/shard_map/while/body/eval_jaxpr/tkgd,ukd->kgtu/dot_general | solution.py:87
  128.7 2.8 %collective-permute-start.3 = (f32[128,4,128]{2,0,1:T(8,128)}, f32[128,4,128]{2,0,1:T(8,128)S(1)}, u32[]{:S(2)}, u32[]{:S(2)}) collective-permute-start(f32[128,4,128]{2,0,1:T(8,128)} %fusion.104), channel_id=1, source_target_pairs={{1,0},{2,1},{3,2},{4,3},{5,4},{6,5},{7,6},{8,7},{9,8},{10,9},{11,1... | collective-permute-start | bytes 786440 | tf_op jit(solution)/shard_map/while/body/eval_jaxpr/ppermute | solution.py:17
  131.5 5.6 %bitcast_add_fusion.2 = f32[128,4,16,128]{0,3,2,1:T(8,128)} fusion(f32[128,4,16,128]{0,3,2,1:T(8,128)} %get-tuple-element.1313, bf16[4,16,128,128]{2,3,1,0:T(8,128)(2,1)} %copy-done, bf16[4,128,4,128]{3,1,2,0:T(8,128)(2,1)S(1)} %get-tuple-element.1337, s32[]{:T(128)S(6)} %select_n.161), kind=kOutput, calls=%fused_computation.17.clone.1 | convolution fusion | flops 269484032 | bytes 10616836 | tf_op jit(solution)/shard_map/while/body/eval_jaxpr/kgtu,ukd->tkgd/dot_general | solution.py:91
  140.4 2.4 %fusion.102 = bf16[4,16,128,128]{2,3,1,0:T(8,128)(2,1)S(1)} fusion(f32[4,128,128,16]{2,1,3,0:T(8,128)S(1)} %fusion.101, bf16[128,4,16,128]{3,0,2,1:T(8,128)(2,1)S(1)} %copy-done.5, f32[4,16,128]{2,1,0:T(8,128)} %get-tuple-element.1342, f32[4,16,128]{2,1,0:T(8,128)S(1)} %get-tuple-element.1339, pred[128,128]{0,1:T(8,128)(4,1)S(1)} %compare_and_fusion.6, ...), kind=kOutput, calls=%fused_computation.20.clone.1 | convolution fusion | flops 276824064 | bytes 8601600 | tf_op jit(solution)/shard_map/while/body/eval_jaxpr/tkgd,ukd->kgtu/dot_general | solution.py:87
  143.5 2.7 %collective-permute-start.2 = (f32[128,4,128]{2,0,1:T(8,128)S(1)}, f32[128,4,128]{2,0,1:T(8,128)S(1)}, u32[]{:S(2)}, u32[]{:S(2)}) collective-permute-start(f32[128,4,128]{2,0,1:T(8,128)S(1)} %fusion.103), channel_id=1, source_target_pairs={{1,0},{2,1},{3,2},{4,3},{5,4},{6,5},{7,6},{8,7},{9,8},{10,9},{11,1... | collective-permute-start | bytes 786440 | tf_op jit(solution)/shard_map/while/body/eval_jaxpr/ppermute | solution.py:17
  148.0 3.2 %collective-permute-start.3 = (f32[128,4,128]{2,0,1:T(8,128)}, f32[128,4,128]{2,0,1:T(8,128)S(1)}, u32[]{:S(2)}, u32[]{:S(2)}) collective-permute-start(f32[128,4,128]{2,0,1:T(8,128)} %fusion.104), channel_id=1, source_target_pairs={{1,0},{2,1},{3,2},{4,3},{5,4},{6,5},{7,6},{8,7},{9,8},{10,9},{11,1... | collective-permute-start | bytes 786440 | tf_op jit(solution)/shard_map/while/body/eval_jaxpr/ppermute | solution.py:17
  151.2 5.6 %bitcast_add_fusion.2 = f32[128,4,16,128]{0,3,2,1:T(8,128)} fusion(f32[128,4,16,128]{0,3,2,1:T(8,128)} %get-tuple-element.1313, bf16[4,16,128,128]{2,3,1,0:T(8,128)(2,1)} %copy-done, bf16[4,128,4,128]{3,1,2,0:T(8,128)(2,1)S(1)} %get-tuple-element.1337, s32[]{:T(128)S(6)} %select_n.161), kind=kOutput, calls=%fused_computation.17.clone.1 | convolution fusion | flops 269484032 | bytes 10616836 | tf_op jit(solution)/shard_map/while/body/eval_jaxpr/kgtu,ukd->tkgd/dot_general | solution.py:91
  160.1 2.4 %fusion.102 = bf16[4,16,128,128]{2,3,1,0:T(8,128)(2,1)S(1)} fusion(f32[4,128,128,16]{2,1,3,0:T(8,128)S(1)} %fusion.101, bf16[128,4,16,128]{3,0,2,1:T(8,128)(2,1)S(1)} %copy-done.5, f32[4,16,128]{2,1,0:T(8,128)} %get-tuple-element.1342, f32[4,16,128]{2,1,0:T(8,128)S(1)} %get-tuple-element.1339, pred[128,128]{0,1:T(8,128)(4,1)S(1)} %compare_and_fusion.6, ...), kind=kOutput, calls=%fused_computation.20.clone.1 | convolution fusion | flops 276824064 | bytes 8601600 | tf_op jit(solution)/shard_map/while/body/eval_jaxpr/tkgd,ukd->kgtu/dot_general | solution.py:87
  166.9 3.2 %collective-permute-start.3 = (f32[128,4,128]{2,0,1:T(8,128)}, f32[128,4,128]{2,0,1:T(8,128)S(1)}, u32[]{:S(2)}, u32[]{:S(2)}) collective-permute-start(f32[128,4,128]{2,0,1:T(8,128)} %fusion.104), channel_id=1, source_target_pairs={{1,0},{2,1},{3,2},{4,3},{5,4},{6,5},{7,6},{8,7},{9,8},{10,9},{11,1... | collective-permute-start | bytes 786440 | tf_op jit(solution)/shard_map/while/body/eval_jaxpr/ppermute | solution.py:17
  170.1 5.6 %bitcast_add_fusion.2 = f32[128,4,16,128]{0,3,2,1:T(8,128)} fusion(f32[128,4,16,128]{0,3,2,1:T(8,128)} %get-tuple-element.1313, bf16[4,16,128,128]{2,3,1,0:T(8,128)(2,1)} %copy-done, bf16[4,128,4,128]{3,1,2,0:T(8,128)(2,1)S(1)} %get-tuple-element.1337, s32[]{:T(128)S(6)} %select_n.161), kind=kOutput, calls=%fused_computation.17.clone.1 | convolution fusion | flops 269484032 | bytes 10616836 | tf_op jit(solution)/shard_map/while/body/eval_jaxpr/kgtu,ukd->tkgd/dot_general | solution.py:91
  175.7 4.1 %convert_element_type.74 = bf16[128,4,16,128]{0,3,2,1:T(8,128)(2,1)} convert(f32[128,4,16,128]{0,3,2,1:T(8,128)} %get-tuple-element.874) | non-fusion elementwise | flops 1048576 | bytes 6291456 | tf_op jit(solution)/shard_map/convert_element_type | solution.py:120
  179.7 4.1 %copy.106 = bf16[128,8192]{1,0:T(8,128)(2,1)} copy(bf16[128,8192]{0,1:T(8,128)(2,1)} %bitcast.211) | data formatting | bytes 4194304 | tf_op jit(solution)/shard_map/reshape | solution.py:120
  187.2 4.1 %fusion.54 = bf16[128,4,128]{0,2,1:T(8,128)(2,1)S(1)} fusion(f32[128,4,128]{0,2,1:T(8,128)S(1)} %copy.72, bf16[128,4,16,128]{0,3,2,1:T(8,128)(2,1)} %bitcast.209, f32[4,128,128,16]{2,1,3,0:T(8,128)} %copy-done.3, f32[4,16,128]{2,1,0:T(8,128)S(1)} %get-tuple-element.1358, pred[128,128]{0,1:T(8,128)(4,1)S(1)} %compare_and_fusion.2), kind=kOutput, calls=%fused_computation.68 | convolution fusion | flops 273809408 | bytes 6733824 | tf_op jit(solution)/shard_map/kgtu,tkgd->ukd/dot_general | solution.py:97
  (158 shorter events, 72.7 us)
Async XLA Ops:
  9.5 6.8 %copy-start.2 = (bf16[128,8192]{0,1:T(8,128)(2,1)}, bf16[128,8192]{0,1:T(8,128)(2,1)S(1)}, u32[]{:S(2)}) copy-start(bf16[128,8192]{0,1:T(8,128)(2,1)S(1)} %copy.59) | copy-start | bytes 6291460
  35.0 1.9 %copy-start.3 = (f32[4,128,128,16]{2,1,3,0:T(8,128)}, f32[4,128,128,16]{2,1,3,0:T(8,128)S(1)}, u32[]{:S(2)}) copy-start(f32[4,128,128,16]{2,1,3,0:T(8,128)S(1)} %get-tuple-element.1081) | copy-start | bytes 12582916
  38.1 9.5 %collective-permute-start.1 = (bf16[128,4,128]{2,1,0:T(4,128)(2,1)S(1)}, bf16[128,4,128]{2,1,0:T(4,128)(2,1)S(1)}, u32[]{:S(2)}, u32[]{:S(2)}) collective-permute-start(bf16[128,4,128]{2,1,0:T(4,128)(2,1)S(1)} %get-tuple-element.1264), channel_id=1, source_target_pairs={{0,1},{1,2},{2,3},{3,4},{4,5},{5,6},{6,7},{7,8},{8,9},{9,10},{10,1... | collective-permute-start | bytes 393224 | tf_op jit(solution)/shard_map/while/body/eval_jaxpr/ppermute | solution.py:17
  41.8 3.9 %collective-permute-start = (bf16[128,4,128]{2,0,1:T(8,128)(2,1)S(1)}, bf16[128,4,128]{2,0,1:T(8,128)(2,1)S(1)}, u32[]{:S(2)}, u32[]{:S(2)}) collective-permute-start(bf16[128,4,128]{2,0,1:T(8,128)(2,1)S(1)} %get-tuple-element.1263), channel_id=1, source_target_pairs={{0,1},{1,2},{2,3},{3,4},{4,5},{5,6},{6,7},{7,8},{8,9},{9,10},{10,1... | collective-permute-start | bytes 393224 | tf_op jit(solution)/shard_map/while/body/eval_jaxpr/ppermute | solution.py:17
  48.4 10.2 %collective-permute-start.1 = (bf16[128,4,128]{2,1,0:T(4,128)(2,1)S(1)}, bf16[128,4,128]{2,1,0:T(4,128)(2,1)S(1)}, u32[]{:S(2)}, u32[]{:S(2)}) collective-permute-start(bf16[128,4,128]{2,1,0:T(4,128)(2,1)S(1)} %get-tuple-element.1264), channel_id=1, source_target_pairs={{0,1},{1,2},{2,3},{3,4},{4,5},{5,6},{6,7},{7,8},{8,9},{9,10},{10,1... | collective-permute-start | bytes 393224 | tf_op jit(solution)/shard_map/while/body/eval_jaxpr/ppermute | solution.py:17
  52.7 3.9 %collective-permute-start = (bf16[128,4,128]{2,0,1:T(8,128)(2,1)S(1)}, bf16[128,4,128]{2,0,1:T(8,128)(2,1)S(1)}, u32[]{:S(2)}, u32[]{:S(2)}) collective-permute-start(bf16[128,4,128]{2,0,1:T(8,128)(2,1)S(1)} %get-tuple-element.1263), channel_id=1, source_target_pairs={{0,1},{1,2},{2,3},{3,4},{4,5},{5,6},{6,7},{7,8},{8,9},{9,10},{10,1... | collective-permute-start | bytes 393224 | tf_op jit(solution)/shard_map/while/body/eval_jaxpr/ppermute | solution.py:17
  59.3 10.1 %collective-permute-start.1 = (bf16[128,4,128]{2,1,0:T(4,128)(2,1)S(1)}, bf16[128,4,128]{2,1,0:T(4,128)(2,1)S(1)}, u32[]{:S(2)}, u32[]{:S(2)}) collective-permute-start(bf16[128,4,128]{2,1,0:T(4,128)(2,1)S(1)} %get-tuple-element.1264), channel_id=1, source_target_pairs={{0,1},{1,2},{2,3},{3,4},{4,5},{5,6},{6,7},{7,8},{8,9},{9,10},{10,1... | collective-permute-start | bytes 393224 | tf_op jit(solution)/shard_map/while/body/eval_jaxpr/ppermute | solution.py:17
  63.7 3.9 %collective-permute-start = (bf16[128,4,128]{2,0,1:T(8,128)(2,1)S(1)}, bf16[128,4,128]{2,0,1:T(8,128)(2,1)S(1)}, u32[]{:S(2)}, u32[]{:S(2)}) collective-permute-start(bf16[128,4,128]{2,0,1:T(8,128)(2,1)S(1)} %get-tuple-element.1263), channel_id=1, source_target_pairs={{0,1},{1,2},{2,3},{3,4},{4,5},{5,6},{6,7},{7,8},{8,9},{9,10},{10,1... | collective-permute-start | bytes 393224 | tf_op jit(solution)/shard_map/while/body/eval_jaxpr/ppermute | solution.py:17
  70.3 10.7 %collective-permute-start.1 = (bf16[128,4,128]{2,1,0:T(4,128)(2,1)S(1)}, bf16[128,4,128]{2,1,0:T(4,128)(2,1)S(1)}, u32[]{:S(2)}, u32[]{:S(2)}) collective-permute-start(bf16[128,4,128]{2,1,0:T(4,128)(2,1)S(1)} %get-tuple-element.1264), channel_id=1, source_target_pairs={{0,1},{1,2},{2,3},{3,4},{4,5},{5,6},{6,7},{7,8},{8,9},{9,10},{10,1... | collective-permute-start | bytes 393224 | tf_op jit(solution)/shard_map/while/body/eval_jaxpr/ppermute | solution.py:17
  74.6 4.4 %collective-permute-start = (bf16[128,4,128]{2,0,1:T(8,128)(2,1)S(1)}, bf16[128,4,128]{2,0,1:T(8,128)(2,1)S(1)}, u32[]{:S(2)}, u32[]{:S(2)}) collective-permute-start(bf16[128,4,128]{2,0,1:T(8,128)(2,1)S(1)} %get-tuple-element.1263), channel_id=1, source_target_pairs={{0,1},{1,2},{2,3},{3,4},{4,5},{5,6},{6,7},{7,8},{8,9},{9,10},{10,1... | collective-permute-start | bytes 393224 | tf_op jit(solution)/shard_map/while/body/eval_jaxpr/ppermute | solution.py:17
  86.3 1.3 copy-start.4
  96.1 3.3 %copy-start.5 = (bf16[128,4,16,128]{3,0,2,1:T(8,128)(2,1)S(1)}, bf16[128,4,16,128]{3,0,2,1:T(8,128)(2,1)}, u32[]{:S(2)}) copy-start(bf16[128,4,16,128]{3,0,2,1:T(8,128)(2,1)} %get-tuple-element.1341) | copy-start | bytes 6291460 | tf_op jit(solution)/shard_map/while
  101.8 8.8 %copy-start = (bf16[4,16,128,128]{2,3,1,0:T(8,128)(2,1)}, bf16[4,16,128,128]{2,3,1,0:T(8,128)(2,1)S(1)}, u32[]{:S(2)}) copy-start(bf16[4,16,128,128]{2,3,1,0:T(8,128)(2,1)S(1)} %fusion.102) | copy-start | bytes 6291460 | tf_op jit(solution)/shard_map/while
  102.5 15.6 %collective-permute-start.2 = (f32[128,4,128]{2,0,1:T(8,128)S(1)}, f32[128,4,128]{2,0,1:T(8,128)S(1)}, u32[]{:S(2)}, u32[]{:S(2)}) collective-permute-start(f32[128,4,128]{2,0,1:T(8,128)S(1)} %fusion.103), channel_id=1, source_target_pairs={{1,0},{2,1},{3,2},{4,3},{5,4},{6,5},{7,6},{8,7},{9,8},{10,9},{11,1... | collective-permute-start | bytes 786440 | tf_op jit(solution)/shard_map/while/body/eval_jaxpr/ppermute | solution.py:17
  110.6 7.9 %collective-permute-start.3 = (f32[128,4,128]{2,0,1:T(8,128)}, f32[128,4,128]{2,0,1:T(8,128)S(1)}, u32[]{:S(2)}, u32[]{:S(2)}) collective-permute-start(f32[128,4,128]{2,0,1:T(8,128)} %fusion.104), channel_id=1, source_target_pairs={{1,0},{2,1},{3,2},{4,3},{5,4},{6,5},{7,6},{8,7},{9,8},{10,9},{11,1... | collective-permute-start | bytes 786440 | tf_op jit(solution)/shard_map/while/body/eval_jaxpr/ppermute | solution.py:17
  118.5 3.3 %copy-start.5 = (bf16[128,4,16,128]{3,0,2,1:T(8,128)(2,1)S(1)}, bf16[128,4,16,128]{3,0,2,1:T(8,128)(2,1)}, u32[]{:S(2)}) copy-start(bf16[128,4,16,128]{3,0,2,1:T(8,128)(2,1)} %get-tuple-element.1341) | copy-start | bytes 6291460 | tf_op jit(solution)/shard_map/while
  124.3 4.4 %copy-start = (bf16[4,16,128,128]{2,3,1,0:T(8,128)(2,1)}, bf16[4,16,128,128]{2,3,1,0:T(8,128)(2,1)S(1)}, u32[]{:S(2)}) copy-start(bf16[4,16,128,128]{2,3,1,0:T(8,128)(2,1)S(1)} %fusion.102) | copy-start | bytes 6291460 | tf_op jit(solution)/shard_map/while
  125.0 12.0 %collective-permute-start.2 = (f32[128,4,128]{2,0,1:T(8,128)S(1)}, f32[128,4,128]{2,0,1:T(8,128)S(1)}, u32[]{:S(2)}, u32[]{:S(2)}) collective-permute-start(f32[128,4,128]{2,0,1:T(8,128)S(1)} %fusion.103), channel_id=1, source_target_pairs={{1,0},{2,1},{3,2},{4,3},{5,4},{6,5},{7,6},{8,7},{9,8},{10,9},{11,1... | collective-permute-start | bytes 786440 | tf_op jit(solution)/shard_map/while/body/eval_jaxpr/ppermute | solution.py:17
  128.7 8.4 %collective-permute-start.3 = (f32[128,4,128]{2,0,1:T(8,128)}, f32[128,4,128]{2,0,1:T(8,128)S(1)}, u32[]{:S(2)}, u32[]{:S(2)}) collective-permute-start(f32[128,4,128]{2,0,1:T(8,128)} %fusion.104), channel_id=1, source_target_pairs={{1,0},{2,1},{3,2},{4,3},{5,4},{6,5},{7,6},{8,7},{9,8},{10,9},{11,1... | collective-permute-start | bytes 786440 | tf_op jit(solution)/shard_map/while/body/eval_jaxpr/ppermute | solution.py:17
  137.1 3.3 %copy-start.5 = (bf16[128,4,16,128]{3,0,2,1:T(8,128)(2,1)S(1)}, bf16[128,4,16,128]{3,0,2,1:T(8,128)(2,1)}, u32[]{:S(2)}) copy-start(bf16[128,4,16,128]{3,0,2,1:T(8,128)(2,1)} %get-tuple-element.1341) | copy-start | bytes 6291460 | tf_op jit(solution)/shard_map/while
  142.8 5.2 %copy-start = (bf16[4,16,128,128]{2,3,1,0:T(8,128)(2,1)}, bf16[4,16,128,128]{2,3,1,0:T(8,128)(2,1)S(1)}, u32[]{:S(2)}) copy-start(bf16[4,16,128,128]{2,3,1,0:T(8,128)(2,1)S(1)} %fusion.102) | copy-start | bytes 6291460 | tf_op jit(solution)/shard_map/while
  143.5 13.2 %collective-permute-start.2 = (f32[128,4,128]{2,0,1:T(8,128)S(1)}, f32[128,4,128]{2,0,1:T(8,128)S(1)}, u32[]{:S(2)}, u32[]{:S(2)}) collective-permute-start(f32[128,4,128]{2,0,1:T(8,128)S(1)} %fusion.103), channel_id=1, source_target_pairs={{1,0},{2,1},{3,2},{4,3},{5,4},{6,5},{7,6},{8,7},{9,8},{10,9},{11,1... | collective-permute-start | bytes 786440 | tf_op jit(solution)/shard_map/while/body/eval_jaxpr/ppermute | solution.py:17
  148.0 8.8 %collective-permute-start.3 = (f32[128,4,128]{2,0,1:T(8,128)}, f32[128,4,128]{2,0,1:T(8,128)S(1)}, u32[]{:S(2)}, u32[]{:S(2)}) collective-permute-start(f32[128,4,128]{2,0,1:T(8,128)} %fusion.104), channel_id=1, source_target_pairs={{1,0},{2,1},{3,2},{4,3},{5,4},{6,5},{7,6},{8,7},{9,8},{10,9},{11,1... | collective-permute-start | bytes 786440 | tf_op jit(solution)/shard_map/while/body/eval_jaxpr/ppermute | solution.py:17
  156.8 3.3 %copy-start.5 = (bf16[128,4,16,128]{3,0,2,1:T(8,128)(2,1)S(1)}, bf16[128,4,16,128]{3,0,2,1:T(8,128)(2,1)}, u32[]{:S(2)}) copy-start(bf16[128,4,16,128]{3,0,2,1:T(8,128)(2,1)} %get-tuple-element.1341) | copy-start | bytes 6291460 | tf_op jit(solution)/shard_map/while
  162.5 4.4 %copy-start = (bf16[4,16,128,128]{2,3,1,0:T(8,128)(2,1)}, bf16[4,16,128,128]{2,3,1,0:T(8,128)(2,1)S(1)}, u32[]{:S(2)}) copy-start(bf16[4,16,128,128]{2,3,1,0:T(8,128)(2,1)S(1)} %fusion.102) | copy-start | bytes 6291460 | tf_op jit(solution)/shard_map/while
  163.2 12.4 %collective-permute-start.2 = (f32[128,4,128]{2,0,1:T(8,128)S(1)}, f32[128,4,128]{2,0,1:T(8,128)S(1)}, u32[]{:S(2)}, u32[]{:S(2)}) collective-permute-start(f32[128,4,128]{2,0,1:T(8,128)S(1)} %fusion.103), channel_id=1, source_target_pairs={{1,0},{2,1},{3,2},{4,3},{5,4},{6,5},{7,6},{8,7},{9,8},{10,9},{11,1... | collective-permute-start | bytes 786440 | tf_op jit(solution)/shard_map/while/body/eval_jaxpr/ppermute | solution.py:17
  166.9 8.8 %collective-permute-start.3 = (f32[128,4,128]{2,0,1:T(8,128)}, f32[128,4,128]{2,0,1:T(8,128)S(1)}, u32[]{:S(2)}, u32[]{:S(2)}) collective-permute-start(f32[128,4,128]{2,0,1:T(8,128)} %fusion.104), channel_id=1, source_target_pairs={{1,0},{2,1},{3,2},{4,3},{5,4},{6,5},{7,6},{8,7},{9,8},{10,9},{11,1... | collective-permute-start | bytes 786440 | tf_op jit(solution)/shard_map/while/body/eval_jaxpr/ppermute | solution.py:17
  175.7 8.3 %copy-start.1 = (bf16[128,8192]{0,1:T(8,128)(2,1)S(1)}, bf16[128,8192]{0,1:T(8,128)(2,1)}, u32[]{:S(2)}) copy-start(bf16[128,8192]{0,1:T(8,128)(2,1)} %copy.53) | copy-start | bytes 6291460
where the time goes:
time: 194 us; the launch traced here: 192 us
  matrix products  63.5 us (33%)
  starting transfers between devices  48.5 us (25%)
  local copies, waits for them, and re-layouts  45.7 us (24%)
  other arithmetic  29.9 us (15%)
  waiting for transfers between devices  2.61 us (1%)
    ppermute x16, starting transfers between devices, shifted(): return lax.ppermute(x, axis, pairs)  48.5 us
    unnamed x20, local copies, waits for them, and re-layouts  32.8 us
    dot_general x5, matrix products, grad_tile(): jnp.einsum('kgtu,ukd->tkgd', grad_scores, key_block, preferred_element_ty...  25.1 us
    dot_general x5, matrix products, grad_tile(): jnp.einsum('tkgd,ukd->kgtu', grad_four, value_block, preferred_element_ty...  14.2 us
    dot_general x5, matrix products, grad_tile(): jnp.einsum('kgtu,tkgd->ukd', probs.astype(jnp.bfloat16), grad_four, prefe...  11 us
    dot_general x9, matrix products, tile_scores(): jnp.einsum('tkgd,ukd->kgtu', query_four, key_block, preferred_element_typ...  8.06 us
    reduce_sum x9, other arithmetic, doc_index(): jnp.sum((ends[None, :] <= positions[:, None]).astype(jnp.int32), axis=1)  7.3 us
    and x9, other arithmetic, visibility(): return visible & (query_doc[:, None] == doc_index(ends, key_pos)[None, :])  7.1 us
  transfers between devices with their start and end apart: 16, of which 5 were waited for; matrix products, arithmetic and copies ran while one was open for 22% of the time, Pallas kernels for 0%

commit v1 on v0

v1 whole, which is shorter than its diff:
```python
import functools
import math

import jax
import jax.numpy as jnp
from jax import lax
from jax.experimental import pallas as pl
from jax.experimental.pallas import tpu as pltpu
from jax.sharding import PartitionSpec as P

HQ = 64
HK = 4
HD = 128
SPAN = 4
PER = HQ // HK
FACTOR = 1.0 / math.sqrt(HD)
LOG2E = math.log2(math.e)
F32 = jnp.float32
BF = jnp.bfloat16
NT = (((1,), (1,)), ((), ()))
NN = (((1,), (0,)), ((), ()))
MIB = 2**20


def dot(a, b, dims):
    return lax.dot_general(a, b, dims, preferred_element_type=F32)


def starts_row(len_ref, qpos):
    def step(j, c):
        end, start = c
        end = end + len_ref[j]
        return end, jnp.where(end <= qpos, end, start)

    return lax.fori_loop(0, len_ref.shape[0], step, (jnp.int32(0), jnp.zeros_like(qpos)))[1]


def main_kernel(len_ref, place_ref, q_ref, do_ref, delta_ref, *refs, heads):
    k_refs, v_refs = refs[0:5], refs[5:10]
    dq_ref, own_ref, far_ref, swap_ref = refs[10:14]
    kall, vall, kt, bias, acck, accv = refs[14:]
    rows = q_ref.shape[0]
    place = place_ref[0]
    core = place % 2
    dists = (0, SPAN, 2, 1 + 2 * core, 3 - 2 * core)
    for j in range(5):
        kall[j * rows : (j + 1) * rows, :] = k_refs[j][...]
        vall[j * rows : (j + 1) * rows, :] = v_refs[j][...]
    kt[...] = kall[...].astype(F32).T.astype(BF)
    u = lax.broadcasted_iota(jnp.int32, (rows, rows), 0)
    t = lax.broadcasted_iota(jnp.int32, (rows, rows), 1)
    tri = u <= t

    @pl.when(pl.program_id(0) == 0)
    def _():
        qpos = place * rows + lax.broadcasted_iota(jnp.int32, (1, rows), 1)
        start = starts_row(len_ref, qpos)
        for n in range(4):
            if n == 0:
                pos = jnp.where(tri, place * rows + u, (place - SPAN) * rows + u)
            else:
                pos = (place - dists[n + 1]) * rows + u
            bias[n * rows : (n + 1) * rows, :] = jnp.where(pos >= start, 0.0, -jnp.inf).astype(F32)

    def tile(x, n, c):
        if n == 0:
            return jnp.where(tri, x[0:rows, c], x[rows : 2 * rows, c])
        return x[(n + 1) * rows : (n + 2) * rows, c]

    for ch in range(PER // heads):
        hs = [ch * heads + i for i in range(heads)]
        q2 = jnp.concatenate([q_ref[:, h * HD : (h + 1) * HD] for h in hs], axis=0)
        do2 = jnp.concatenate([do_ref[:, h * HD : (h + 1) * HD] for h in hs], axis=0)
        s = dot(kall[...], q2, NT)
        dp = dot(vall[...], do2, NT)
        pb = [[None] * heads for _ in range(5)]
        db = [[None] * heads for _ in range(5)]
        for i, h in enumerate(hs):
            c = slice(i * rows, (i + 1) * rows)
            tiles = [tile(s, n, c) + bias[n * rows : (n + 1) * rows, :] for n in range(4)]
            top = jnp.max(functools.reduce(jnp.maximum, tiles), axis=0, keepdims=True)
            es = [jnp.exp2((x - top) * (FACTOR * LOG2E)) for x in tiles]
            rl = 1.0 / jnp.sum(functools.reduce(jnp.add, es), axis=0, keepdims=True)
            dl = delta_ref[h : h + 1, :]
            for n in range(4):
                p = es[n] * rl
                d = (FACTOR * p) * (tile(dp, n, c) - dl)
                if n == 0:
                    pb[0][i] = jnp.where(tri, p, 0.0).astype(BF)
                    pb[1][i] = jnp.where(tri, 0.0, p).astype(BF)
                    db[0][i] = jnp.where(tri, d, 0.0).astype(BF)
                    db[1][i] = jnp.where(tri, 0.0, d).astype(BF)
                else:
                    pb[n + 1][i] = p.astype(BF)
                    db[n + 1][i] = d.astype(BF)
        probs = jnp.concatenate([jnp.concatenate(r, axis=1) for r in pb], axis=0)
        grads = jnp.concatenate([jnp.concatenate(r, axis=1) for r in db], axis=0)
        dv = dot(probs, do2, NN)
        dk = dot(grads, q2, NN)
        if ch == 0:
            accv[...] = dv
            acck[...] = dk
        else:
            accv[...] += dv
            acck[...] += dk
        dqt = dot(kt[...], grads, NN)
        for i, h in enumerate(hs):
            dq_ref[:, h * HD : (h + 1) * HD] = dqt[:, i * rows : (i + 1) * rows].T.astype(BF)
    for w, acc in enumerate((acck, accv)):
        own_ref[w] = acc[0:rows, :]
        far_ref[w] = acc[rows : 2 * rows, :]
        far_ref[2 + w] = acc[2 * rows : 3 * rows, :]
        swap_ref[2 + w] = acc[3 * rows : 4 * rows, :].astype(BF)
        swap_ref[w] = acc[4 * rows : 5 * rows, :].astype(BF)


def main_call(lengths, place, q, do, delta, ks, vs, heads=4):
    rows = q.shape[0]
    big = pl.BlockSpec((rows, PER * HD), lambda g, *_: (0, g))
    small = pl.BlockSpec((rows, HD), lambda g, *_: (0, g))

    def part(n):
        return pl.BlockSpec((n, rows, HD), lambda g, *_: (0, 0, g))

    return pl.pallas_call(
        functools.partial(main_kernel, heads=heads),
        grid_spec=pltpu.PrefetchScalarGridSpec(
            num_scalar_prefetch=2,
            grid=(HK,),
            in_specs=[big, big, pl.BlockSpec((PER, rows), lambda g, *_: (g, 0))] + [small] * 10,
            out_specs=[big, part(2), part(4), part(4)],
            scratch_shapes=[
                pltpu.VMEM((5 * rows, HD), BF),
                pltpu.VMEM((5 * rows, HD), BF),
                pltpu.VMEM((HD, 5 * rows), BF),
                pltpu.VMEM((4 * rows, rows), F32),
                pltpu.VMEM((5 * rows, HD), F32),
                pltpu.VMEM((5 * rows, HD), F32),
            ],
        ),
        out_shape=[
            jax.ShapeDtypeStruct((rows, HQ * HD), BF),
            jax.ShapeDtypeStruct((2, rows, HK * HD), F32),
            jax.ShapeDtypeStruct((4, rows, HK * HD), F32),
            jax.ShapeDtypeStruct((4, rows, HK * HD), BF),
        ],
        compiler_params=pltpu.CompilerParams(vmem_limit_bytes=50 * MIB),
        name="main",
    )(lengths, place, q, do, delta, *ks, *vs)


def delta_kernel(o_ref, do_ref, out_ref):
    rows = o_ref.shape[0]
    lane = lax.broadcasted_iota(jnp.int32, (rows, HD), 1)
    acc = jnp.zeros((rows, HD), F32)
    for h in range(PER):
        c = slice(h * HD, (h + 1) * HD)
        col = jnp.sum(o_ref[:, c].astype(F32) * do_ref[:, c].astype(F32), axis=1, keepdims=True)
        acc = jnp.where(lane == h, col, acc)
    out_ref[...] = acc.T[0:PER, :]


def delta_call(o, do):
    rows = o.shape[0]
    big = pl.BlockSpec((rows, PER * HD), lambda g: (0, g))
    return pl.pallas_call(
        delta_kernel,
        grid=(HK,),
        in_specs=[big, big],
        out_specs=pl.BlockSpec((PER, rows), lambda g: (g, 0)),
        out_shape=jax.ShapeDtypeStruct((HQ, rows), F32),
        cost_estimate=pl.CostEstimate(flops=10**8, bytes_accessed=4 * MIB, transcendentals=0),
        name="delta",
    )(o, do)


def moved(x, by):
    size = lax.axis_size("ctx")
    return lax.ppermute(x, "ctx", [(i, i + by) for i in range(size) if 0 <= i + by < size])


def swapped(x):
    size = lax.axis_size("ctx")
    return lax.ppermute(x, "ctx", [(i, i ^ 1) for i in range(size)])


def on_device(queries, keys, values, outputs, d_out, lengths):
    rows = queries.shape[0]
    place = lax.axis_index("ctx").astype(jnp.int32)
    even = place % 2 == 0
    k4, k2 = moved(keys, 4), moved(keys, 2)
    v4, v2 = moved(values, 4), moved(values, 2)
    delta = delta_call(outputs, d_out)
    k2s, v2s = swapped(k2), swapped(v2)
    sel = swapped(jnp.where(even, jnp.stack([keys, values]), jnp.stack([k4, v4])))
    d_queries, own, far, swap = main_call(
        lengths,
        place.reshape(1),
        queries,
        d_out,
        delta,
        (keys, k4, k2, k2s, sel[0]),
        (values, v4, v2, v2s, sel[1]),
    )
    back = swapped(swap).astype(F32)
    near, mid = back[0:2], back[2:4]
    far4 = (far[0:2] + jnp.where(even, 0.0, near)).astype(BF)
    far2 = (far[2:4] + mid).astype(BF)
    got4, got2 = moved(far4, -4), moved(far2, -2)
    total = own + jnp.where(even, near, 0.0) + got4.astype(F32) + got2.astype(F32)
    total = total.astype(BF)
    return d_queries, total[0], total[1]


def solution(mesh):
    spec = P(("group", "ctx"), None)
    return jax.shard_map(
        on_device,
        mesh=mesh,
        in_specs=(spec,) * 5 + (P("group"),),
        out_specs=(spec,) * 3,
        check_vma=False,
    )
```

time: 194 us -> 66.4 us (0.34)
  the two profiles are of different devices: /device:TPU:25 before, /device:TPU:6 now
where the time goes in v1:
time: 66.4 us; the launch traced here: 65.8 us
  Pallas kernels  24.9 us (38%)
  starting transfers between devices  19.4 us (29%)
  waiting for transfers between devices  17.7 us (27%)
  other arithmetic  1.54 us (2%)
  local copies, waits for them, and re-layouts  1.51 us (2%)
  between operations  0.78 us (1%)
    pallas_call x1, Pallas kernels, main_call(): pl.pallas_call(functools.partial(main_kernel, heads=heads), grid_spec=plt...  20.4 us
    ppermute x6, starting transfers between devices, moved(): lax.ppermute(x, 'ctx', [(i, i + by) for i in range(size) if 0 <= i + by <...  18.5 us
    ppermute x6, waiting for transfers between devices, moved(): lax.ppermute(x, 'ctx', [(i, i + by) for i in range(size) if 0 <= i + by <...  15.1 us
    pallas_call x1, Pallas kernels, delta_call(): pl.pallas_call(delta_kernel, grid=(HK,), in_specs=[big, big], out_specs=p...  4.46 us
    ppermute x4, waiting for transfers between devices, swapped(): return lax.ppermute(x, 'ctx', [(i, i ^ 1) for i in range(size)])  2.58 us
  transfers between devices with their start and end apart: 10, of which 6 were waited for; matrix products, arithmetic and copies ran while one was open for 0% of the time, Pallas kernels for 7%

profile of v1, /device:TPU:6, one launch (start us, length us, event | category | flops | bytes accessed | tf_op | source)
XLA Modules:
  0.0 65.8 jit_solution(14294816322918328245)
XLA Ops:
  0.6 3.5 %collective-permute-start = (bf16[128,512]{1,0:T(8,128)(2,1)}, bf16[128,512]{1,0:T(8,128)(2,1)S(1)}, u32[]{:S(2)}, u32[]{:S(2)}) collective-permute-start(bf16[128,512]{1,0:T(8,128)(2,1)} %refs_0_.1), channel_id=1, source_target_pairs={{0,4},{1,5},{2,6},{3,7},{4,8},{5,9},{6,10},{7,11},{8,12},{9,13},{1... | collective-permute-start | bytes 393224 | tf_op jit(solution)/shard_map/ppermute | solution.py:179
  4.1 3.5 %collective-permute-start.3 = (bf16[128,512]{1,0:T(8,128)(2,1)}, bf16[128,512]{1,0:T(8,128)(2,1)S(1)}, u32[]{:S(2)}, u32[]{:S(2)}) collective-permute-start(bf16[128,512]{1,0:T(8,128)(2,1)} %refs_5_.1), channel_id=1, source_target_pairs={{0,4},{1,5},{2,6},{3,7},{4,8},{5,9},{6,10},{7,11},{8,12},{9,13},{1... | collective-permute-start | bytes 393224 | tf_op jit(solution)/shard_map/ppermute | solution.py:179
  7.6 0.0 collective-permute-done.refs_1_
  7.6 2.8 %collective-permute-done.3.refs_6_ = bf16[128,512]{1,0:T(8,128)(2,1)S(1)} collective-permute-done((bf16[128,512]{1,0:T(8,128)(2,1)}, bf16[128,512]{1,0:T(8,128)(2,1)S(1)}, u32[]{:S(2)}, u32[]{:S(2)}) %collective-permute-start.3) | collective-permute-done | bytes 131104 | tf_op jit(solution)/shard_map/ppermute | solution.py:179
  10.4 1.0 %maximum_select_fusion = bf16[2,128,512]{2,1,0:T(8,128)(2,1)S(1)} fusion(bf16[1,128,512]{2,1,0:T(8,128)(2,1)} %bitcast.14, bf16[1,128,512]{2,1,0:T(8,128)(2,1)} %bitcast.13, bf16[1,128,512]{2,1,0:T(8,128)(2,1)S(1)} %bitcast.16, bf16[1,128,512]{2,1,0:T(8,128)(2,1)S(1)} %bitcast.15, pred[]{:T(512)S(6)} %eq.5), kind=kLoop, calls=%fused_computation.4 | loop fusion | flops 393216 | bytes 786433 | tf_op jit(solution)/shard_map/jit(_where)/select_n | solution.py:195
  11.5 0.0 copy-start
  11.5 0.0 copy-start.1
  11.5 0.0 copy-start.3
  11.5 0.1 collective-permute-start.4
  11.6 4.4 %collective-permute-start.1 = (bf16[128,512]{1,0:T(8,128)(2,1)}, bf16[128,512]{1,0:T(8,128)(2,1)S(1)}, u32[]{:S(2)}, u32[]{:S(2)}) collective-permute-start(bf16[128,512]{1,0:T(8,128)(2,1)} %refs_0_.1), channel_id=1, source_target_pairs={{0,2},{1,3},{2,4},{3,5},{4,6},{5,7},{6,8},{7,9},{8,10},{9,11},{10,... | collective-permute-start | bytes 393224 | tf_op jit(solution)/shard_map/ppermute | solution.py:179
  15.9 3.4 %collective-permute-start.5 = (bf16[128,512]{1,0:T(8,128)(2,1)}, bf16[128,512]{1,0:T(8,128)(2,1)S(1)}, u32[]{:S(2)}, u32[]{:S(2)}) collective-permute-start(bf16[128,512]{1,0:T(8,128)(2,1)} %refs_5_.1), channel_id=1, source_target_pairs={{0,2},{1,3},{2,4},{3,5},{4,6},{5,7},{6,8},{7,9},{8,10},{9,11},{10,... | collective-permute-start | bytes 393224 | tf_op jit(solution)/shard_map/ppermute | solution.py:179
  19.3 4.5 %delta.1.delta_ref = f32[64,128]{1,0:T(8,128)} custom-call(bf16[128,8192]{1,0:T(8,128)(2,1)} %o_ref.1, bf16[128,8192]{1,0:T(8,128)(2,1)} %do_ref.3), custom_call_target="tpu_custom_call" | custom-call | flops 100000000 | bytes 4194304 | tf_op jit(solution)/shard_map/delta/pallas_call | solution.py:166
  23.8 0.0 collective-permute-done.1.refs_2_
  23.8 0.0 collective-permute-start.2
  23.8 0.0 collective-permute-done.5.refs_7_
  23.8 0.5 collective-permute-start.6
  24.3 0.0 collective-permute-done.4
  24.3 0.8 %collective-permute-done.2.refs_3_ = bf16[128,512]{1,0:T(8,128)(2,1)S(1)} collective-permute-done((bf16[128,512]{1,0:T(8,128)(2,1)S(1)}, bf16[128,512]{1,0:T(8,128)(2,1)S(1)}, u32[]{:S(2)}, u32[]{:S(2)}) %collective-permute-start.2) | collective-permute-done | bytes 131104 | tf_op jit(solution)/shard_map/ppermute | solution.py:184
  25.1 0.2 collective-permute-done.6.refs_8_
  25.3 0.0 copy-start.2
  25.4 0.7 %copy-done.2 = f32[64,128]{1,0:T(8,128)S(1)} copy-done((f32[64,128]{1,0:T(8,128)S(1)}, f32[64,128]{1,0:T(8,128)}, u32[]{:S(2)}) %copy-start.2) | copy-done | bytes 32792
  26.1 20.4 %main.1 = (bf16[128,8192]{1,0:T(8,128)(2,1)}, f32[2,128,512]{2,1,0:T(8,128)S(1)}, f32[4,128,512]{2,1,0:T(8,128)S(1)}, bf16[4,128,512]{2,1,0:T(8,128)(2,1)S(1)}) custom-call(s32[8]{0:T(128)S(1)} %copy-done.3, s32[1]{0:T(128)} %bitcast.place_ref, bf16[128,8192]{1,0:T(8,128)(2,1)} %q_ref.1, bf16[128,8192]{1,0:T(8,128)(2,1)} %do_ref.3, f32[64,128]{1,0:T(8,128)S(1)} %copy-done.2, ...), custom_call_target="tpu_custom_call" | custom-call | tf_op jit(solution)/shard_map/main/pallas_call | solution.py:125
  46.5 0.3 collective-permute-start.7
  46.9 1.6 %collective-permute-done.7 = bf16[4,128,512]{2,1,0:T(8,128)(2,1)S(1)} collective-permute-done((bf16[4,128,512]{2,1,0:T(8,128)(2,1)S(1)}, bf16[4,128,512]{2,1,0:T(8,128)(2,1)S(1)}, u32[]{:S(2)}, u32[]{:S(2)}) %collective-permute-start.7) | collective-permute-done | bytes 524320 | tf_op jit(solution)/shard_map/ppermute | solution.py:184
  48.5 0.1 convert_element_type.18
  48.6 0.3 add_convert_fusion.1
  48.8 1.3 %collective-permute-start.8 = (bf16[2,128,512]{2,1,0:T(8,128)(2,1)S(1)}, bf16[2,128,512]{2,1,0:T(8,128)(2,1)S(1)}, u32[]{:S(2)}, u32[]{:S(2)}) collective-permute-start(bf16[2,128,512]{2,1,0:T(8,128)(2,1)S(1)} %get-tuple-element.11), channel_id=1, source_target_pairs={{4,0},{5,1},{6,2},{7,3},{8,4},{9,5},{10,6},{11,7},{12,8},{13,9},{1... | collective-permute-start | bytes 786440 | tf_op jit(solution)/shard_map/ppermute | solution.py:179
  50.1 2.4 %collective-permute-start.9 = (bf16[2,128,512]{2,1,0:T(8,128)(2,1)S(1)}, bf16[2,128,512]{2,1,0:T(8,128)(2,1)S(1)}, u32[]{:S(2)}, u32[]{:S(2)}) collective-permute-start(bf16[2,128,512]{2,1,0:T(8,128)(2,1)S(1)} %get-tuple-element.12), channel_id=1, source_target_pairs={{2,0},{3,1},{4,2},{5,3},{6,4},{7,5},{8,6},{9,7},{10,8},{11,9},{12,... | collective-permute-start | bytes 786440 | tf_op jit(solution)/shard_map/ppermute | solution.py:179
  52.6 6.7 %collective-permute-done.8 = bf16[2,128,512]{2,1,0:T(8,128)(2,1)S(1)} collective-permute-done((bf16[2,128,512]{2,1,0:T(8,128)(2,1)S(1)}, bf16[2,128,512]{2,1,0:T(8,128)(2,1)S(1)}, u32[]{:S(2)}, u32[]{:S(2)}) %collective-permute-start.8) | collective-permute-done | bytes 262176 | tf_op jit(solution)/shard_map/ppermute | solution.py:179
  59.3 5.6 %collective-permute-done.9 = bf16[2,128,512]{2,1,0:T(8,128)(2,1)S(1)} collective-permute-done((bf16[2,128,512]{2,1,0:T(8,128)(2,1)S(1)}, bf16[2,128,512]{2,1,0:T(8,128)(2,1)S(1)}, u32[]{:S(2)}, u32[]{:S(2)}) %collective-permute-start.9) | collective-permute-done | bytes 262176 | tf_op jit(solution)/shard_map/ppermute | solution.py:179
  64.9 0.2 add_convert_fusion
  65.1 0.7 %slice_bitcast_fusion = (bf16[128,512]{1,0:T(8,128)(2,1)}, bf16[128,512]{1,0:T(8,128)(2,1)}) fusion(bf16[2,128,512]{2,1,0:T(8,128)(2,1)S(1)} %add_convert_fusion), kind=kLoop, calls=%fused_computation.5 | loop fusion | bytes 524288 | tf_op jit(solution)/shard_map/squeeze | solution.py:212
  (4 shorter events, 0.0 us)
Async XLA Ops:
  0.6 7.0 %collective-permute-start = (bf16[128,512]{1,0:T(8,128)(2,1)}, bf16[128,512]{1,0:T(8,128)(2,1)S(1)}, u32[]{:S(2)}, u32[]{:S(2)}) collective-permute-start(bf16[128,512]{1,0:T(8,128)(2,1)} %refs_0_.1), channel_id=1, source_target_pairs={{0,4},{1,5},{2,6},{3,7},{4,8},{5,9},{6,10},{7,11},{8,12},{9,13},{1... | collective-permute-start | bytes 393224 | tf_op jit(solution)/shard_map/ppermute | solution.py:179
  4.1 6.3 %collective-permute-start.3 = (bf16[128,512]{1,0:T(8,128)(2,1)}, bf16[128,512]{1,0:T(8,128)(2,1)S(1)}, u32[]{:S(2)}, u32[]{:S(2)}) collective-permute-start(bf16[128,512]{1,0:T(8,128)(2,1)} %refs_5_.1), channel_id=1, source_target_pairs={{0,4},{1,5},{2,6},{3,7},{4,8},{5,9},{6,10},{7,11},{8,12},{9,13},{1... | collective-permute-start | bytes 393224 | tf_op jit(solution)/shard_map/ppermute | solution.py:179
  11.5 13.9 %copy-start = (bf16[128,512]{1,0:T(8,128)(2,1)S(1)}, bf16[128,512]{1,0:T(8,128)(2,1)}, u32[]{:S(2)}) copy-start(bf16[128,512]{1,0:T(8,128)(2,1)} %refs_0_.1) | copy-start | bytes 393220
  11.5 13.9 %copy-start.1 = (bf16[128,512]{1,0:T(8,128)(2,1)S(1)}, bf16[128,512]{1,0:T(8,128)(2,1)}, u32[]{:S(2)}) copy-start(bf16[128,512]{1,0:T(8,128)(2,1)} %refs_5_.1) | copy-start | bytes 393220
  11.5 13.9 %copy-start.3 = (s32[8]{0:T(128)S(1)}, s32[8]{0:T(128)}, u32[]{:S(2)}) copy-start(s32[8]{0:T(128)} %len_ref.1) | copy-start | bytes 100
  11.5 12.8 %collective-permute-start.4 = (bf16[2,128,512]{2,1,0:T(8,128)(2,1)S(1)}, bf16[2,128,512]{2,1,0:T(8,128)(2,1)S(1)}, u32[]{:S(2)}, u32[]{:S(2)}) collective-permute-start(bf16[2,128,512]{2,1,0:T(8,128)(2,1)S(1)} %maximum_select_fusion), channel_id=1, source_target_pairs={{0,1},{1,0},{2,3},{3,2},{4,5},{5,4},{6,7},{7,6},{8,9},{9,8},{10,11... | collective-permute-start | bytes 786440 | tf_op jit(solution)/shard_map/ppermute | solution.py:184
  11.6 12.2 %collective-permute-start.1 = (bf16[128,512]{1,0:T(8,128)(2,1)}, bf16[128,512]{1,0:T(8,128)(2,1)S(1)}, u32[]{:S(2)}, u32[]{:S(2)}) collective-permute-start(bf16[128,512]{1,0:T(8,128)(2,1)} %refs_0_.1), channel_id=1, source_target_pairs={{0,2},{1,3},{2,4},{3,5},{4,6},{5,7},{6,8},{7,9},{8,10},{9,11},{10,... | collective-permute-start | bytes 393224 | tf_op jit(solution)/shard_map/ppermute | solution.py:179
  15.9 7.9 %collective-permute-start.5 = (bf16[128,512]{1,0:T(8,128)(2,1)}, bf16[128,512]{1,0:T(8,128)(2,1)S(1)}, u32[]{:S(2)}, u32[]{:S(2)}) collective-permute-start(bf16[128,512]{1,0:T(8,128)(2,1)} %refs_5_.1), channel_id=1, source_target_pairs={{0,2},{1,3},{2,4},{3,5},{4,6},{5,7},{6,8},{7,9},{8,10},{9,11},{10,... | collective-permute-start | bytes 393224 | tf_op jit(solution)/shard_map/ppermute | solution.py:179
  23.8 1.3 %collective-permute-start.2 = (bf16[128,512]{1,0:T(8,128)(2,1)S(1)}, bf16[128,512]{1,0:T(8,128)(2,1)S(1)}, u32[]{:S(2)}, u32[]{:S(2)}) collective-permute-start(bf16[128,512]{1,0:T(8,128)(2,1)S(1)} %collective-permute-done.1.refs_2_), channel_id=1, source_target_pairs={{0,1},{1,0},{2,3},{3,2},{4,5},{5,4},{6,7},{7,6},{8,9},{9,8},{10,11... | collective-permute-start | bytes 393224 | tf_op jit(solution)/shard_map/ppermute | solution.py:184
  23.8 1.5 %collective-permute-start.6 = (bf16[128,512]{1,0:T(8,128)(2,1)S(1)}, bf16[128,512]{1,0:T(8,128)(2,1)S(1)}, u32[]{:S(2)}, u32[]{:S(2)}) collective-permute-start(bf16[128,512]{1,0:T(8,128)(2,1)S(1)} %collective-permute-done.5.refs_7_), channel_id=1, source_target_pairs={{0,1},{1,0},{2,3},{3,2},{4,5},{5,4},{6,7},{7,6},{8,9},{9,8},{10,11... | collective-permute-start | bytes 393224 | tf_op jit(solution)/shard_map/ppermute | solution.py:184
  25.3 0.8 %copy-start.2 = (f32[64,128]{1,0:T(8,128)S(1)}, f32[64,128]{1,0:T(8,128)}, u32[]{:S(2)}) copy-start(f32[64,128]{1,0:T(8,128)} %delta.1.delta_ref) | copy-start | bytes 98308
  46.5 1.9 %collective-permute-start.7 = (bf16[4,128,512]{2,1,0:T(8,128)(2,1)S(1)}, bf16[4,128,512]{2,1,0:T(8,128)(2,1)S(1)}, u32[]{:S(2)}, u32[]{:S(2)}) collective-permute-start(bf16[4,128,512]{2,1,0:T(8,128)(2,1)S(1)} %get-tuple-element.9), channel_id=1, source_target_pairs={{0,1},{1,0},{2,3},{3,2},{4,5},{5,4},{6,7},{7,6},{8,9},{9,8},{10,11... | collective-permute-start | bytes 1572872 | tf_op jit(solution)/shard_map/ppermute | solution.py:184
  48.8 10.4 %collective-permute-start.8 = (bf16[2,128,512]{2,1,0:T(8,128)(2,1)S(1)}, bf16[2,128,512]{2,1,0:T(8,128)(2,1)S(1)}, u32[]{:S(2)}, u32[]{:S(2)}) collective-permute-start(bf16[2,128,512]{2,1,0:T(8,128)(2,1)S(1)} %get-tuple-element.11), channel_id=1, source_target_pairs={{4,0},{5,1},{6,2},{7,3},{8,4},{9,5},{10,6},{11,7},{12,8},{13,9},{1... | collective-permute-start | bytes 786440 | tf_op jit(solution)/shard_map/ppermute | solution.py:179
  50.1 14.8 %collective-permute-start.9 = (bf16[2,128,512]{2,1,0:T(8,128)(2,1)S(1)}, bf16[2,128,512]{2,1,0:T(8,128)(2,1)S(1)}, u32[]{:S(2)}, u32[]{:S(2)}) collective-permute-start(bf16[2,128,512]{2,1,0:T(8,128)(2,1)S(1)} %get-tuple-element.12), channel_id=1, source_target_pairs={{2,0},{3,1},{4,2},{5,3},{6,4},{7,5},{8,6},{9,7},{10,8},{11,9},{12,... | collective-permute-start | bytes 786440 | tf_op jit(solution)/shard_map/ppermute | solution.py:179

commit v2 on v1

--- a/solution.py
+++ b/solution.py
@@ -35,17 +35,20 @@
     return lax.fori_loop(0, len_ref.shape[0], step, (jnp.int32(0), jnp.zeros_like(qpos)))[1]
 
 
-def main_kernel(len_ref, place_ref, q_ref, do_ref, delta_ref, *refs, heads):
-    k_refs, v_refs = refs[0:5], refs[5:10]
-    dq_ref, own_ref, far_ref, swap_ref = refs[10:14]
-    kall, vall, kt, bias, acck, accv = refs[14:]
+def main_kernel(len_ref, place_ref, q_ref, do_ref, delta_ref, *refs, heads, kept):
+    kv_refs = refs[0:6]
+    dq_ref, own_ref, far_ref, swap_ref = refs[6 + kept : 10 + kept]
+    kall, vall, kt, bias, acck, accv = refs[10 + kept :]
     rows = q_ref.shape[0]
     place = place_ref[0]
     core = place % 2
     dists = (0, SPAN, 2, 1 + 2 * core, 3 - 2 * core)
     for j in range(5):
-        kall[j * rows : (j + 1) * rows, :] = k_refs[j][...]
-        vall[j * rows : (j + 1) * rows, :] = v_refs[j][...]
+        pair = kv_refs[j][...]
+        if j == 4:
+            pair = jnp.where(core == 0, pair, kv_refs[5][...])
+        kall[j * rows : (j + 1) * rows, :] = pair[:, :HD]
+        vall[j * rows : (j + 1) * rows, :] = pair[:, HD:]
     kt[...] = kall[...].astype(F32).T.astype(BF)
     u = lax.broadcasted_iota(jnp.int32, (rows, rows), 0)
     t = lax.broadcasted_iota(jnp.int32, (rows, rows), 1)
@@ -107,28 +110,31 @@
         for i, h in enumerate(hs):
             dq_ref[:, h * HD : (h + 1) * HD] = dqt[:, i * rows : (i + 1) * rows].T.astype(BF)
     for w, acc in enumerate((acck, accv)):
-        own_ref[w] = acc[0:rows, :]
-        far_ref[w] = acc[rows : 2 * rows, :]
-        far_ref[2 + w] = acc[2 * rows : 3 * rows, :]
-        swap_ref[2 + w] = acc[3 * rows : 4 * rows, :].astype(BF)
-        swap_ref[w] = acc[4 * rows : 5 * rows, :].astype(BF)
-
-
-def main_call(lengths, place, q, do, delta, ks, vs, heads=4):
+        c = slice(w * HD, (w + 1) * HD)
+        own_ref[:, c] = acc[0:rows, :]
+        far_ref[0, :, c] = acc[rows : 2 * rows, :]
+        far_ref[1, :, c] = acc[2 * rows : 3 * rows, :]
+        swap_ref[1, :, c] = acc[3 * rows : 4 * rows, :].astype(BF)
+        swap_ref[0, :, c] = acc[4 * rows : 5 * rows, :].astype(BF)
+
+
+def main_call(lengths, place, q, do, delta, kvs, dq, parts, first, last, local, base, width):
     rows = q.shape[0]
-    big = pl.BlockSpec((rows, PER * HD), lambda g, *_: (0, g))
-    small = pl.BlockSpec((rows, HD), lambda g, *_: (0, g))
-
-    def part(n):
-        return pl.BlockSpec((n, rows, HD), lambda g, *_: (0, 0, g))
-
-    return pl.pallas_call(
-        functools.partial(main_kernel, heads=heads),
+    big = pl.BlockSpec((rows, PER * HD), lambda g, *_: (0, first + g))
+    pair = pl.BlockSpec((rows, 2 * HD), lambda g, *_: (0, local + g))
+    own = pl.BlockSpec((rows, 2 * HD), lambda g, *_: (0, base + g))
+    far = pl.BlockSpec((2, rows, 2 * HD), lambda g, *_: (0, 0, base + g))
+    kept = [] if dq is None else [(0, dq)]
+    kept += [] if parts is None else [(1 + i, x) for i, x in enumerate(parts)]
+    return pl.pallas_call(
+        functools.partial(main_kernel, heads=4, kept=len(kept)),
         grid_spec=pltpu.PrefetchScalarGridSpec(
             num_scalar_prefetch=2,
-            grid=(HK,),
-            in_specs=[big, big, pl.BlockSpec((PER, rows), lambda g, *_: (g, 0))] + [small] * 10,
-            out_specs=[big, part(2), part(4), part(4)],
+            grid=(last - first,),
+            in_specs=[big, big, pl.BlockSpec((PER, rows), lambda g, *_: (first + g, 0))]
+            + [pair] * 6
+            + [pl.BlockSpec(memory_space=pl.ANY)] * len(kept),
+            out_specs=[big, own, far, far],
             scratch_shapes=[
                 pltpu.VMEM((5 * rows, HD), BF),
                 pltpu.VMEM((5 * rows, HD), BF),
@@ -140,24 +146,30 @@
         ),
         out_shape=[
             jax.ShapeDtypeStruct((rows, HQ * HD), BF),
-            jax.ShapeDtypeStruct((2, rows, HK * HD), F32),
-            jax.ShapeDtypeStruct((4, rows, HK * HD), F32),
-            jax.ShapeDtypeStruct((4, rows, HK * HD), BF),
+            jax.ShapeDtypeStruct((rows, width * 2 * HD), F32),
+            jax.ShapeDtypeStruct((2, rows, width * 2 * HD), F32),
+            jax.ShapeDtypeStruct((2, rows, width * 2 * HD), BF),
         ],
-        compiler_params=pltpu.CompilerParams(vmem_limit_bytes=50 * MIB),
+        input_output_aliases={11 + i: o for i, (o, _) in enumerate(kept)},
+        compiler_params=pltpu.CompilerParams(vmem_limit_bytes=58 * MIB),
+        cost_estimate=pl.CostEstimate(
+            flops=(last - first) * 5 * 10**9,
+            bytes_accessed=(last - first) * 2 * MIB,
+            transcendentals=(last - first) * 10**6,
+        ),
         name="main",
-    )(lengths, place, q, do, delta, *ks, *vs)
+    )(lengths, place, q, do, delta, *kvs, *[x for _, x in kept])
 
 
 def delta_kernel(o_ref, do_ref, out_ref):
     rows = o_ref.shape[0]
-    lane = lax.broadcasted_iota(jnp.int32, (rows, HD), 1)
-    acc = jnp.zeros((rows, HD), F32)
+    ones = jnp.ones((8, 2 * HD), BF)
     for h in range(PER):
         c = slice(h * HD, (h + 1) * HD)
-        col = jnp.sum(o_ref[:, c].astype(F32) * do_ref[:, c].astype(F32), axis=1, keepdims=True)
-        acc = jnp.where(lane == h, col, acc)
-    out_ref[...] = acc.T[0:PER, :]
+        x = o_ref[:, c].astype(F32) * do_ref[:, c].astype(F32)
+        high = x.astype(BF)
+        low = (x - high.astype(F32)).astype(BF)
+        out_ref[h : h + 1, :] = dot(ones, jnp.concatenate([high, low], axis=1), NT)[0:1, :]
 
 
 def delta_call(o, do):
@@ -176,7 +188,7 @@
 
 def moved(x, by):
     size = lax.axis_size("ctx")
-    return lax.ppermute(x, "ctx", [(i, i + by) for i in range(size) if 0 <= i + by < size])
+    return lax.ppermute(x, "ctx", [(i, (i + by) % size) for i in range(size)])
 
 
 def swapped(x):
@@ -184,32 +196,91 @@
     return lax.ppermute(x, "ctx", [(i, i ^ 1) for i in range(size)])
 
 
+def pack_kernel(k_ref, v_ref, *out_refs):
+    at = 0
+    for out_ref in out_refs:
+        for i in range(out_ref.shape[1] // (2 * HD)):
+            c = slice(at * HD, (at + 1) * HD)
+            out_ref[:, 2 * i * HD : (2 * i + 1) * HD] = k_ref[:, c]
+            out_ref[:, (2 * i + 1) * HD : (2 * i + 2) * HD] = v_ref[:, c]
+            at += 1
+
+
+def pack_call(keys, values):
+    rows = keys.shape[0]
+    return pl.pallas_call(
+        pack_kernel,
+        out_shape=[jax.ShapeDtypeStruct((rows, (e - f) * 2 * HD), BF) for f, e in FORTH],
+        name="pack",
+    )(keys, values)
+
+
+def sum_kernel(place_ref, *refs):
+    even = place_ref[0] % 2 == 0
+    dk_ref, dv_ref = refs[-2:]
+    at = 0
+    for n in range(len(refs) // 4):
+        mine, near, got4, got2 = refs[4 * n : 4 * n + 4]
+        for i in range(mine.shape[1] // (2 * HD)):
+            for w, out_ref in enumerate((dk_ref, dv_ref)):
+                c = slice((2 * i + w) * HD, (2 * i + w + 1) * HD)
+                total = mine[:, c] + jnp.where(even, near[0, :, c].astype(F32), 0.0)
+                total = total + got4[:, c].astype(F32) + got2[:, c].astype(F32)
+                out_ref[:, at * HD : (at + 1) * HD] = total.astype(BF)
+            at += 1
+
+
+def sum_call(index, sums):
+    rows = sums[0].shape[0]
+    return pl.pallas_call(
+        sum_kernel,
+        in_specs=[pl.BlockSpec(memory_space=pltpu.SMEM)] + [pl.BlockSpec(memory_space=pltpu.VMEM)] * len(sums),
+        out_shape=[jax.ShapeDtypeStruct((rows, HK * HD), BF)] * 2,
+        name="sum",
+    )(index, *sums)
+
+
+FORTH = ((0, 1), (1, 4))
+CALLS = ((0, 1), (1, 2), (2, 4))
+BACK = ((0, 2), (2, 4))
+
+
 def on_device(queries, keys, values, outputs, d_out, lengths):
-    rows = queries.shape[0]
     place = lax.axis_index("ctx").astype(jnp.int32)
     even = place % 2 == 0
-    k4, k2 = moved(keys, 4), moved(keys, 2)
-    v4, v2 = moved(values, 4), moved(values, 2)
+    index = place.reshape(1)
+    own = pack_call(keys, values)
+    two = [moved(x, 2) for x in own]
+    four = [moved(x, 4) for x in own]
+    mates = [swapped(x) for x in own]
     delta = delta_call(outputs, d_out)
-    k2s, v2s = swapped(k2), swapped(v2)
-    sel = swapped(jnp.where(even, jnp.stack([keys, values]), jnp.stack([k4, v4])))
-    d_queries, own, far, swap = main_call(
-        lengths,
-        place.reshape(1),
-        queries,
-        d_out,
-        delta,
-        (keys, k4, k2, k2s, sel[0]),
-        (values, v4, v2, v2s, sel[1]),
-    )
-    back = swapped(swap).astype(F32)
-    near, mid = back[0:2], back[2:4]
-    far4 = (far[0:2] + jnp.where(even, 0.0, near)).astype(BF)
-    far2 = (far[2:4] + mid).astype(BF)
-    got4, got2 = moved(far4, -4), moved(far2, -2)
-    total = own + jnp.where(even, near, 0.0) + got4.astype(F32) + got2.astype(F32)
-    total = total.astype(BF)
-    return d_queries, total[0], total[1]
+    d_queries, sums, kvs, pending = None, [], None, None
+    for first, end in BACK:
+        parts = None
+        for a, b in CALLS:
+            if not first <= a < end:
+                continue
+            g = [f <= a < e for f, e in FORTH].index(True)
+            if a == FORTH[g][0]:
+                far, mid = four[g], two[g]
+                if d_queries is not None:
+                    far, mid, d_queries = lax.optimization_barrier((far, mid, d_queries))
+                kvs = (own[g], far, mid, swapped(mid), swapped(far), mates[g])
+            d_queries, *parts = main_call(
+                lengths, index, queries, d_out, delta, kvs, d_queries, parts, a, b, a - FORTH[g][0], a - first, end - first
+            )
+        mine, far, swap = parts
+        if pending is not None:
+            swap, *pending = lax.optimization_barrier((swap, *pending))
+            sums += pending
+        back = swapped(swap)
+        far4 = (far[0] + jnp.where(even, 0.0, back[0].astype(F32))).astype(BF)
+        far2 = (far[1] + back[1].astype(F32)).astype(BF)
+        if end < HK:
+            far4, far2, d_queries = lax.optimization_barrier((far4, far2, d_queries))
+        pending = (mine, back, moved(far4, -4), moved(far2, -2))
+    d_keys, d_values = sum_call(index, (*sums, *pending))
+    return d_queries, d_keys, d_values
 
 
 def solution(mesh):

time: 66.4 us -> 68.8 us (1.036)
  Pallas kernels: 24.9 us -> 34.2 us
  starting transfers between devices: 19.4 us -> 12.2 us
  waiting for transfers between devices: 17.7 us -> 16.8 us
  other arithmetic: 1.54 us -> 2.39 us
    pallas_call x1 -> x5, Pallas kernels: 20.4 us -> 29.7 us  [the longest x3 25.8 us: main_call(): pl.pallas_call(functools.partial(main_kernel, heads=4, kept=len(kept)), g...]
    ppermute x6 -> x8, starting transfers between devices: 18.5 us -> 11.2 us  [moved(): return lax.ppermute(x, 'ctx', [(i, (i + by) % size) for i in range(size)])]
    ppermute x6 -> x8, waiting for transfers between devices: 15.1 us -> 12.2 us  [moved(): return lax.ppermute(x, 'ctx', [(i, (i + by) % size) for i in range(size)])]
    ppermute x4 -> x8, waiting for transfers between devices: 2.58 us -> 4.56 us  [swapped(): return lax.ppermute(x, 'ctx', [(i, i ^ 1) for i in range(size)])]
    convert_element_type x3 -> x2, other arithmetic: 0.53 us -> 2.39 us  [on_device(): far2 = (far[1] + back[1].astype(F32)).astype(BF)]
    unnamed x8 -> x34, local copies, waits for them, and re-layouts: 0.77 us -> 1.97 us
    select_n x1 -> x0, other arithmetic: 1.01 us -> none  [on_device(): jnp.where(even, jnp.stack([keys, values]), jnp.stack([k4, v4]))]
    squeeze x2 -> x0, local copies, waits for them, and re-layouts: 0.73 us -> none  [the longest x1 0.72 us: on_device(): return (d_queries, total[0], total[1])]
  transfers between devices with their start and end apart: 10 -> 16, of which waited for: 6 -> 8; matrix products, arithmetic and copies ran while one was open for 0% -> 0% of each run, Pallas kernels for 7% -> 34%
where the time goes in v2:
time: 68.8 us; the launch traced here: 68.4 us
  Pallas kernels  34.2 us (50%)
  waiting for transfers between devices  16.8 us (24%)
  starting transfers between devices  12.2 us (18%)
  other arithmetic  2.39 us (3%)
  local copies, waits for them, and re-layouts  1.97 us (3%)
  between operations  0.82 us (1%)
    pallas_call x3, Pallas kernels, main_call(): pl.pallas_call(functools.partial(main_kernel, heads=4, kept=len(kept)), g...  25.8 us
    ppermute x8, waiting for transfers between devices, moved(): return lax.ppermute(x, 'ctx', [(i, (i + by) % size) for i in range(size)])  12.2 us
    ppermute x8, starting transfers between devices, moved(): return lax.ppermute(x, 'ctx', [(i, (i + by) % size) for i in range(size)])  11.2 us
    ppermute x8, waiting for transfers between devices, swapped(): return lax.ppermute(x, 'ctx', [(i, i ^ 1) for i in range(size)])  4.56 us
    pallas_call x1, Pallas kernels, delta_call(): pl.pallas_call(delta_kernel, grid=(HK,), in_specs=[big, big], out_specs=p...  4.5 us
    convert_element_type x2, other arithmetic, on_device(): far2 = (far[1] + back[1].astype(F32)).astype(BF)  2.39 us
    pallas_call x1, Pallas kernels, sum_call(): pl.pallas_call(sum_kernel, in_specs=[pl.BlockSpec(memory_space=pltpu.SMEM...  2.19 us
    unnamed x34, local copies, waits for them, and re-layouts  1.97 us
  transfers between devices with their start and end apart: 16, of which 8 were waited for; matrix products, arithmetic and copies ran while one was open for 0% of the time, Pallas kernels for 34%

profile of v2, /device:TPU:6, one launch (start us, length us, event | category | flops | bytes accessed | tf_op | source)
XLA Modules:
  0.0 68.4 jit_solution(10733708523981788724)
XLA Ops:
  0.6 1.7 %pack.1 = (bf16[128,256]{1,0:T(8,128)(2,1)}, bf16[128,768]{1,0:T(8,128)(2,1)}) custom-call(bf16[128,512]{1,0:T(8,128)(2,1)} %k_ref.1, bf16[128,512]{1,0:T(8,128)(2,1)} %v_ref.1), custom_call_target="tpu_custom_call" | custom-call | tf_op jit(solution)/shard_map/pack/pallas_call | solution.py:211
  2.3 1.5 %collective-permute-start.3 = (bf16[128,256]{1,0:T(8,128)(2,1)}, bf16[128,256]{1,0:T(8,128)(2,1)S(1)}, u32[]{:S(2)}, u32[]{:S(2)}) collective-permute-start(bf16[128,256]{1,0:T(8,128)(2,1)} %get-tuple-element.31.refs_0_), channel_id=1, source_target_pairs={{0,2},{1,3},{2,4},{3,5},{4,6},{5,7},{6,8},{7,9},{8,10},{9,11},{10,... | collective-permute-start | bytes 196616 | tf_op jit(solution)/shard_map/ppermute | solution.py:191
  3.9 1.6 %collective-permute-start.2 = (bf16[128,256]{1,0:T(8,128)(2,1)}, bf16[128,256]{1,0:T(8,128)(2,1)S(1)}, u32[]{:S(2)}, u32[]{:S(2)}) collective-permute-start(bf16[128,256]{1,0:T(8,128)(2,1)} %get-tuple-element.31.refs_0_), channel_id=1, source_target_pairs={{0,4},{1,5},{2,6},{3,7},{4,8},{5,9},{6,10},{7,11},{8,12},{9,13},{1... | collective-permute-start | bytes 196616 | tf_op jit(solution)/shard_map/ppermute | solution.py:191
  5.5 1.3 %collective-permute-done.3.refs_2_ = bf16[128,256]{1,0:T(8,128)(2,1)S(1)} collective-permute-done((bf16[128,256]{1,0:T(8,128)(2,1)}, bf16[128,256]{1,0:T(8,128)(2,1)S(1)}, u32[]{:S(2)}, u32[]{:S(2)}) %collective-permute-start.3) | collective-permute-done | bytes 65568 | tf_op jit(solution)/shard_map/ppermute | solution.py:191
  6.8 3.3 %collective-permute-done.2.refs_1_ = bf16[128,256]{1,0:T(8,128)(2,1)S(1)} collective-permute-done((bf16[128,256]{1,0:T(8,128)(2,1)}, bf16[128,256]{1,0:T(8,128)(2,1)S(1)}, u32[]{:S(2)}, u32[]{:S(2)}) %collective-permute-start.2) | collective-permute-done | bytes 65568 | tf_op jit(solution)/shard_map/ppermute | solution.py:191
  10.2 1.7 %collective-permute-start.1 = (bf16[128,768]{1,0:T(8,128)(2,1)}, bf16[128,768]{1,0:T(8,128)(2,1)S(1)}, u32[]{:S(2)}, u32[]{:S(2)}) collective-permute-start(bf16[128,768]{1,0:T(8,128)(2,1)} %get-tuple-element.30.refs_0_), channel_id=1, source_target_pairs={{0,2},{1,3},{2,4},{3,5},{4,6},{5,7},{6,8},{7,9},{8,10},{9,11},{10,... | collective-permute-start | bytes 589832 | tf_op jit(solution)/shard_map/ppermute | solution.py:191
  11.9 4.5 %delta.1.delta_ref = f32[64,128]{1,0:T(8,128)} custom-call(bf16[128,8192]{1,0:T(8,128)(2,1)} %o_ref.1, bf16[128,8192]{1,0:T(8,128)(2,1)} %do_ref.7), custom_call_target="tpu_custom_call" | custom-call | flops 100000000 | bytes 4194304 | tf_op jit(solution)/shard_map/delta/pallas_call | solution.py:178
  16.4 0.1 collective-permute-start.9
  16.6 0.5 copy-done.14
  17.0 0.1 copy-done.15
  17.2 7.1 %main.3 = (bf16[128,8192]{1,0:T(8,128)(2,1)}, f32[128,512]{1,0:T(8,128)}, f32[2,128,512]{2,1,0:T(8,128)}, bf16[2,128,512]{2,1,0:T(8,128)(2,1)}) custom-call(s32[8]{0:T(128)} %len_ref.5, s32[1]{0:T(128)} %bitcast.place_ref, bf16[128,8192]{1,0:T(8,128)(2,1)} %q_ref.5, bf16[128,8192]{1,0:T(8,128)(2,1)} %do_ref.7, f32[64,128]{1,0:T(8,128)} %delta.1.delta_ref, ...), custom_call_target="tpu_custom_call" | custom-call | flops 5000000000 | bytes 2097152 | tf_op jit(solution)/shard_map/main/pallas_call | solution.py:129
  24.3 0.6 collective-permute-start.7
  24.9 0.1 collective-permute-start.8
  25.0 1.0 %collective-permute-done.7.refs_3_ = bf16[128,768]{1,0:T(8,128)(2,1)S(1)} collective-permute-done((bf16[128,768]{1,0:T(8,128)(2,1)S(1)}, bf16[128,768]{1,0:T(8,128)(2,1)S(1)}, u32[]{:S(2)}, u32[]{:S(2)}) %collective-permute-start.7) | collective-permute-done | bytes 196640 | tf_op jit(solution)/shard_map/ppermute | solution.py:196
  26.0 0.4 collective-permute-done.8.refs_4_
  26.3 0.3 copy-done.10
  26.6 0.4 copy-done.11
  27.0 7.1 %main.4 = (bf16[128,8192]{1,0:T(8,128)(2,1)}, f32[128,512]{1,0:T(8,128)}, f32[2,128,512]{2,1,0:T(8,128)}, bf16[2,128,512]{2,1,0:T(8,128)(2,1)}) custom-call(s32[8]{0:T(128)} %len_ref.5, s32[1]{0:T(128)} %bitcast.place_ref, bf16[128,8192]{1,0:T(8,128)(2,1)} %q_ref.5, ...), custom_call_target="tpu_custom_call", output_to_operand_aliasing={{0}: (11, {}), {1}: (12, {}), {2}: (13, {}), {3}: (14, {})} | custom-call | flops 5000000000 | bytes 2097152 | tf_op jit(solution)/shard_map/main/pallas_call | solution.py:129
  34.1 0.3 collective-permute-start.10
  34.4 1.5 %collective-permute-done.10.refs_1_ = bf16[2,128,512]{2,1,0:T(8,128)(2,1)S(1)} collective-permute-done((bf16[2,128,512]{2,1,0:T(8,128)(2,1)}, bf16[2,128,512]{2,1,0:T(8,128)(2,1)S(1)}, u32[]{:S(2)}, u32[]{:S(2)}) %collective-permute-start.10) | collective-permute-done | bytes 262176 | tf_op jit(solution)/shard_map/ppermute | solution.py:196
  35.9 1.2 %fusion.1 = (bf16[128,512]{1,0:T(8,128)(2,1)S(1)}, bf16[128,512]{1,0:T(8,128)(2,1)S(1)}) fusion(f32[2,128,512]{2,1,0:T(8,128)} %get-tuple-element.39, bf16[2,128,512]{2,1,0:T(8,128)(2,1)S(1)} %collective-permute-done.10.refs_1_, pred[]{:T(512)S(6)} %eq.5), kind=kLoop, calls=%fused_computation.5 | loop fusion | flops 458752 | bytes 1048577 | tf_op jit(solution)/shard_map/convert_element_type | solution.py:278
  37.1 2.5 %collective-permute-start.11 = (bf16[128,512]{1,0:T(8,128)(2,1)S(1)}, bf16[128,512]{1,0:T(8,128)(2,1)S(1)}, u32[]{:S(2)}, u32[]{:S(2)}) collective-permute-start(bf16[128,512]{1,0:T(8,128)(2,1)S(1)} %get-tuple-element.46), channel_id=1, source_target_pairs={{0,12},{1,13},{2,14},{3,15},{4,0},{5,1},{6,2},{7,3},{8,4},{9,5},{1... | collective-permute-start | bytes 393224 | tf_op jit(solution)/shard_map/ppermute | solution.py:191
  39.6 1.7 %collective-permute-start.12 = (bf16[128,512]{1,0:T(8,128)(2,1)S(1)}, bf16[128,512]{1,0:T(8,128)(2,1)S(1)}, u32[]{:S(2)}, u32[]{:S(2)}) collective-permute-start(bf16[128,512]{1,0:T(8,128)(2,1)S(1)} %get-tuple-element.47), channel_id=1, source_target_pairs={{0,14},{1,15},{2,0},{3,1},{4,2},{5,3},{6,4},{7,5},{8,6},{9,7},{10,... | collective-permute-start | bytes 393224 | tf_op jit(solution)/shard_map/ppermute | solution.py:191
  41.3 11.6 %main.5 = (bf16[128,8192]{1,0:T(8,128)(2,1)}, f32[128,512]{1,0:T(8,128)}, f32[2,128,512]{2,1,0:T(8,128)}, bf16[2,128,512]{2,1,0:T(8,128)(2,1)}) custom-call(s32[8]{0:T(128)} %len_ref.5, s32[1]{0:T(128)} %bitcast.place_ref, bf16[128,8192]{1,0:T(8,128)(2,1)} %q_ref.5, bf16[128,8192]{1,0:T(8,128)(2,1)} %do_ref.7, ...), custom_call_target="tpu_custom_call", output_to_operand_aliasing={{0}: (11, {})} | custom-call | flops 10000000000 | bytes 4194304 | tf_op jit(solution)/shard_map/main/pallas_call | solution.py:129
  53.0 1.7 %collective-permute-done.13.refs_5_ = bf16[2,128,512]{2,1,0:T(8,128)(2,1)S(1)} collective-permute-done((bf16[2,128,512]{2,1,0:T(8,128)(2,1)}, bf16[2,128,512]{2,1,0:T(8,128)(2,1)S(1)}, u32[]{:S(2)}, u32[]{:S(2)}) %collective-permute-start.13) | collective-permute-done | bytes 262176 | tf_op jit(solution)/shard_map/ppermute | solution.py:196
  54.7 1.2 %fusion.3 = (bf16[128,512]{1,0:T(8,128)(2,1)S(1)}, bf16[128,512]{1,0:T(8,128)(2,1)S(1)}) fusion(f32[2,128,512]{2,1,0:T(8,128)} %get-tuple-element.54, bf16[2,128,512]{2,1,0:T(8,128)(2,1)S(1)} %collective-permute-done.13.refs_5_, pred[]{:T(512)S(6)} %eq.5), kind=kLoop, calls=%fused_computation.7 | loop fusion | flops 458752 | bytes 1048577 | tf_op jit(solution)/shard_map/convert_element_type | solution.py:278
  55.9 0.4 collective-permute-start.14
  56.4 1.7 %collective-permute-start.15 = (bf16[128,512]{1,0:T(8,128)(2,1)S(1)}, bf16[128,512]{1,0:T(8,128)(2,1)S(1)}, u32[]{:S(2)}, u32[]{:S(2)}) collective-permute-start(bf16[128,512]{1,0:T(8,128)(2,1)S(1)} %get-tuple-element.57), channel_id=1, source_target_pairs={{0,14},{1,15},{2,0},{3,1},{4,2},{5,3},{6,4},{7,5},{8,6},{9,7},{10,... | collective-permute-start | bytes 393224 | tf_op jit(solution)/shard_map/ppermute | solution.py:191
  58.1 3.5 %collective-permute-done.14.refs_6_ = bf16[128,512]{1,0:T(8,128)(2,1)S(1)} collective-permute-done((bf16[128,512]{1,0:T(8,128)(2,1)S(1)}, bf16[128,512]{1,0:T(8,128)(2,1)S(1)}, u32[]{:S(2)}, u32[]{:S(2)}) %collective-permute-start.14) | collective-permute-done | bytes 131104 | tf_op jit(solution)/shard_map/ppermute | solution.py:191
  61.5 4.1 %collective-permute-done.15.refs_7_ = bf16[128,512]{1,0:T(8,128)(2,1)S(1)} collective-permute-done((bf16[128,512]{1,0:T(8,128)(2,1)S(1)}, bf16[128,512]{1,0:T(8,128)(2,1)S(1)}, u32[]{:S(2)}, u32[]{:S(2)}) %collective-permute-start.15) | collective-permute-done | bytes 131104 | tf_op jit(solution)/shard_map/ppermute | solution.py:191
  65.6 0.6 copy-done.5
  66.3 2.2 %sum.1 = (bf16[128,512]{1,0:T(8,128)(2,1)}, bf16[128,512]{1,0:T(8,128)(2,1)}) custom-call(s32[1]{0:T(128)} %bitcast.place_ref, f32[128,512]{1,0:T(8,128)} %get-tuple-element.48.refs_0_, bf16[2,128,512]{2,1,0:T(8,128)(2,1)} %copy-done, bf16[128,512]{1,0:T(8,128)(2,1)} %copy-done.2, bf16[128,512]{1,0:T(8,128)(2,1)} %copy-done.3, ...), custom_call_target="tpu_custom_call" | custom-call | tf_op jit(solution)/shard_map/sum/pallas_call | solution.py:235
  (42 shorter events, 0.2 us)
Async XLA Ops:
  2.3 4.5 %collective-permute-start.3 = (bf16[128,256]{1,0:T(8,128)(2,1)}, bf16[128,256]{1,0:T(8,128)(2,1)S(1)}, u32[]{:S(2)}, u32[]{:S(2)}) collective-permute-start(bf16[128,256]{1,0:T(8,128)(2,1)} %get-tuple-element.31.refs_0_), channel_id=1, source_target_pairs={{0,2},{1,3},{2,4},{3,5},{4,6},{5,7},{6,8},{7,9},{8,10},{9,11},{10,... | collective-permute-start | bytes 196616 | tf_op jit(solution)/shard_map/ppermute | solution.py:191
  3.9 6.3 %collective-permute-start.2 = (bf16[128,256]{1,0:T(8,128)(2,1)}, bf16[128,256]{1,0:T(8,128)(2,1)S(1)}, u32[]{:S(2)}, u32[]{:S(2)}) collective-permute-start(bf16[128,256]{1,0:T(8,128)(2,1)} %get-tuple-element.31.refs_0_), channel_id=1, source_target_pairs={{0,4},{1,5},{2,6},{3,7},{4,8},{5,9},{6,10},{7,11},{8,12},{9,13},{1... | collective-permute-start | bytes 196616 | tf_op jit(solution)/shard_map/ppermute | solution.py:191
  5.5 10.9 %collective-permute-start.6 = (bf16[128,256]{1,0:T(8,128)(2,1)}, bf16[128,256]{1,0:T(8,128)(2,1)S(1)}, u32[]{:S(2)}, u32[]{:S(2)}) collective-permute-start(bf16[128,256]{1,0:T(8,128)(2,1)} %get-tuple-element.31.refs_0_), channel_id=1, source_target_pairs={{0,1},{1,0},{2,3},{3,2},{4,5},{5,4},{6,7},{7,6},{8,9},{9,8},{10,11... | collective-permute-start | bytes 196616 | tf_op jit(solution)/shard_map/ppermute | solution.py:196
  6.8 9.6 %copy-start.12 = (bf16[128,256]{1,0:T(8,128)(2,1)}, bf16[128,256]{1,0:T(8,128)(2,1)S(1)}, u32[]{:S(2)}) copy-start(bf16[128,256]{1,0:T(8,128)(2,1)S(1)} %collective-permute-done.3.refs_2_) | copy-start | bytes 196612
  6.8 9.7 %collective-permute-start.4 = (bf16[128,256]{1,0:T(8,128)(2,1)S(1)}, bf16[128,256]{1,0:T(8,128)(2,1)S(1)}, u32[]{:S(2)}, u32[]{:S(2)}) collective-permute-start(bf16[128,256]{1,0:T(8,128)(2,1)S(1)} %collective-permute-done.3.refs_2_), channel_id=1, source_target_pairs={{0,1},{1,0},{2,3},{3,2},{4,5},{5,4},{6,7},{7,6},{8,9},{9,8},{10,11... | collective-permute-start | bytes 196616 | tf_op jit(solution)/shard_map/ppermute | solution.py:196
  10.2 6.2 %copy-start.13 = (bf16[128,256]{1,0:T(8,128)(2,1)}, bf16[128,256]{1,0:T(8,128)(2,1)S(1)}, u32[]{:S(2)}) copy-start(bf16[128,256]{1,0:T(8,128)(2,1)S(1)} %collective-permute-done.2.refs_1_) | copy-start | bytes 196612
  10.2 6.4 %collective-permute-start.5 = (bf16[128,256]{1,0:T(8,128)(2,1)S(1)}, bf16[128,256]{1,0:T(8,128)(2,1)S(1)}, u32[]{:S(2)}, u32[]{:S(2)}) collective-permute-start(bf16[128,256]{1,0:T(8,128)(2,1)S(1)} %collective-permute-done.2.refs_1_), channel_id=1, source_target_pairs={{0,1},{1,0},{2,3},{3,2},{4,5},{5,4},{6,7},{7,6},{8,9},{9,8},{10,11... | collective-permute-start | bytes 196616 | tf_op jit(solution)/shard_map/ppermute | solution.py:196
  10.2 14.1 %collective-permute-start = (bf16[128,768]{1,0:T(8,128)(2,1)}, bf16[128,768]{1,0:T(8,128)(2,1)S(1)}, u32[]{:S(2)}, u32[]{:S(2)}) collective-permute-start(bf16[128,768]{1,0:T(8,128)(2,1)} %get-tuple-element.30.refs_0_), channel_id=1, source_target_pairs={{0,4},{1,5},{2,6},{3,7},{4,8},{5,9},{6,10},{7,11},{8,12},{9,13},{1... | collective-permute-start | bytes 589832 | tf_op jit(solution)/shard_map/ppermute | solution.py:191
  10.2 14.1 %collective-permute-start.1 = (bf16[128,768]{1,0:T(8,128)(2,1)}, bf16[128,768]{1,0:T(8,128)(2,1)S(1)}, u32[]{:S(2)}, u32[]{:S(2)}) collective-permute-start(bf16[128,768]{1,0:T(8,128)(2,1)} %get-tuple-element.30.refs_0_), channel_id=1, source_target_pairs={{0,2},{1,3},{2,4},{3,5},{4,6},{5,7},{6,8},{7,9},{8,10},{9,11},{10,... | collective-permute-start | bytes 589832 | tf_op jit(solution)/shard_map/ppermute | solution.py:191
  11.9 4.5 %copy-start.6 = (bf16[128,768]{1,0:T(8,128)(2,1)S(1)}, bf16[128,768]{1,0:T(8,128)(2,1)}, u32[]{:S(2)}) copy-start(bf16[128,768]{1,0:T(8,128)(2,1)} %get-tuple-element.30.refs_0_) | copy-start | bytes 589828
  16.4 0.6 copy-start.14
  16.4 8.5 %collective-permute-start.9 = (bf16[128,768]{1,0:T(8,128)(2,1)S(1)}, bf16[128,768]{1,0:T(8,128)(2,1)S(1)}, u32[]{:S(2)}, u32[]{:S(2)}) collective-permute-start(bf16[128,768]{1,0:T(8,128)(2,1)S(1)} %copy-done.6), channel_id=1, source_target_pairs={{0,1},{1,0},{2,3},{3,2},{4,5},{5,4},{6,7},{7,6},{8,9},{9,8},{10,11... | collective-permute-start | bytes 589832 | tf_op jit(solution)/shard_map/ppermute | solution.py:196
  16.5 0.6 copy-start.16
  24.3 2.0 %copy-start.7 = (bf16[128,768]{1,0:T(8,128)(2,1)}, bf16[128,768]{1,0:T(8,128)(2,1)S(1)}, u32[]{:S(2)}) copy-start(bf16[128,768]{1,0:T(8,128)(2,1)S(1)} %collective-permute-done.refs_1_) | copy-start | bytes 589828
  24.3 2.0 %copy-start.8 = (bf16[128,768]{1,0:T(8,128)(2,1)}, bf16[128,768]{1,0:T(8,128)(2,1)S(1)}, u32[]{:S(2)}) copy-start(bf16[128,768]{1,0:T(8,128)(2,1)S(1)} %collective-permute-done.1.refs_2_) | copy-start | bytes 589828
  24.3 1.6 %collective-permute-start.7 = (bf16[128,768]{1,0:T(8,128)(2,1)S(1)}, bf16[128,768]{1,0:T(8,128)(2,1)S(1)}, u32[]{:S(2)}, u32[]{:S(2)}) collective-permute-start(bf16[128,768]{1,0:T(8,128)(2,1)S(1)} %collective-permute-done.1.refs_2_), channel_id=1, source_target_pairs={{0,1},{1,0},{2,3},{3,2},{4,5},{5,4},{6,7},{7,6},{8,9},{9,8},{10,11... | collective-permute-start | bytes 589832 | tf_op jit(solution)/shard_map/ppermute | solution.py:196
  24.9 1.4 %collective-permute-start.8 = (bf16[128,768]{1,0:T(8,128)(2,1)S(1)}, bf16[128,768]{1,0:T(8,128)(2,1)S(1)}, u32[]{:S(2)}, u32[]{:S(2)}) collective-permute-start(bf16[128,768]{1,0:T(8,128)(2,1)S(1)} %collective-permute-done.refs_1_), channel_id=1, source_target_pairs={{0,1},{1,0},{2,3},{3,2},{4,5},{5,4},{6,7},{7,6},{8,9},{9,8},{10,11... | collective-permute-start | bytes 589832 | tf_op jit(solution)/shard_map/ppermute | solution.py:196
  25.0 1.4 %copy-start.9 = (bf16[128,768]{1,0:T(8,128)(2,1)}, bf16[128,768]{1,0:T(8,128)(2,1)S(1)}, u32[]{:S(2)}) copy-start(bf16[128,768]{1,0:T(8,128)(2,1)S(1)} %collective-permute-done.9.refs_5_) | copy-start | bytes 589828
  26.0 0.7 copy-start.10
  26.3 0.7 %copy-start.11 = (bf16[128,768]{1,0:T(8,128)(2,1)}, bf16[128,768]{1,0:T(8,128)(2,1)S(1)}, u32[]{:S(2)}) copy-start(bf16[128,768]{1,0:T(8,128)(2,1)S(1)} %collective-permute-done.8.refs_4_) | copy-start | bytes 589828
  34.1 1.7 %collective-permute-start.10 = (bf16[2,128,512]{2,1,0:T(8,128)(2,1)}, bf16[2,128,512]{2,1,0:T(8,128)(2,1)S(1)}, u32[]{:S(2)}, u32[]{:S(2)}) collective-permute-start(bf16[2,128,512]{2,1,0:T(8,128)(2,1)} %get-tuple-element.40), channel_id=1, source_target_pairs={{0,1},{1,0},{2,3},{3,2},{4,5},{5,4},{6,7},{7,6},{8,9},{9,8},{10,11... | collective-permute-start | bytes 786440 | tf_op jit(solution)/shard_map/ppermute | solution.py:196
  35.9 17.0 %copy-start = (bf16[2,128,512]{2,1,0:T(8,128)(2,1)}, bf16[2,128,512]{2,1,0:T(8,128)(2,1)S(1)}, u32[]{:S(2)}) copy-start(bf16[2,128,512]{2,1,0:T(8,128)(2,1)S(1)} %collective-permute-done.10.refs_1_) | copy-start | bytes 786436
  37.1 15.8 %collective-permute-start.11 = (bf16[128,512]{1,0:T(8,128)(2,1)S(1)}, bf16[128,512]{1,0:T(8,128)(2,1)S(1)}, u32[]{:S(2)}, u32[]{:S(2)}) collective-permute-start(bf16[128,512]{1,0:T(8,128)(2,1)S(1)} %get-tuple-element.46), channel_id=1, source_target_pairs={{0,12},{1,13},{2,14},{3,15},{4,0},{5,1},{6,2},{7,3},{8,4},{9,5},{1... | collective-permute-start | bytes 393224 | tf_op jit(solution)/shard_map/ppermute | solution.py:191
  39.6 13.3 %collective-permute-start.12 = (bf16[128,512]{1,0:T(8,128)(2,1)S(1)}, bf16[128,512]{1,0:T(8,128)(2,1)S(1)}, u32[]{:S(2)}, u32[]{:S(2)}) collective-permute-start(bf16[128,512]{1,0:T(8,128)(2,1)S(1)} %get-tuple-element.47), channel_id=1, source_target_pairs={{0,14},{1,15},{2,0},{3,1},{4,2},{5,3},{6,4},{7,5},{8,6},{9,7},{10,... | collective-permute-start | bytes 393224 | tf_op jit(solution)/shard_map/ppermute | solution.py:191
  52.9 12.7 %copy-start.2 = (bf16[128,512]{1,0:T(8,128)(2,1)}, bf16[128,512]{1,0:T(8,128)(2,1)S(1)}, u32[]{:S(2)}) copy-start(bf16[128,512]{1,0:T(8,128)(2,1)S(1)} %collective-permute-done.11.refs_2_) | copy-start | bytes 393220
  52.9 12.7 %copy-start.3 = (bf16[128,512]{1,0:T(8,128)(2,1)}, bf16[128,512]{1,0:T(8,128)(2,1)S(1)}, u32[]{:S(2)}) copy-start(bf16[128,512]{1,0:T(8,128)(2,1)S(1)} %collective-permute-done.12.refs_3_) | copy-start | bytes 393220
  52.9 1.8 %collective-permute-start.13 = (bf16[2,128,512]{2,1,0:T(8,128)(2,1)}, bf16[2,128,512]{2,1,0:T(8,128)(2,1)S(1)}, u32[]{:S(2)}, u32[]{:S(2)}) collective-permute-start(bf16[2,128,512]{2,1,0:T(8,128)(2,1)} %get-tuple-element.53), channel_id=1, source_target_pairs={{0,1},{1,0},{2,3},{3,2},{4,5},{5,4},{6,7},{7,6},{8,9},{9,8},{10,11... | collective-permute-start | bytes 786440 | tf_op jit(solution)/shard_map/ppermute | solution.py:196
  54.7 10.9 %copy-start.1 = (bf16[2,128,512]{2,1,0:T(8,128)(2,1)}, bf16[2,128,512]{2,1,0:T(8,128)(2,1)S(1)}, u32[]{:S(2)}) copy-start(bf16[2,128,512]{2,1,0:T(8,128)(2,1)S(1)} %collective-permute-done.13.refs_5_) | copy-start | bytes 786436
  55.9 5.6 %collective-permute-start.14 = (bf16[128,512]{1,0:T(8,128)(2,1)S(1)}, bf16[128,512]{1,0:T(8,128)(2,1)S(1)}, u32[]{:S(2)}, u32[]{:S(2)}) collective-permute-start(bf16[128,512]{1,0:T(8,128)(2,1)S(1)} %get-tuple-element.58), channel_id=1, source_target_pairs={{0,12},{1,13},{2,14},{3,15},{4,0},{5,1},{6,2},{7,3},{8,4},{9,5},{1... | collective-permute-start | bytes 393224 | tf_op jit(solution)/shard_map/ppermute | solution.py:191
  56.4 9.3 %collective-permute-start.15 = (bf16[128,512]{1,0:T(8,128)(2,1)S(1)}, bf16[128,512]{1,0:T(8,128)(2,1)S(1)}, u32[]{:S(2)}, u32[]{:S(2)}) collective-permute-start(bf16[128,512]{1,0:T(8,128)(2,1)S(1)} %get-tuple-element.57), channel_id=1, source_target_pairs={{0,14},{1,15},{2,0},{3,1},{4,2},{5,3},{6,4},{7,5},{8,6},{9,7},{10,... | collective-permute-start | bytes 393224 | tf_op jit(solution)/shard_map/ppermute | solution.py:191
  61.5 4.1 %copy-start.4 = (bf16[128,512]{1,0:T(8,128)(2,1)}, bf16[128,512]{1,0:T(8,128)(2,1)S(1)}, u32[]{:S(2)}) copy-start(bf16[128,512]{1,0:T(8,128)(2,1)S(1)} %collective-permute-done.14.refs_6_) | copy-start | bytes 393220
  65.6 0.6 copy-start.5
  (1 other events, 0.6 us)

commit v3 on v1

v3 whole, which is shorter than its diff:
```python
import functools
import math

import jax
import jax.numpy as jnp
from jax import lax
from jax.experimental import pallas as pl
from jax.experimental.pallas import tpu as pltpu
from jax.sharding import PartitionSpec as P

HQ = 64
HK = 4
HD = 128
SPAN = 4
PER = HQ // HK
FACTOR = 1.0 / math.sqrt(HD)
LOG2E = math.log2(math.e)
F32 = jnp.float32
BF = jnp.bfloat16
NT = (((1,), (1,)), ((), ()))
NN = (((1,), (0,)), ((), ()))
MIB = 2**20
CHUNK = 4
STEPS = 1
LATE_STEPS = 1


def dot(a, b, dims):
    return lax.dot_general(a, b, dims, preferred_element_type=F32)


def starts_row(len_ref, qpos):
    def step(j, c):
        end, start = c
        end = end + len_ref[j]
        return end, jnp.where(end <= qpos, end, start)

    return lax.fori_loop(0, len_ref.shape[0], step, (jnp.int32(0), jnp.zeros_like(qpos)))[1]


def stacked(ref, hs):
    return jnp.concatenate([ref[:, h * HD : (h + 1) * HD] for h in hs], axis=0)


def chunks(steps):
    return [list(range(i, i + CHUNK)) for i in range(0, PER // steps, CHUNK)]


def main_kernel(len_ref, place_ref, q_ref, do_ref, delta_ref, *refs):
    k_refs, v_refs = refs[0:6], refs[6:12]
    d_ref, p_ref, far_ref, swap_ref = refs[12:16]
    kall, vall, bias, acck, accv = refs[16:]
    rows = q_ref.shape[0]
    place = place_ref[0]
    core = place % 2
    dists = (SPAN, 2, 1 + 2 * core, 3 - 2 * core)
    u = lax.broadcasted_iota(jnp.int32, (rows, rows), 0)
    t = lax.broadcasted_iota(jnp.int32, (rows, rows), 1)
    tri = u <= t

    @pl.when((pl.program_id(0) == 0) & (pl.program_id(1) == 0))
    def _():
        start = starts_row(len_ref, place * rows + lax.broadcasted_iota(jnp.int32, (1, rows), 1))
        for n in range(4):
            pos = (place - dists[n]) * rows + u
            if n == 0:
                pos = jnp.where(tri, place * rows + u, pos)
            bias[n * rows : (n + 1) * rows, :] = jnp.where(pos >= start, 0.0, -jnp.inf).astype(F32)

    @pl.when(pl.program_id(1) == 0)
    def _():
        for all_ref, block_refs in ((kall, k_refs), (vall, v_refs)):
            for j in range(5):
                block = block_refs[j][...]
                if j == 4:
                    block = jnp.where(core == 0, block, block_refs[5][...])
                all_ref[j * rows : (j + 1) * rows, :] = block
        acck[...] = jnp.zeros_like(acck)
        accv[...] = jnp.zeros_like(accv)

    def tile(x, n, c):
        if n == 0:
            return jnp.where(tri, x[0:rows, c], x[rows : 2 * rows, c])
        return x[(n + 1) * rows : (n + 2) * rows, c]

    for hs in chunks(STEPS):
        q2 = stacked(q_ref, hs)
        do2 = stacked(do_ref, hs)
        s = dot(kall[...], q2, NT)
        dp = dot(vall[...], do2, NT)
        pb = [[None] * CHUNK for _ in range(4)]
        db = [[None] * CHUNK for _ in range(4)]
        for i, h in enumerate(hs):
            c = slice(i * rows, (i + 1) * rows)
            at = slice(h * rows, (h + 1) * rows)
            tiles = [tile(s, n, c) + bias[n * rows : (n + 1) * rows, :] for n in range(4)]
            top = jnp.max(functools.reduce(jnp.maximum, tiles), axis=0, keepdims=True)
            es = [jnp.exp2((x - top) * (FACTOR * LOG2E)) for x in tiles]
            rl = 1.0 / jnp.sum(functools.reduce(jnp.add, es), axis=0, keepdims=True)
            dl = delta_ref[pl.ds(pl.program_id(1) * (PER // STEPS) + h, 1), :]
            for n in range(4):
                p = es[n] * rl
                d = (FACTOR * p) * (tile(dp, n, c) - dl)
                if n == 0:
                    p_ref[:, at] = jnp.where(tri, p, 0.0).astype(BF)
                    d_ref[0:rows, at] = jnp.where(tri, d, 0.0).astype(BF)
                    p, d = jnp.where(tri, 0.0, p), jnp.where(tri, 0.0, d)
                pb[n][i] = p.astype(BF)
                db[n][i] = d.astype(BF)
        probs = jnp.concatenate([jnp.concatenate(r, axis=1) for r in pb], axis=0)
        grads = jnp.concatenate([jnp.concatenate(r, axis=1) for r in db], axis=0)
        d_ref[rows:, hs[0] * rows : (hs[-1] + 1) * rows] = grads
        accv[...] += dot(probs, do2, NN)
        acck[...] += dot(grads, q2, NN)

    @pl.when(pl.program_id(1) == STEPS - 1)
    def _():
        for w, acc in enumerate((acck, accv)):
            far_ref[w] = acc[0:rows, :]
            far_ref[2 + w] = acc[rows : 2 * rows, :]
            swap_ref[2 + w] = acc[2 * rows : 3 * rows, :].astype(BF)
            swap_ref[w] = acc[3 * rows : 4 * rows, :].astype(BF)


def specs(rows, steps):
    def wide(height):
        return pl.BlockSpec((height, PER // steps * HD), lambda g, i, *_: (0, g * steps + i))

    head = pl.BlockSpec((rows, HD), lambda g, i, *_: (0, g))

    def heads(n):
        return pl.BlockSpec((n, rows, HD), lambda g, i, *_: (0, 0, g))

    return wide, head, heads


def in_hbm(*xs):
    return [pltpu.with_memory_space_constraint(x, pltpu.HBM) for x in xs]


def main_call(lengths, index, q, do, delta, ks, vs):
    rows = q.shape[0]
    wide, head, heads = specs(rows, STEPS)
    return pl.pallas_call(
        main_kernel,
        grid_spec=pltpu.PrefetchScalarGridSpec(
            num_scalar_prefetch=2,
            grid=(HK, STEPS),
            in_specs=[wide(rows), wide(rows), pl.BlockSpec((PER, rows), lambda g, *_: (g, 0))] + [head] * 12,
            out_specs=[wide(5 * rows), wide(rows), heads(4), heads(4)],
            scratch_shapes=[
                pltpu.VMEM((5 * rows, HD), BF),
                pltpu.VMEM((5 * rows, HD), BF),
                pltpu.VMEM((4 * rows, rows), F32),
                pltpu.VMEM((4 * rows, HD), F32),
                pltpu.VMEM((4 * rows, HD), F32),
            ],
        ),
        out_shape=[
            pltpu.HBM((5 * rows, HQ * HD), BF),
            pltpu.HBM((rows, HQ * HD), BF),
            jax.ShapeDtypeStruct((4, rows, HK * HD), F32),
            jax.ShapeDtypeStruct((4, rows, HK * HD), BF),
        ],
        compiler_params=pltpu.CompilerParams(vmem_limit_bytes=40 * MIB),
        cost_estimate=pl.CostEstimate(flops=16 * 10**9, bytes_accessed=16 * MIB, transcendentals=4 * 10**6),
        name="main",
    )(lengths, index, *in_hbm(q, do, delta, *ks, *vs))


def late_kernel(place_ref, q_ref, do_ref, d_ref, p_ref, *refs):
    k_refs = refs[0:6]
    dq_ref, own_ref, kt = refs[6:]
    rows = q_ref.shape[0]
    core = place_ref[0] % 2

    @pl.when(pl.program_id(1) == 0)
    def _():
        for j in range(5):
            block = k_refs[j][...]
            if j == 4:
                block = jnp.where(core == 0, block, k_refs[5][...])
            kt[:, j * rows : (j + 1) * rows] = block.astype(F32).T.astype(BF)
        own_ref[...] = jnp.zeros_like(own_ref)

    for hs in chunks(LATE_STEPS):
        at = slice(hs[0] * rows, (hs[-1] + 1) * rows)
        dqt = dot(kt[...], d_ref[:, at], NN)
        for i, h in enumerate(hs):
            dq_ref[:, h * HD : (h + 1) * HD] = dqt[:, i * rows : (i + 1) * rows].T.astype(BF)
        own_ref[0] += dot(d_ref[0:rows, at], stacked(q_ref, hs), NN)
        own_ref[1] += dot(p_ref[:, at], stacked(do_ref, hs), NN)


def late_call(index, q, do, grads, probs, ks):
    rows = q.shape[0]
    wide, head, heads = specs(rows, LATE_STEPS)
    return pl.pallas_call(
        late_kernel,
        grid_spec=pltpu.PrefetchScalarGridSpec(
            num_scalar_prefetch=1,
            grid=(HK, LATE_STEPS),
            in_specs=[wide(rows), wide(rows), wide(5 * rows), wide(rows)] + [head] * 6,
            out_specs=[wide(rows), heads(2)],
            scratch_shapes=[pltpu.VMEM((HD, 5 * rows), BF)],
        ),
        out_shape=[jax.ShapeDtypeStruct((rows, HQ * HD), BF), jax.ShapeDtypeStruct((2, rows, HK * HD), F32)],
        compiler_params=pltpu.CompilerParams(vmem_limit_bytes=40 * MIB),
        cost_estimate=pl.CostEstimate(flops=8 * 10**9, bytes_accessed=20 * MIB, transcendentals=0),
        name="late",
    )(index, *in_hbm(q, do, grads, probs, *ks))


def delta_kernel(o_ref, do_ref, out_ref):
    rows = o_ref.shape[0]
    ones = jnp.ones((8, 2 * HD), BF)
    for h in range(PER):
        c = slice(h * HD, (h + 1) * HD)
        x = o_ref[:, c].astype(F32) * do_ref[:, c].astype(F32)
        high = x.astype(BF)
        low = (x - high.astype(F32)).astype(BF)
        out_ref[h : h + 1, :] = dot(ones, jnp.concatenate([high, low], axis=1), NT)[0:1, :]


def delta_call(o, do):
    rows = o.shape[0]
    big = pl.BlockSpec((rows, PER * HD), lambda g: (0, g))
    return pl.pallas_call(
        delta_kernel,
        grid=(HK,),
        in_specs=[big, big],
        out_specs=pl.BlockSpec((PER, rows), lambda g: (g, 0)),
        out_shape=jax.ShapeDtypeStruct((HQ, rows), F32),
        cost_estimate=pl.CostEstimate(flops=10**8, bytes_accessed=4 * MIB, transcendentals=0),
        name="delta",
    )(o, do)


def moved(x, by):
    size = lax.axis_size("ctx")
    return lax.ppermute(x, "ctx", [(i, (i + by) % size) for i in range(size)])


def swapped(x):
    size = lax.axis_size("ctx")
    return lax.ppermute(x, "ctx", [(i, i ^ 1) for i in range(size)])


def moved(x, by):
    size = lax.axis_size("ctx")
    return lax.ppermute(x, "ctx", [(i, (i + by) % size) for i in range(size)])


def swapped(x):
    size = lax.axis_size("ctx")
    return lax.ppermute(x, "ctx", [(i, i ^ 1) for i in range(size)])


def on_device(queries, keys, values, outputs, d_out, lengths):
    place = lax.axis_index("ctx").astype(jnp.int32)
    even = place % 2 == 0
    index = place.reshape(1)
    k2, k4 = moved(keys, 2), moved(keys, 4)
    v2, v4 = moved(values, 2), moved(values, 4)
    km, vm = swapped(keys), swapped(values)
    delta = delta_call(outputs, d_out)
    k2, k4, v2, v4, delta = lax.optimization_barrier((k2, k4, v2, v4, delta))
    ks = (keys, k4, k2, swapped(k2), swapped(k4), km)
    vs = (values, v4, v2, swapped(v2), swapped(v4), vm)
    grads, probs, far, swap = main_call(lengths, index, queries, d_out, delta, ks, vs)
    back = swapped(swap).astype(F32)
    near, mid = back[0:2], back[2:4]
    far4 = [(far[w] + jnp.where(even, 0.0, near[w])).astype(BF) for w in range(2)]
    far2 = [(far[2 + w] + mid[w]).astype(BF) for w in range(2)]
    index, *both = lax.optimization_barrier((index, *far4, *far2))
    got = [moved(x, -4 if i < 2 else -2).astype(F32) for i, x in enumerate(both)]
    d_queries, own = late_call(index, queries, d_out, grads, probs, ks)
    total = [(own[w] + jnp.where(even, near[w], 0.0) + got[w] + got[2 + w]).astype(BF) for w in range(2)]
    return d_queries, total[0], total[1]


def solution(mesh):
    spec = P(("group", "ctx"), None)
    return jax.shard_map(
        on_device,
        mesh=mesh,
        in_specs=(spec,) * 5 + (P("group"),),
        out_specs=(spec,) * 3,
        check_vma=False,
    )
```

time: 66.4 us -> 56.9 us (0.86)
  waiting for transfers between devices: 17.7 us -> 7.68 us
  Pallas kernels: 24.9 us -> 31.9 us
  starting transfers between devices: 19.4 us -> 13.7 us
  local copies, waits for them, and re-layouts: 1.51 us -> 0.65 us
    ppermute x6 -> x8, waiting for transfers between devices: 15.1 us -> 5.1 us  [moved(): return lax.ppermute(x, 'ctx', [(i, (i + by) % size) for i in range(size)])]
    pallas_call x1 -> x2, Pallas kernels: 20.4 us -> 27.5 us  [the longest x1 18.4 us: main_call(): pl.pallas_call(main_kernel, grid_spec=pltpu.PrefetchScalarGridSpec(num_sc...]
    ppermute x6 -> x8, starting transfers between devices: 18.5 us -> 11.6 us  [moved(): return lax.ppermute(x, 'ctx', [(i, (i + by) % size) for i in range(size)])]
    ppermute x4 -> x7, starting transfers between devices: 0.9 us -> 2.06 us  [swapped(): return lax.ppermute(x, 'ctx', [(i, i ^ 1) for i in range(size)])]
    select_n x1 -> x0, other arithmetic: 1.01 us -> none  [on_device(): jnp.where(even, jnp.stack([keys, values]), jnp.stack([k4, v4]))]
    squeeze x2 -> x0, local copies, waits for them, and re-layouts: 0.73 us -> none  [the longest x1 0.72 us: on_device(): return (d_queries, total[0], total[1])]
    convert_element_type x2, other arithmetic: 0.42 us -> 1.12 us  [the longest x1 0.86 us: on_device(): (own[w] + jnp.where(even, near[w], 0.0) + got[w] + got[2 + w]).astype(BF)]
    ppermute x4 -> x7, waiting for transfers between devices: 2.58 us -> 2.58 us  [swapped(): return lax.ppermute(x, 'ctx', [(i, i ^ 1) for i in range(size)])]
  transfers between devices with their start and end apart: 10 -> 15, of which waited for: 6 -> 7; matrix products, arithmetic and copies ran while one was open for 0% -> 0% of each run, Pallas kernels for 7% -> 24%
where the time goes in v3:
time: 56.9 us; the launch traced here: 55.9 us
  Pallas kernels  31.9 us (56%)
  starting transfers between devices  13.7 us (24%)
  waiting for transfers between devices  7.68 us (13%)
  other arithmetic  1.24 us (2%)
  between operations  0.76 us (1%)
  local copies, waits for them, and re-layouts  0.65 us (1%)
    pallas_call x1, Pallas kernels, main_call(): pl.pallas_call(main_kernel, grid_spec=pltpu.PrefetchScalarGridSpec(num_sc...  18.4 us
    ppermute x8, starting transfers between devices, moved(): return lax.ppermute(x, 'ctx', [(i, (i + by) % size) for i in range(size)])  11.6 us
    pallas_call x1, Pallas kernels, late_call(): pl.pallas_call(late_kernel, grid_spec=pltpu.PrefetchScalarGridSpec(num_sc...  9.04 us
    ppermute x8, waiting for transfers between devices, moved(): return lax.ppermute(x, 'ctx', [(i, (i + by) % size) for i in range(size)])  5.1 us
    pallas_call x1, Pallas kernels, delta_call(): pl.pallas_call(delta_kernel, grid=(HK,), in_specs=[big, big], out_specs=p...  4.45 us
    ppermute x7, waiting for transfers between devices, swapped(): return lax.ppermute(x, 'ctx', [(i, i ^ 1) for i in range(size)])  2.58 us
    ppermute x7, starting transfers between devices, swapped(): return lax.ppermute(x, 'ctx', [(i, i ^ 1) for i in range(size)])  2.06 us
  transfers between devices with their start and end apart: 15, of which 7 were waited for; matrix products, arithmetic and copies ran while one was open for 0% of the time, Pallas kernels for 24%

profile of v3, /device:TPU:6, one launch (start us, length us, event | category | flops | bytes accessed | tf_op | source)
XLA Modules:
  0.0 55.9 jit_solution(5807672487557897198)
XLA Ops:
  0.6 0.0 copy-start.1
  0.7 1.6 %collective-permute-start.3 = (bf16[128,512]{1,0:T(8,128)(2,1)}, bf16[128,512]{1,0:T(8,128)(2,1)S(1)}, u32[]{:S(2)}, u32[]{:S(2)}) collective-permute-start(bf16[128,512]{1,0:T(8,128)(2,1)} %refs_6_.1), channel_id=1, source_target_pairs={{0,4},{1,5},{2,6},{3,7},{4,8},{5,9},{6,10},{7,11},{8,12},{9,13},{1... | collective-permute-start | bytes 393224 | tf_op jit(solution)/shard_map/ppermute | solution.py:251
  2.3 1.5 %collective-permute-start.2 = (bf16[128,512]{1,0:T(8,128)(2,1)}, bf16[128,512]{1,0:T(8,128)(2,1)S(1)}, u32[]{:S(2)}, u32[]{:S(2)}) collective-permute-start(bf16[128,512]{1,0:T(8,128)(2,1)} %refs_6_.1), channel_id=1, source_target_pairs={{0,2},{1,3},{2,4},{3,5},{4,6},{5,7},{6,8},{7,9},{8,10},{9,11},{10,... | collective-permute-start | bytes 393224 | tf_op jit(solution)/shard_map/ppermute | solution.py:251
  3.8 1.6 %collective-permute-start.1 = (bf16[128,512]{1,0:T(8,128)(2,1)}, bf16[128,512]{1,0:T(8,128)(2,1)S(1)}, u32[]{:S(2)}, u32[]{:S(2)}) collective-permute-start(bf16[128,512]{1,0:T(8,128)(2,1)} %refs_0_.3), channel_id=1, source_target_pairs={{0,4},{1,5},{2,6},{3,7},{4,8},{5,9},{6,10},{7,11},{8,12},{9,13},{1... | collective-permute-start | bytes 393224 | tf_op jit(solution)/shard_map/ppermute | solution.py:251
  5.4 1.5 %collective-permute-start = (bf16[128,512]{1,0:T(8,128)(2,1)}, bf16[128,512]{1,0:T(8,128)(2,1)S(1)}, u32[]{:S(2)}, u32[]{:S(2)}) collective-permute-start(bf16[128,512]{1,0:T(8,128)(2,1)} %refs_0_.3), channel_id=1, source_target_pairs={{0,2},{1,3},{2,4},{3,5},{4,6},{5,7},{6,8},{7,9},{8,10},{9,11},{10,... | collective-permute-start | bytes 393224 | tf_op jit(solution)/shard_map/ppermute | solution.py:251
  6.9 4.5 %delta.1.delta_ref = f32[64,128]{1,0:T(8,128)} custom-call(bf16[128,8192]{1,0:T(8,128)(2,1)} %o_ref.1, bf16[128,8192]{1,0:T(8,128)(2,1)} %do_ref.5), custom_call_target="tpu_custom_call" | custom-call | flops 100000000 | bytes 4194304 | tf_op jit(solution)/shard_map/delta/pallas_call | solution.py:228
  11.4 0.0 collective-permute-done.3.refs_7_
  11.4 0.0 copy-start.7
  11.4 0.6 %collective-permute-start.6 = (bf16[128,512]{1,0:T(8,128)(2,1)S(1)}, bf16[128,512]{1,0:T(8,128)(2,1)S(1)}, u32[]{:S(2)}, u32[]{:S(2)}) collective-permute-start(bf16[128,512]{1,0:T(8,128)(2,1)S(1)} %copy-done.1), channel_id=1, source_target_pairs={{0,1},{1,0},{2,3},{3,2},{4,5},{5,4},{6,7},{7,6},{8,9},{9,8},{10,11... | collective-permute-start | bytes 393224 | tf_op jit(solution)/shard_map/ppermute | solution.py:256
  12.0 2.8 %collective-permute-done.1.refs_1_ = bf16[128,512]{1,0:T(8,128)(2,1)S(1)} collective-permute-done((bf16[128,512]{1,0:T(8,128)(2,1)}, bf16[128,512]{1,0:T(8,128)(2,1)S(1)}, u32[]{:S(2)}, u32[]{:S(2)}) %collective-permute-start.1) | collective-permute-done | bytes 131104 | tf_op jit(solution)/shard_map/ppermute | solution.py:251
  14.7 0.1 collective-permute-start.8
  14.8 0.5 collective-permute-start.7
  15.3 0.1 collective-permute-start.5
  15.4 0.4 collective-permute-start.4
  15.8 0.3 collective-permute-done.8.refs_10_
  16.1 0.2 collective-permute-done.7.refs_9_
  16.3 0.3 collective-permute-done.5.refs_4_
  16.6 0.2 collective-permute-done.4.refs_3_
  16.9 0.1 copy-done.11
  17.0 0.3 copy-done.5
  17.3 0.2 copy-done.6
  17.5 18.4 %main.1 = (bf16[640,8192]{1,0:T(8,128)(2,1)}, bf16[128,8192]{1,0:T(8,128)(2,1)}, f32[4,128,512]{2,1,0:T(8,128)S(1)}, bf16[4,128,512]{2,1,0:T(8,128)(2,1)S(1)}) custom-call(s32[8]{0:T(128)S(1)} %copy-done, s32[1]{0:T(128)} %bitcast.place_ref, bf16[128,8192]{1,0:T(8,128)(2,1)} %q_ref.3, bf16[128,8192]{1,0:T(8,128)(2,1)} %do_ref.5, f32[64,128]{1,0:T(8,128)} %delta.1.delta_ref, ...), custom_call_target="tpu_custom_call" | custom-call | flops 16000000000 | bytes 16777216 | tf_op jit(solution)/shard_map/main/pallas_call | solution.py:144
  35.9 0.4 collective-permute-start.10
  36.3 1.6 %collective-permute-done.10 = bf16[4,128,512]{2,1,0:T(8,128)(2,1)S(1)} collective-permute-done((bf16[4,128,512]{2,1,0:T(8,128)(2,1)S(1)}, bf16[4,128,512]{2,1,0:T(8,128)(2,1)S(1)}, u32[]{:S(2)}, u32[]{:S(2)}) %collective-permute-start.10) | collective-permute-done | bytes 524320 | tf_op jit(solution)/shard_map/ppermute | solution.py:256
  37.9 0.1 convert_element_type.45
  38.0 0.3 fusion.9
  38.3 1.9 %collective-permute-start.11 = (bf16[128,512]{1,0:T(8,128)(2,1)S(1)}, bf16[128,512]{1,0:T(8,128)(2,1)S(1)}, u32[]{:S(2)}, u32[]{:S(2)}) collective-permute-start(bf16[128,512]{1,0:T(8,128)(2,1)S(1)} %get-tuple-element.31), channel_id=1, source_target_pairs={{0,12},{1,13},{2,14},{3,15},{4,0},{5,1},{6,2},{7,3},{8,4},{9,5},{1... | collective-permute-start | bytes 393224 | tf_op jit(solution)/shard_map/ppermute | solution.py:251
  40.2 3.1 %collective-permute-start.12 = (bf16[128,512]{1,0:T(8,128)(2,1)S(1)}, bf16[128,512]{1,0:T(8,128)(2,1)S(1)}, u32[]{:S(2)}, u32[]{:S(2)}) collective-permute-start(bf16[128,512]{1,0:T(8,128)(2,1)S(1)} %get-tuple-element.32), channel_id=1, source_target_pairs={{0,14},{1,15},{2,0},{3,1},{4,2},{5,3},{6,4},{7,5},{8,6},{9,7},{10,... | collective-permute-start | bytes 393224 | tf_op jit(solution)/shard_map/ppermute | solution.py:251
  43.2 0.4 collective-permute-start.13
  43.7 9.0 %late.1 = (bf16[128,8192]{1,0:T(8,128)(2,1)}, f32[2,128,512]{2,1,0:T(8,128)S(1)}) custom-call(s32[1]{0:T(128)} %bitcast.place_ref, bf16[128,8192]{1,0:T(8,128)(2,1)} %q_ref.3, bf16[128,8192]{1,0:T(8,128)(2,1)} %do_ref.5, bf16[640,8192]{1,0:T(8,128)(2,1)} %get-tuple-element.27.d_ref, bf16[128,8192]{1,0:T(8,128)(2,1)} %get-tuple-element.28.p_ref, ...), custom_call_target="tpu_custom_call" | custom-call | flops 8000000000 | bytes 20971520 | tf_op jit(solution)/shard_map/late/pallas_call | solution.py:198
  52.7 2.3 %collective-permute-done.14 = bf16[128,512]{1,0:T(8,128)(2,1)S(1)} collective-permute-done((bf16[128,512]{1,0:T(8,128)(2,1)S(1)}, bf16[128,512]{1,0:T(8,128)(2,1)S(1)}, u32[]{:S(2)}, u32[]{:S(2)}) %collective-permute-start.14) | collective-permute-done | bytes 131104 | tf_op jit(solution)/shard_map/ppermute | solution.py:251
  55.1 0.9 %fusion.3 = (bf16[128,512]{1,0:T(8,128)(2,1)}, bf16[128,512]{1,0:T(8,128)(2,1)}) fusion(bf16[128,512]{1,0:T(8,128)(2,1)S(1)} %collective-permute-done.14, bf16[128,512]{1,0:T(8,128)(2,1)S(1)} %collective-permute-done.13, f32[2,128,512]{2,1,0:T(8,128)S(1)} %get-tuple-element.30, f32[4,128,512]{2,1,0:T(8,128)S(1)} %convert_element_type.45, pred[]{:T(512)S(6)} %eq.5, ...), kind=kLoop, calls=%fused_computation.6 | loop fusion | flops 917504 | bytes 1835009 | tf_op jit(solution)/shard_map/convert_element_type | solution.py:278
  (28 shorter events, 0.1 us)
Async XLA Ops:
  0.6 10.7 %copy-start.1 = (bf16[128,512]{1,0:T(8,128)(2,1)S(1)}, bf16[128,512]{1,0:T(8,128)(2,1)}, u32[]{:S(2)}) copy-start(bf16[128,512]{1,0:T(8,128)(2,1)} %refs_0_.3) | copy-start | bytes 393220
  0.6 16.8 %copy-start = (s32[8]{0:T(128)S(1)}, s32[8]{0:T(128)}, u32[]{:S(2)}) copy-start(s32[8]{0:T(128)} %len_ref.1) | copy-start | bytes 100
  0.7 10.7 %collective-permute-start.3 = (bf16[128,512]{1,0:T(8,128)(2,1)}, bf16[128,512]{1,0:T(8,128)(2,1)S(1)}, u32[]{:S(2)}, u32[]{:S(2)}) collective-permute-start(bf16[128,512]{1,0:T(8,128)(2,1)} %refs_6_.1), channel_id=1, source_target_pairs={{0,4},{1,5},{2,6},{3,7},{4,8},{5,9},{6,10},{7,11},{8,12},{9,13},{1... | collective-permute-start | bytes 393224 | tf_op jit(solution)/shard_map/ppermute | solution.py:251
  2.3 9.7 %collective-permute-start.2 = (bf16[128,512]{1,0:T(8,128)(2,1)}, bf16[128,512]{1,0:T(8,128)(2,1)S(1)}, u32[]{:S(2)}, u32[]{:S(2)}) collective-permute-start(bf16[128,512]{1,0:T(8,128)(2,1)} %refs_6_.1), channel_id=1, source_target_pairs={{0,2},{1,3},{2,4},{3,5},{4,6},{5,7},{6,8},{7,9},{8,10},{9,11},{10,... | collective-permute-start | bytes 393224 | tf_op jit(solution)/shard_map/ppermute | solution.py:251
  3.8 10.9 %collective-permute-start.1 = (bf16[128,512]{1,0:T(8,128)(2,1)}, bf16[128,512]{1,0:T(8,128)(2,1)S(1)}, u32[]{:S(2)}, u32[]{:S(2)}) collective-permute-start(bf16[128,512]{1,0:T(8,128)(2,1)} %refs_0_.3), channel_id=1, source_target_pairs={{0,4},{1,5},{2,6},{3,7},{4,8},{5,9},{6,10},{7,11},{8,12},{9,13},{1... | collective-permute-start | bytes 393224 | tf_op jit(solution)/shard_map/ppermute | solution.py:251
  5.4 9.3 %collective-permute-start = (bf16[128,512]{1,0:T(8,128)(2,1)}, bf16[128,512]{1,0:T(8,128)(2,1)S(1)}, u32[]{:S(2)}, u32[]{:S(2)}) collective-permute-start(bf16[128,512]{1,0:T(8,128)(2,1)} %refs_0_.3), channel_id=1, source_target_pairs={{0,2},{1,3},{2,4},{3,5},{4,6},{5,7},{6,8},{7,9},{8,10},{9,11},{10,... | collective-permute-start | bytes 393224 | tf_op jit(solution)/shard_map/ppermute | solution.py:251
  6.9 8.5 %collective-permute-start.9 = (bf16[128,512]{1,0:T(8,128)(2,1)}, bf16[128,512]{1,0:T(8,128)(2,1)S(1)}, u32[]{:S(2)}, u32[]{:S(2)}) collective-permute-start(bf16[128,512]{1,0:T(8,128)(2,1)} %refs_6_.1), channel_id=1, source_target_pairs={{0,1},{1,0},{2,3},{3,2},{4,5},{5,4},{6,7},{7,6},{8,9},{9,8},{10,11... | collective-permute-start | bytes 393224 | tf_op jit(solution)/shard_map/ppermute | solution.py:256
  11.4 5.5 %copy-start.7 = (bf16[128,512]{1,0:T(8,128)(2,1)}, bf16[128,512]{1,0:T(8,128)(2,1)S(1)}, u32[]{:S(2)}) copy-start(bf16[128,512]{1,0:T(8,128)(2,1)S(1)} %collective-permute-done.3.refs_7_) | copy-start | bytes 393220
  11.4 4.4 %collective-permute-start.6 = (bf16[128,512]{1,0:T(8,128)(2,1)S(1)}, bf16[128,512]{1,0:T(8,128)(2,1)S(1)}, u32[]{:S(2)}, u32[]{:S(2)}) collective-permute-start(bf16[128,512]{1,0:T(8,128)(2,1)S(1)} %copy-done.1), channel_id=1, source_target_pairs={{0,1},{1,0},{2,3},{3,2},{4,5},{5,4},{6,7},{7,6},{8,9},{9,8},{10,11... | collective-permute-start | bytes 393224 | tf_op jit(solution)/shard_map/ppermute | solution.py:256
  11.9 4.9 %copy-start.8 = (bf16[128,512]{1,0:T(8,128)(2,1)}, bf16[128,512]{1,0:T(8,128)(2,1)S(1)}, u32[]{:S(2)}) copy-start(bf16[128,512]{1,0:T(8,128)(2,1)S(1)} %collective-permute-done.2.refs_8_) | copy-start | bytes 393220
  14.7 2.1 %copy-start.2 = (bf16[128,512]{1,0:T(8,128)(2,1)}, bf16[128,512]{1,0:T(8,128)(2,1)S(1)}, u32[]{:S(2)}) copy-start(bf16[128,512]{1,0:T(8,128)(2,1)S(1)} %collective-permute-done.1.refs_1_) | copy-start | bytes 393220
  14.7 2.1 %copy-start.3 = (bf16[128,512]{1,0:T(8,128)(2,1)}, bf16[128,512]{1,0:T(8,128)(2,1)S(1)}, u32[]{:S(2)}) copy-start(bf16[128,512]{1,0:T(8,128)(2,1)S(1)} %collective-permute-done.refs_2_) | copy-start | bytes 393220
  14.7 1.4 %collective-permute-start.8 = (bf16[128,512]{1,0:T(8,128)(2,1)S(1)}, bf16[128,512]{1,0:T(8,128)(2,1)S(1)}, u32[]{:S(2)}, u32[]{:S(2)}) collective-permute-start(bf16[128,512]{1,0:T(8,128)(2,1)S(1)} %collective-permute-done.3.refs_7_), channel_id=1, source_target_pairs={{0,1},{1,0},{2,3},{3,2},{4,5},{5,4},{6,7},{7,6},{8,9},{9,8},{10,11... | collective-permute-start | bytes 393224 | tf_op jit(solution)/shard_map/ppermute | solution.py:256
  14.8 1.5 %collective-permute-start.7 = (bf16[128,512]{1,0:T(8,128)(2,1)S(1)}, bf16[128,512]{1,0:T(8,128)(2,1)S(1)}, u32[]{:S(2)}, u32[]{:S(2)}) collective-permute-start(bf16[128,512]{1,0:T(8,128)(2,1)S(1)} %collective-permute-done.2.refs_8_), channel_id=1, source_target_pairs={{0,1},{1,0},{2,3},{3,2},{4,5},{5,4},{6,7},{7,6},{8,9},{9,8},{10,11... | collective-permute-start | bytes 393224 | tf_op jit(solution)/shard_map/ppermute | solution.py:256
  15.3 1.3 %collective-permute-start.5 = (bf16[128,512]{1,0:T(8,128)(2,1)S(1)}, bf16[128,512]{1,0:T(8,128)(2,1)S(1)}, u32[]{:S(2)}, u32[]{:S(2)}) collective-permute-start(bf16[128,512]{1,0:T(8,128)(2,1)S(1)} %collective-permute-done.1.refs_1_), channel_id=1, source_target_pairs={{0,1},{1,0},{2,3},{3,2},{4,5},{5,4},{6,7},{7,6},{8,9},{9,8},{10,11... | collective-permute-start | bytes 393224 | tf_op jit(solution)/shard_map/ppermute | solution.py:256
  15.4 1.5 %copy-start.9 = (bf16[128,512]{1,0:T(8,128)(2,1)}, bf16[128,512]{1,0:T(8,128)(2,1)S(1)}, u32[]{:S(2)}) copy-start(bf16[128,512]{1,0:T(8,128)(2,1)S(1)} %collective-permute-done.9.refs_11_) | copy-start | bytes 393220
  15.4 1.5 %collective-permute-start.4 = (bf16[128,512]{1,0:T(8,128)(2,1)S(1)}, bf16[128,512]{1,0:T(8,128)(2,1)S(1)}, u32[]{:S(2)}, u32[]{:S(2)}) collective-permute-start(bf16[128,512]{1,0:T(8,128)(2,1)S(1)} %collective-permute-done.refs_2_), channel_id=1, source_target_pairs={{0,1},{1,0},{2,3},{3,2},{4,5},{5,4},{6,7},{7,6},{8,9},{9,8},{10,11... | collective-permute-start | bytes 393224 | tf_op jit(solution)/shard_map/ppermute | solution.py:256
  15.8 1.1 %copy-start.4 = (bf16[128,512]{1,0:T(8,128)(2,1)}, bf16[128,512]{1,0:T(8,128)(2,1)S(1)}, u32[]{:S(2)}) copy-start(bf16[128,512]{1,0:T(8,128)(2,1)S(1)} %collective-permute-done.6.refs_5_) | copy-start | bytes 393220
  16.1 0.7 %copy-start.10 = (bf16[128,512]{1,0:T(8,128)(2,1)}, bf16[128,512]{1,0:T(8,128)(2,1)S(1)}, u32[]{:S(2)}) copy-start(bf16[128,512]{1,0:T(8,128)(2,1)S(1)} %collective-permute-done.8.refs_10_) | copy-start | bytes 393220
  16.3 0.7 %copy-start.11 = (bf16[128,512]{1,0:T(8,128)(2,1)}, bf16[128,512]{1,0:T(8,128)(2,1)S(1)}, u32[]{:S(2)}) copy-start(bf16[128,512]{1,0:T(8,128)(2,1)S(1)} %collective-permute-done.7.refs_9_) | copy-start | bytes 393220
  16.6 0.7 %copy-start.5 = (bf16[128,512]{1,0:T(8,128)(2,1)}, bf16[128,512]{1,0:T(8,128)(2,1)S(1)}, u32[]{:S(2)}) copy-start(bf16[128,512]{1,0:T(8,128)(2,1)S(1)} %collective-permute-done.5.refs_4_) | copy-start | bytes 393220
  16.8 0.7 %copy-start.6 = (bf16[128,512]{1,0:T(8,128)(2,1)}, bf16[128,512]{1,0:T(8,128)(2,1)S(1)}, u32[]{:S(2)}) copy-start(bf16[128,512]{1,0:T(8,128)(2,1)S(1)} %collective-permute-done.4.refs_3_) | copy-start | bytes 393220
  35.9 2.0 %collective-permute-start.10 = (bf16[4,128,512]{2,1,0:T(8,128)(2,1)S(1)}, bf16[4,128,512]{2,1,0:T(8,128)(2,1)S(1)}, u32[]{:S(2)}, u32[]{:S(2)}) collective-permute-start(bf16[4,128,512]{2,1,0:T(8,128)(2,1)S(1)} %get-tuple-element.25), channel_id=1, source_target_pairs={{0,1},{1,0},{2,3},{3,2},{4,5},{5,4},{6,7},{7,6},{8,9},{9,8},{10,11... | collective-permute-start | bytes 1572872 | tf_op jit(solution)/shard_map/ppermute | solution.py:256
  38.3 14.4 %collective-permute-start.11 = (bf16[128,512]{1,0:T(8,128)(2,1)S(1)}, bf16[128,512]{1,0:T(8,128)(2,1)S(1)}, u32[]{:S(2)}, u32[]{:S(2)}) collective-permute-start(bf16[128,512]{1,0:T(8,128)(2,1)S(1)} %get-tuple-element.31), channel_id=1, source_target_pairs={{0,12},{1,13},{2,14},{3,15},{4,0},{5,1},{6,2},{7,3},{8,4},{9,5},{1... | collective-permute-start | bytes 393224 | tf_op jit(solution)/shard_map/ppermute | solution.py:251
  40.2 12.6 %collective-permute-start.12 = (bf16[128,512]{1,0:T(8,128)(2,1)S(1)}, bf16[128,512]{1,0:T(8,128)(2,1)S(1)}, u32[]{:S(2)}, u32[]{:S(2)}) collective-permute-start(bf16[128,512]{1,0:T(8,128)(2,1)S(1)} %get-tuple-element.32), channel_id=1, source_target_pairs={{0,14},{1,15},{2,0},{3,1},{4,2},{5,3},{6,4},{7,5},{8,6},{9,7},{10,... | collective-permute-start | bytes 393224 | tf_op jit(solution)/shard_map/ppermute | solution.py:251
  43.2 9.5 %collective-permute-start.13 = (bf16[128,512]{1,0:T(8,128)(2,1)S(1)}, bf16[128,512]{1,0:T(8,128)(2,1)S(1)}, u32[]{:S(2)}, u32[]{:S(2)}) collective-permute-start(bf16[128,512]{1,0:T(8,128)(2,1)S(1)} %get-tuple-element.33), channel_id=1, source_target_pairs={{0,12},{1,13},{2,14},{3,15},{4,0},{5,1},{6,2},{7,3},{8,4},{9,5},{1... | collective-permute-start | bytes 393224 | tf_op jit(solution)/shard_map/ppermute | solution.py:251
  43.7 11.4 %collective-permute-start.14 = (bf16[128,512]{1,0:T(8,128)(2,1)S(1)}, bf16[128,512]{1,0:T(8,128)(2,1)S(1)}, u32[]{:S(2)}, u32[]{:S(2)}) collective-permute-start(bf16[128,512]{1,0:T(8,128)(2,1)S(1)} %get-tuple-element.34), channel_id=1, source_target_pairs={{0,14},{1,15},{2,0},{3,1},{4,2},{5,3},{6,4},{7,5},{8,6},{9,7},{10,... | collective-permute-start | bytes 393224 | tf_op jit(solution)/shard_map/ppermute | solution.py:251

commit v4 on v3

--- a/solution.py
+++ b/solution.py
@@ -83,11 +83,28 @@
             return jnp.where(tri, x[0:rows, c], x[rows : 2 * rows, c])
         return x[(n + 1) * rows : (n + 2) * rows, c]
 
-    for hs in chunks(STEPS):
+    def products(hs):
         q2 = stacked(q_ref, hs)
         do2 = stacked(do_ref, hs)
-        s = dot(kall[...], q2, NT)
-        dp = dot(vall[...], do2, NT)
+        return q2, do2, dot(kall[...], q2, NT), dot(vall[...], do2, NT)
+
+    def spread(ch, probs, grads, q2, do2):
+        dv = dot(probs, do2, NN)
+        dk = dot(grads, q2, NN)
+        if ch == 0:
+            accv[...] = dv
+            acck[...] = dk
+        else:
+            accv[...] += dv
+            acck[...] += dk
+
+    todo = chunks(STEPS)
+    ahead = products(todo[0])
+    behind = None
+    for ch, hs in enumerate(todo):
+        q2, do2, s, dp = ahead
+        if ch + 1 < len(todo):
+            ahead = products(todo[ch + 1])
         pb = [[None] * CHUNK for _ in range(4)]
         db = [[None] * CHUNK for _ in range(4)]
         for i, h in enumerate(hs):
@@ -110,8 +127,7 @@
         probs = jnp.concatenate([jnp.concatenate(r, axis=1) for r in pb], axis=0)
         grads = jnp.concatenate([jnp.concatenate(r, axis=1) for r in db], axis=0)
         d_ref[rows:, hs[0] * rows : (hs[-1] + 1) * rows] = grads
-        accv[...] += dot(probs, do2, NN)
-        acck[...] += dot(grads, q2, NN)
+        spread(ch, probs, grads, q2, do2)
 
     @pl.when(pl.program_id(1) == STEPS - 1)
     def _():
@@ -260,12 +276,16 @@
     place = lax.axis_index("ctx").astype(jnp.int32)
     even = place % 2 == 0
     index = place.reshape(1)
-    k2, k4 = moved(keys, 2), moved(keys, 4)
-    v2, v4 = moved(values, 2), moved(values, 4)
+    k4 = moved(keys, 4)
+    k2 = moved(keys, 2)
+    v4 = moved(values, 4)
+    v2 = moved(values, 2)
     km, vm = swapped(keys), swapped(values)
     delta = delta_call(outputs, d_out)
-    k2, k4, v2, v4, delta = lax.optimization_barrier((k2, k4, v2, v4, delta))
-    ks = (keys, k4, k2, swapped(k2), swapped(k4), km)
+    k4, k2, delta = lax.optimization_barrier((k4, k2, delta))
+    k2s, k4s = swapped(k2), swapped(k4)
+    v4, v2, k2s, k4s = lax.optimization_barrier((v4, v2, k2s, k4s))
+    ks = (keys, k4, k2, k2s, k4s, km)
     vs = (values, v4, v2, swapped(v2), swapped(v4), vm)
     grads, probs, far, swap = main_call(lengths, index, queries, d_out, delta, ks, vs)
     back = swapped(swap).astype(F32)

time: 56.9 us -> 54.4 us (0.956)
  starting transfers between devices: 13.7 us -> 12.4 us
  Pallas kernels: 31.9 us -> 31.3 us
    ppermute x8, starting transfers between devices: 11.6 us -> 10.4 us  [moved(): return lax.ppermute(x, 'ctx', [(i, (i + by) % size) for i in range(size)])]
    pallas_call x1, Pallas kernels: 18.4 us -> 17.8 us  [main_call(): pl.pallas_call(main_kernel, grid_spec=pltpu.PrefetchScalarGridSpec(num_sc...]
  transfers between devices with their start and end apart: 15 -> 15, of which waited for: 7 -> 6; matrix products, arithmetic and copies ran while one was open for 0% -> 0% of each run, Pallas kernels for 24% -> 25%
where the time goes in v4:
time: 54.4 us; the launch traced here: 53.5 us
  Pallas kernels  31.3 us (58%)
  starting transfers between devices  12.4 us (23%)
  waiting for transfers between devices  7.14 us (13%)
  other arithmetic  1.24 us (2%)
  between operations  0.8 us (1%)
  local copies, waits for them, and re-layouts  0.64 us (1%)
    pallas_call x1, Pallas kernels, main_call(): pl.pallas_call(main_kernel, grid_spec=pltpu.PrefetchScalarGridSpec(num_sc...  17.8 us
    ppermute x8, starting transfers between devices, moved(): return lax.ppermute(x, 'ctx', [(i, (i + by) % size) for i in range(size)])  10.4 us
    pallas_call x1, Pallas kernels, late_call(): pl.pallas_call(late_kernel, grid_spec=pltpu.PrefetchScalarGridSpec(num_sc...  9.04 us
    ppermute x8, waiting for transfers between devices, moved(): return lax.ppermute(x, 'ctx', [(i, (i + by) % size) for i in range(size)])  4.54 us
    pallas_call x1, Pallas kernels, delta_call(): pl.pallas_call(delta_kernel, grid=(HK,), in_specs=[big, big], out_specs=p...  4.45 us
    ppermute x7, waiting for transfers between devices, swapped(): return lax.ppermute(x, 'ctx', [(i, i ^ 1) for i in range(size)])  2.6 us
    ppermute x7, starting transfers between devices, swapped(): return lax.ppermute(x, 'ctx', [(i, i ^ 1) for i in range(size)])  2.02 us
  transfers between devices with their start and end apart: 15, of which 6 were waited for; matrix products, arithmetic and copies ran while one was open for 0% of the time, Pallas kernels for 25%

profile of v4, /device:TPU:6, one launch (start us, length us, event | category | flops | bytes accessed | tf_op | source)
XLA Modules:
  0.0 53.5 jit_solution(12082455015874663685)
XLA Ops:
  0.6 0.0 copy-start.2
  0.6 0.0 copy-start.1
  0.7 1.6 %collective-permute-start.1 = (bf16[128,512]{1,0:T(8,128)(2,1)}, bf16[128,512]{1,0:T(8,128)(2,1)S(1)}, u32[]{:S(2)}, u32[]{:S(2)}) collective-permute-start(bf16[128,512]{1,0:T(8,128)(2,1)} %refs_0_.3), channel_id=1, source_target_pairs={{0,2},{1,3},{2,4},{3,5},{4,6},{5,7},{6,8},{7,9},{8,10},{9,11},{10,... | collective-permute-start | bytes 393224 | tf_op jit(solution)/shard_map/ppermute | solution.py:267
  2.3 1.6 %collective-permute-start = (bf16[128,512]{1,0:T(8,128)(2,1)}, bf16[128,512]{1,0:T(8,128)(2,1)S(1)}, u32[]{:S(2)}, u32[]{:S(2)}) collective-permute-start(bf16[128,512]{1,0:T(8,128)(2,1)} %refs_0_.3), channel_id=1, source_target_pairs={{0,4},{1,5},{2,6},{3,7},{4,8},{5,9},{6,10},{7,11},{8,12},{9,13},{1... | collective-permute-start | bytes 393224 | tf_op jit(solution)/shard_map/ppermute | solution.py:267
  3.8 1.5 %collective-permute-start.3 = (bf16[128,512]{1,0:T(8,128)(2,1)}, bf16[128,512]{1,0:T(8,128)(2,1)S(1)}, u32[]{:S(2)}, u32[]{:S(2)}) collective-permute-start(bf16[128,512]{1,0:T(8,128)(2,1)} %refs_6_.1), channel_id=1, source_target_pairs={{0,2},{1,3},{2,4},{3,5},{4,6},{5,7},{6,8},{7,9},{8,10},{9,11},{10,... | collective-permute-start | bytes 393224 | tf_op jit(solution)/shard_map/ppermute | solution.py:267
  5.3 1.6 %collective-permute-start.2 = (bf16[128,512]{1,0:T(8,128)(2,1)}, bf16[128,512]{1,0:T(8,128)(2,1)S(1)}, u32[]{:S(2)}, u32[]{:S(2)}) collective-permute-start(bf16[128,512]{1,0:T(8,128)(2,1)} %refs_6_.1), channel_id=1, source_target_pairs={{0,4},{1,5},{2,6},{3,7},{4,8},{5,9},{6,10},{7,11},{8,12},{9,13},{1... | collective-permute-start | bytes 393224 | tf_op jit(solution)/shard_map/ppermute | solution.py:267
  6.9 4.5 %delta.1.delta_ref = f32[64,128]{1,0:T(8,128)} custom-call(bf16[128,8192]{1,0:T(8,128)(2,1)} %o_ref.1, bf16[128,8192]{1,0:T(8,128)(2,1)} %do_ref.5), custom_call_target="tpu_custom_call" | custom-call | flops 100000000 | bytes 4194304 | tf_op jit(solution)/shard_map/delta/pallas_call | solution.py:244
  11.4 0.0 collective-permute-done.1.refs_2_
  11.4 0.5 collective-permute-done.refs_1_
  11.9 0.0 collective-permute-start.5
  11.9 0.5 collective-permute-start.4
  12.4 0.0 collective-permute-start.9
  12.4 0.6 %collective-permute-start.6 = (bf16[128,512]{1,0:T(8,128)(2,1)S(1)}, bf16[128,512]{1,0:T(8,128)(2,1)S(1)}, u32[]{:S(2)}, u32[]{:S(2)}) collective-permute-start(bf16[128,512]{1,0:T(8,128)(2,1)S(1)} %copy-done.2), channel_id=1, source_target_pairs={{0,1},{1,0},{2,3},{3,2},{4,5},{5,4},{6,7},{7,6},{8,9},{9,8},{10,11... | collective-permute-start | bytes 393224 | tf_op jit(solution)/shard_map/ppermute | solution.py:272
  13.0 3.5 %collective-permute-done.2.refs_7_ = bf16[128,512]{1,0:T(8,128)(2,1)S(1)} collective-permute-done((bf16[128,512]{1,0:T(8,128)(2,1)}, bf16[128,512]{1,0:T(8,128)(2,1)S(1)}, u32[]{:S(2)}, u32[]{:S(2)}) %collective-permute-start.2) | collective-permute-done | bytes 131104 | tf_op jit(solution)/shard_map/ppermute | solution.py:267
  16.5 0.1 collective-permute-start.8
  16.6 0.5 collective-permute-start.7
  17.1 0.8 %collective-permute-done.8.refs_10_ = bf16[128,512]{1,0:T(8,128)(2,1)S(1)} collective-permute-done((bf16[128,512]{1,0:T(8,128)(2,1)S(1)}, bf16[128,512]{1,0:T(8,128)(2,1)S(1)}, u32[]{:S(2)}, u32[]{:S(2)}) %collective-permute-start.8) | collective-permute-done | bytes 131104 | tf_op jit(solution)/shard_map/ppermute | solution.py:272
  17.9 0.2 collective-permute-done.7.refs_9_
  18.1 0.4 copy-done.11
  18.5 0.2 copy-done.12
  18.7 17.8 %main.1 = (bf16[640,8192]{1,0:T(8,128)(2,1)}, bf16[128,8192]{1,0:T(8,128)(2,1)}, f32[4,128,512]{2,1,0:T(8,128)S(1)}, bf16[4,128,512]{2,1,0:T(8,128)(2,1)S(1)}) custom-call(s32[8]{0:T(128)S(1)} %copy-done, s32[1]{0:T(128)} %bitcast.place_ref, bf16[128,8192]{1,0:T(8,128)(2,1)} %q_ref.3, bf16[128,8192]{1,0:T(8,128)(2,1)} %do_ref.5, f32[64,128]{1,0:T(8,128)} %delta.1.delta_ref, ...), custom_call_target="tpu_custom_call" | custom-call | flops 16000000000 | bytes 16777216 | tf_op jit(solution)/shard_map/main/pallas_call | solution.py:160
  36.6 0.4 collective-permute-start.10
  37.0 1.6 %collective-permute-done.10 = bf16[4,128,512]{2,1,0:T(8,128)(2,1)S(1)} collective-permute-done((bf16[4,128,512]{2,1,0:T(8,128)(2,1)S(1)}, bf16[4,128,512]{2,1,0:T(8,128)(2,1)S(1)}, u32[]{:S(2)}, u32[]{:S(2)}) %collective-permute-start.10) | collective-permute-done | bytes 524320 | tf_op jit(solution)/shard_map/ppermute | solution.py:272
  38.6 0.1 convert_element_type.45
  38.7 0.3 fusion.9
  39.0 1.8 %collective-permute-start.11 = (bf16[128,512]{1,0:T(8,128)(2,1)S(1)}, bf16[128,512]{1,0:T(8,128)(2,1)S(1)}, u32[]{:S(2)}, u32[]{:S(2)}) collective-permute-start(bf16[128,512]{1,0:T(8,128)(2,1)S(1)} %get-tuple-element.35), channel_id=1, source_target_pairs={{0,12},{1,13},{2,14},{3,15},{4,0},{5,1},{6,2},{7,3},{8,4},{9,5},{1... | collective-permute-start | bytes 393224 | tf_op jit(solution)/shard_map/ppermute | solution.py:267
  40.7 0.1 collective-permute-start.12
  40.9 0.4 collective-permute-start.13
  41.3 1.8 %collective-permute-start.14 = (bf16[128,512]{1,0:T(8,128)(2,1)S(1)}, bf16[128,512]{1,0:T(8,128)(2,1)S(1)}, u32[]{:S(2)}, u32[]{:S(2)}) collective-permute-start(bf16[128,512]{1,0:T(8,128)(2,1)S(1)} %get-tuple-element.38), channel_id=1, source_target_pairs={{0,14},{1,15},{2,0},{3,1},{4,2},{5,3},{6,4},{7,5},{8,6},{9,7},{10,... | collective-permute-start | bytes 393224 | tf_op jit(solution)/shard_map/ppermute | solution.py:267
  43.1 9.0 %late.1 = (bf16[128,8192]{1,0:T(8,128)(2,1)}, f32[2,128,512]{2,1,0:T(8,128)S(1)}) custom-call(s32[1]{0:T(128)} %bitcast.place_ref, bf16[128,8192]{1,0:T(8,128)(2,1)} %q_ref.3, bf16[128,8192]{1,0:T(8,128)(2,1)} %do_ref.5, bf16[640,8192]{1,0:T(8,128)(2,1)} %get-tuple-element.31.d_ref, bf16[128,8192]{1,0:T(8,128)(2,1)} %get-tuple-element.32.p_ref, ...), custom_call_target="tpu_custom_call" | custom-call | flops 8000000000 | bytes 20971520 | tf_op jit(solution)/shard_map/late/pallas_call | solution.py:214
  52.1 0.5 %collective-permute-done.14 = bf16[128,512]{1,0:T(8,128)(2,1)S(1)} collective-permute-done((bf16[128,512]{1,0:T(8,128)(2,1)S(1)}, bf16[128,512]{1,0:T(8,128)(2,1)S(1)}, u32[]{:S(2)}, u32[]{:S(2)}) %collective-permute-start.14) | collective-permute-done | bytes 131104 | tf_op jit(solution)/shard_map/ppermute | solution.py:267
  52.7 0.9 %fusion.3 = (bf16[128,512]{1,0:T(8,128)(2,1)}, bf16[128,512]{1,0:T(8,128)(2,1)}) fusion(bf16[128,512]{1,0:T(8,128)(2,1)S(1)} %collective-permute-done.14, bf16[128,512]{1,0:T(8,128)(2,1)S(1)} %collective-permute-done.13, f32[2,128,512]{2,1,0:T(8,128)S(1)} %get-tuple-element.34, f32[4,128,512]{2,1,0:T(8,128)S(1)} %convert_element_type.45, pred[]{:T(512)S(6)} %eq.5, ...), kind=kLoop, calls=%fused_computation.6 | loop fusion | flops 917504 | bytes 1835009 | tf_op jit(solution)/shard_map/convert_element_type | solution.py:298
  (30 shorter events, 0.1 us)
Async XLA Ops:
  0.6 11.8 %copy-start.2 = (bf16[128,512]{1,0:T(8,128)(2,1)S(1)}, bf16[128,512]{1,0:T(8,128)(2,1)}, u32[]{:S(2)}) copy-start(bf16[128,512]{1,0:T(8,128)(2,1)} %refs_0_.3) | copy-start | bytes 393220
  0.6 11.8 %copy-start.1 = (bf16[128,512]{1,0:T(8,128)(2,1)S(1)}, bf16[128,512]{1,0:T(8,128)(2,1)}, u32[]{:S(2)}) copy-start(bf16[128,512]{1,0:T(8,128)(2,1)} %refs_6_.1) | copy-start | bytes 393220
  0.7 18.1 %copy-start = (s32[8]{0:T(128)S(1)}, s32[8]{0:T(128)}, u32[]{:S(2)}) copy-start(s32[8]{0:T(128)} %len_ref.1) | copy-start | bytes 100
  0.7 10.7 %collective-permute-start.1 = (bf16[128,512]{1,0:T(8,128)(2,1)}, bf16[128,512]{1,0:T(8,128)(2,1)S(1)}, u32[]{:S(2)}, u32[]{:S(2)}) collective-permute-start(bf16[128,512]{1,0:T(8,128)(2,1)} %refs_0_.3), channel_id=1, source_target_pairs={{0,2},{1,3},{2,4},{3,5},{4,6},{5,7},{6,8},{7,9},{8,10},{9,11},{10,... | collective-permute-start | bytes 393224 | tf_op jit(solution)/shard_map/ppermute | solution.py:267
  2.3 9.6 %collective-permute-start = (bf16[128,512]{1,0:T(8,128)(2,1)}, bf16[128,512]{1,0:T(8,128)(2,1)S(1)}, u32[]{:S(2)}, u32[]{:S(2)}) collective-permute-start(bf16[128,512]{1,0:T(8,128)(2,1)} %refs_0_.3), channel_id=1, source_target_pairs={{0,4},{1,5},{2,6},{3,7},{4,8},{5,9},{6,10},{7,11},{8,12},{9,13},{1... | collective-permute-start | bytes 393224 | tf_op jit(solution)/shard_map/ppermute | solution.py:267
  3.8 8.6 %collective-permute-start.3 = (bf16[128,512]{1,0:T(8,128)(2,1)}, bf16[128,512]{1,0:T(8,128)(2,1)S(1)}, u32[]{:S(2)}, u32[]{:S(2)}) collective-permute-start(bf16[128,512]{1,0:T(8,128)(2,1)} %refs_6_.1), channel_id=1, source_target_pairs={{0,2},{1,3},{2,4},{3,5},{4,6},{5,7},{6,8},{7,9},{8,10},{9,11},{10,... | collective-permute-start | bytes 393224 | tf_op jit(solution)/shard_map/ppermute | solution.py:267
  5.3 11.1 %collective-permute-start.2 = (bf16[128,512]{1,0:T(8,128)(2,1)}, bf16[128,512]{1,0:T(8,128)(2,1)S(1)}, u32[]{:S(2)}, u32[]{:S(2)}) collective-permute-start(bf16[128,512]{1,0:T(8,128)(2,1)} %refs_6_.1), channel_id=1, source_target_pairs={{0,4},{1,5},{2,6},{3,7},{4,8},{5,9},{6,10},{7,11},{8,12},{9,13},{1... | collective-permute-start | bytes 393224 | tf_op jit(solution)/shard_map/ppermute | solution.py:267
  11.4 6.7 %copy-start.3 = (bf16[128,512]{1,0:T(8,128)(2,1)}, bf16[128,512]{1,0:T(8,128)(2,1)S(1)}, u32[]{:S(2)}) copy-start(bf16[128,512]{1,0:T(8,128)(2,1)S(1)} %collective-permute-done.1.refs_2_) | copy-start | bytes 393220
  11.9 6.2 %copy-start.4 = (bf16[128,512]{1,0:T(8,128)(2,1)}, bf16[128,512]{1,0:T(8,128)(2,1)S(1)}, u32[]{:S(2)}) copy-start(bf16[128,512]{1,0:T(8,128)(2,1)S(1)} %collective-permute-done.refs_1_) | copy-start | bytes 393220
  11.9 4.6 %collective-permute-start.5 = (bf16[128,512]{1,0:T(8,128)(2,1)S(1)}, bf16[128,512]{1,0:T(8,128)(2,1)S(1)}, u32[]{:S(2)}, u32[]{:S(2)}) collective-permute-start(bf16[128,512]{1,0:T(8,128)(2,1)S(1)} %collective-permute-done.refs_1_), channel_id=1, source_target_pairs={{0,1},{1,0},{2,3},{3,2},{4,5},{5,4},{6,7},{7,6},{8,9},{9,8},{10,11... | collective-permute-start | bytes 393224 | tf_op jit(solution)/shard_map/ppermute | solution.py:272
  11.9 4.6 %collective-permute-start.4 = (bf16[128,512]{1,0:T(8,128)(2,1)S(1)}, bf16[128,512]{1,0:T(8,128)(2,1)S(1)}, u32[]{:S(2)}, u32[]{:S(2)}) collective-permute-start(bf16[128,512]{1,0:T(8,128)(2,1)S(1)} %collective-permute-done.1.refs_2_), channel_id=1, source_target_pairs={{0,1},{1,0},{2,3},{3,2},{4,5},{5,4},{6,7},{7,6},{8,9},{9,8},{10,11... | collective-permute-start | bytes 393224 | tf_op jit(solution)/shard_map/ppermute | solution.py:272
  12.4 4.7 %collective-permute-start.9 = (bf16[128,512]{1,0:T(8,128)(2,1)S(1)}, bf16[128,512]{1,0:T(8,128)(2,1)S(1)}, u32[]{:S(2)}, u32[]{:S(2)}) collective-permute-start(bf16[128,512]{1,0:T(8,128)(2,1)S(1)} %copy-done.1), channel_id=1, source_target_pairs={{0,1},{1,0},{2,3},{3,2},{4,5},{5,4},{6,7},{7,6},{8,9},{9,8},{10,11... | collective-permute-start | bytes 393224 | tf_op jit(solution)/shard_map/ppermute | solution.py:272
  12.4 5.7 %copy-start.8 = (bf16[128,512]{1,0:T(8,128)(2,1)}, bf16[128,512]{1,0:T(8,128)(2,1)S(1)}, u32[]{:S(2)}) copy-start(bf16[128,512]{1,0:T(8,128)(2,1)S(1)} %collective-permute-done.3.refs_8_) | copy-start | bytes 393220
  12.4 4.6 %collective-permute-start.6 = (bf16[128,512]{1,0:T(8,128)(2,1)S(1)}, bf16[128,512]{1,0:T(8,128)(2,1)S(1)}, u32[]{:S(2)}, u32[]{:S(2)}) collective-permute-start(bf16[128,512]{1,0:T(8,128)(2,1)S(1)} %copy-done.2), channel_id=1, source_target_pairs={{0,1},{1,0},{2,3},{3,2},{4,5},{5,4},{6,7},{7,6},{8,9},{9,8},{10,11... | collective-permute-start | bytes 393224 | tf_op jit(solution)/shard_map/ppermute | solution.py:272
  16.5 1.6 %copy-start.9 = (bf16[128,512]{1,0:T(8,128)(2,1)}, bf16[128,512]{1,0:T(8,128)(2,1)S(1)}, u32[]{:S(2)}) copy-start(bf16[128,512]{1,0:T(8,128)(2,1)S(1)} %collective-permute-done.2.refs_7_) | copy-start | bytes 393220
  16.5 1.6 %copy-start.5 = (bf16[128,512]{1,0:T(8,128)(2,1)}, bf16[128,512]{1,0:T(8,128)(2,1)S(1)}, u32[]{:S(2)}) copy-start(bf16[128,512]{1,0:T(8,128)(2,1)S(1)} %collective-permute-done.5.refs_4_) | copy-start | bytes 393220
  16.5 1.6 %copy-start.6 = (bf16[128,512]{1,0:T(8,128)(2,1)}, bf16[128,512]{1,0:T(8,128)(2,1)S(1)}, u32[]{:S(2)}) copy-start(bf16[128,512]{1,0:T(8,128)(2,1)S(1)} %collective-permute-done.4.refs_3_) | copy-start | bytes 393220
  16.5 1.4 %collective-permute-start.8 = (bf16[128,512]{1,0:T(8,128)(2,1)S(1)}, bf16[128,512]{1,0:T(8,128)(2,1)S(1)}, u32[]{:S(2)}, u32[]{:S(2)}) collective-permute-start(bf16[128,512]{1,0:T(8,128)(2,1)S(1)} %collective-permute-done.2.refs_7_), channel_id=1, source_target_pairs={{0,1},{1,0},{2,3},{3,2},{4,5},{5,4},{6,7},{7,6},{8,9},{9,8},{10,11... | collective-permute-start | bytes 393224 | tf_op jit(solution)/shard_map/ppermute | solution.py:272
  16.6 1.5 %collective-permute-start.7 = (bf16[128,512]{1,0:T(8,128)(2,1)S(1)}, bf16[128,512]{1,0:T(8,128)(2,1)S(1)}, u32[]{:S(2)}, u32[]{:S(2)}) collective-permute-start(bf16[128,512]{1,0:T(8,128)(2,1)S(1)} %collective-permute-done.3.refs_8_), channel_id=1, source_target_pairs={{0,1},{1,0},{2,3},{3,2},{4,5},{5,4},{6,7},{7,6},{8,9},{9,8},{10,11... | collective-permute-start | bytes 393224 | tf_op jit(solution)/shard_map/ppermute | solution.py:272
  17.1 1.1 %copy-start.10 = (bf16[128,512]{1,0:T(8,128)(2,1)}, bf16[128,512]{1,0:T(8,128)(2,1)S(1)}, u32[]{:S(2)}) copy-start(bf16[128,512]{1,0:T(8,128)(2,1)S(1)} %collective-permute-done.9.refs_11_) | copy-start | bytes 393220
  17.1 1.1 %copy-start.7 = (bf16[128,512]{1,0:T(8,128)(2,1)}, bf16[128,512]{1,0:T(8,128)(2,1)S(1)}, u32[]{:S(2)}) copy-start(bf16[128,512]{1,0:T(8,128)(2,1)S(1)} %collective-permute-done.6.refs_5_) | copy-start | bytes 393220
  17.9 0.6 %copy-start.11 = (bf16[128,512]{1,0:T(8,128)(2,1)}, bf16[128,512]{1,0:T(8,128)(2,1)S(1)}, u32[]{:S(2)}) copy-start(bf16[128,512]{1,0:T(8,128)(2,1)S(1)} %collective-permute-done.8.refs_10_) | copy-start | bytes 393220
  18.1 0.7 %copy-start.12 = (bf16[128,512]{1,0:T(8,128)(2,1)}, bf16[128,512]{1,0:T(8,128)(2,1)S(1)}, u32[]{:S(2)}) copy-start(bf16[128,512]{1,0:T(8,128)(2,1)S(1)} %collective-permute-done.7.refs_9_) | copy-start | bytes 393220
  36.6 2.0 %collective-permute-start.10 = (bf16[4,128,512]{2,1,0:T(8,128)(2,1)S(1)}, bf16[4,128,512]{2,1,0:T(8,128)(2,1)S(1)}, u32[]{:S(2)}, u32[]{:S(2)}) collective-permute-start(bf16[4,128,512]{2,1,0:T(8,128)(2,1)S(1)} %get-tuple-element.29), channel_id=1, source_target_pairs={{0,1},{1,0},{2,3},{3,2},{4,5},{5,4},{6,7},{7,6},{8,9},{9,8},{10,11... | collective-permute-start | bytes 1572872 | tf_op jit(solution)/shard_map/ppermute | solution.py:272
  39.0 13.2 %collective-permute-start.11 = (bf16[128,512]{1,0:T(8,128)(2,1)S(1)}, bf16[128,512]{1,0:T(8,128)(2,1)S(1)}, u32[]{:S(2)}, u32[]{:S(2)}) collective-permute-start(bf16[128,512]{1,0:T(8,128)(2,1)S(1)} %get-tuple-element.35), channel_id=1, source_target_pairs={{0,12},{1,13},{2,14},{3,15},{4,0},{5,1},{6,2},{7,3},{8,4},{9,5},{1... | collective-permute-start | bytes 393224 | tf_op jit(solution)/shard_map/ppermute | solution.py:267
  40.7 11.4 %collective-permute-start.12 = (bf16[128,512]{1,0:T(8,128)(2,1)S(1)}, bf16[128,512]{1,0:T(8,128)(2,1)S(1)}, u32[]{:S(2)}, u32[]{:S(2)}) collective-permute-start(bf16[128,512]{1,0:T(8,128)(2,1)S(1)} %get-tuple-element.36), channel_id=1, source_target_pairs={{0,14},{1,15},{2,0},{3,1},{4,2},{5,3},{6,4},{7,5},{8,6},{9,7},{10,... | collective-permute-start | bytes 393224 | tf_op jit(solution)/shard_map/ppermute | solution.py:267
  40.9 11.3 %collective-permute-start.13 = (bf16[128,512]{1,0:T(8,128)(2,1)S(1)}, bf16[128,512]{1,0:T(8,128)(2,1)S(1)}, u32[]{:S(2)}, u32[]{:S(2)}) collective-permute-start(bf16[128,512]{1,0:T(8,128)(2,1)S(1)} %get-tuple-element.37), channel_id=1, source_target_pairs={{0,12},{1,13},{2,14},{3,15},{4,0},{5,1},{6,2},{7,3},{8,4},{9,5},{1... | collective-permute-start | bytes 393224 | tf_op jit(solution)/shard_map/ppermute | solution.py:267
  41.3 11.4 %collective-permute-start.14 = (bf16[128,512]{1,0:T(8,128)(2,1)S(1)}, bf16[128,512]{1,0:T(8,128)(2,1)S(1)}, u32[]{:S(2)}, u32[]{:S(2)}) collective-permute-start(bf16[128,512]{1,0:T(8,128)(2,1)S(1)} %get-tuple-element.38), channel_id=1, source_target_pairs={{0,14},{1,15},{2,0},{3,1},{4,2},{5,3},{6,4},{7,5},{8,6},{9,7},{10,... | collective-permute-start | bytes 393224 | tf_op jit(solution)/shard_map/ppermute | solution.py:267

commit v5 on v3

v5 whole, which is shorter than its diff:
```python
import functools
import math

import jax
import jax.numpy as jnp
from jax import lax
from jax.experimental import pallas as pl
from jax.experimental.pallas import tpu as pltpu
from jax.sharding import PartitionSpec as P

HQ = 64
HK = 4
HD = 128
SPAN = 4
PER = HQ // HK
FACTOR = 1.0 / math.sqrt(HD)
LOG2E = math.log2(math.e)
F32 = jnp.float32
BF = jnp.bfloat16
NT = (((1,), (1,)), ((), ()))
NN = (((1,), (0,)), ((), ()))
MIB = 2**20


def dot(a, b, dims):
    return lax.dot_general(a, b, dims, preferred_element_type=F32)


def starts_row(len_ref, qpos):
    def step(j, c):
        end, start = c
        end = end + len_ref[j]
        return end, jnp.where(end <= qpos, end, start)

    return lax.fori_loop(0, len_ref.shape[0], step, (jnp.int32(0), jnp.zeros_like(qpos)))[1]


GROUP = 8
CUTS = (0, 4, 8, 12, 15, 16)


def stacked(ref, half, hs):
    rows = ref.shape[0] // 2
    return jnp.concatenate([ref[half * rows : (half + 1) * rows, h * HD : (h + 1) * HD] for h in hs], axis=0)


def chunks():
    return [(half, list(range(i, i + GROUP))) for half in range(2) for i in range(0, PER, GROUP)]


def gathered(refs, core, half):
    blocks = [refs[j][...] for j in range(4)] + [jnp.where(core == 0, refs[4][...], refs[5][...])]
    rows = blocks[0].shape[0] // 2
    own, far = [(x[:rows], x[rows:]) for x in blocks[:2]]
    edge = [own[half], far[half], own[0] if half else far[1]]
    return jnp.concatenate(edge + blocks[2:], axis=0)


def main_kernel(len_ref, place_ref, q_ref, do_ref, delta_out_ref, *refs):
    k_refs, v_refs = refs[0:6], refs[6:12]
    d_out_ref, p_out_ref, far_ref, swap_ref = refs[12:16]
    kall, vall, bias, acck, accv, q_all, do_all, d_all, p_all, delta_ref, in_sems, out_sems, delta_sem = refs[16:]
    rows = q_ref.shape[0]
    part = rows // 2
    wide = GROUP * part

    def fetch(g):
        c = slice(g * PER * HD, PER * HD if g == 0 else HK * PER * HD)
        pairs = ((q_ref, q_all), (do_ref, do_all))
        return [pltpu.make_async_copy(x.at[:, c], y.at[:, c], in_sems.at[i, g]) for i, (x, y) in enumerate(pairs)]

    def store(n):
        c = slice(cuts[n] * wide, cuts[n + 1] * wide)
        pairs = ((d_all, d_out_ref), (p_all, p_out_ref))
        return [pltpu.make_async_copy(x.at[:, c], y.at[:, c], out_sems.at[i, n]) for i, (x, y) in enumerate(pairs)]

    cuts = CUTS

    rest = pltpu.make_async_copy(delta_out_ref, delta_ref, delta_sem)
    rest.start()
    for copy in fetch(0):
        copy.start()
    place = place_ref[0]
    core = place % 2
    dists = (2, 1 + 2 * core, 3 - 2 * core)
    tri = lax.broadcasted_iota(jnp.int32, (part, rows), 0) <= lax.broadcasted_iota(jnp.int32, (part, rows), 1) % part
    heights = [slice(0, part), slice(part, rows)] + [slice(n * rows, (n + 1) * rows) for n in (1, 2, 3)]

    u = lax.broadcasted_iota(jnp.int32, (part, rows), 0)
    whole = lax.broadcasted_iota(jnp.int32, (rows, rows), 0)
    lane = lax.broadcasted_iota(jnp.int32, (1, rows), 1) % part
    for half in range(2):
        start = starts_row(len_ref, place * rows + half * part + lane)
        at = half * part + u
        spots = [jnp.where(tri, place * rows + at, (place - SPAN) * rows + at)]
        spots += [place * rows + u if half else (place - SPAN) * rows + part + u]
        spots += [(place - n) * rows + whole for n in dists]
        for pos, c in zip(spots, heights):
            bias[half, c, :] = jnp.where(pos >= start, 0.0, -jnp.inf).astype(F32)
        kall[half] = gathered(k_refs, core, half)
        vall[half] = gathered(v_refs, core, half)

    def tiles_of(x, c):
        first = jnp.where(tri, x[0:part, c], x[part : 2 * part, c])
        cut = [slice(2 * part + x0, 2 * part + x1) for x0, x1 in ((0, part), (part, 3 * part), (3 * part, 5 * part), (5 * part, 7 * part))]
        return [first] + [x[y, c] for y in cut]

    def products(g, half, hs):
        c = slice(g * HD, (g + 1) * HD)
        hs = [g * PER + h for h in hs]
        q2 = stacked(q_all, half, hs)
        do2 = stacked(do_all, half, hs)
        return q2, do2, dot(kall[half, :, c], q2, NT), dot(vall[half, :, c], do2, NT)

    todo = [(g, *x) for g in range(HK) for x in chunks()]
    for copy in fetch(0):
        copy.wait()
    rest.wait()
    for copy in fetch(1):
        copy.start()
    ahead = products(*todo[0])
    for ch, (g, half, hs) in enumerate(todo):
        q2, do2, s, dp = ahead
        if g == 0 and todo[ch + 1][0] == 1:
            for copy in fetch(1):
                copy.wait()
        if ch + 1 < len(todo):
            ahead = products(*todo[ch + 1])
        pairs = len(hs) // 2
        pb = [[] for _ in range(6)]
        db = [[] for _ in range(6)]
        for i in range(pairs):
            c = slice(i * rows, (i + 1) * rows)
            tiles = [x + bias[half, y, :] for x, y in zip(tiles_of(s, c), heights)]
            top = functools.reduce(jnp.maximum, tiles[2:])
            edge = jnp.maximum(jnp.maximum(tiles[0], tiles[1]), jnp.maximum(top[:part], top[part:]))
            top = jnp.max(edge, axis=0, keepdims=True)
            es = [jnp.exp2((x - top) * (FACTOR * LOG2E)) for x in tiles]
            total = functools.reduce(jnp.add, es[2:])
            total = (es[0] + es[1]) + (total[:part] + total[part:])
            rl = 1.0 / jnp.sum(total, axis=0, keepdims=True)
            row = ch * pairs + i
            dl = delta_ref[row : row + 1, :]
            for n, (e, x) in enumerate(zip(es, tiles_of(dp, c))):
                p = e * rl
                d = (FACTOR * p) * (x - dl)
                if n == 0:
                    pb[0].append(jnp.where(tri, p, 0.0).astype(BF))
                    db[0].append(jnp.where(tri, d, 0.0).astype(BF))
                    p, d = jnp.where(tri, 0.0, p), jnp.where(tri, 0.0, d)
                pb[n + 1].append(p.astype(BF))
                db[n + 1].append(d.astype(BF))
        pb, db = [[jnp.concatenate(r, axis=1) for r in x] for x in (pb, db)]
        at = slice(ch * GROUP * part, (ch + 1) * GROUP * part)
        p_all[0:part, at] = pb[0]
        p_all[part:, at] = pb[2]
        d_all[:, at] = jnp.concatenate(db, axis=0)
        if ch + 1 in cuts:
            for copy in store(cuts.index(ch + 1) - 1):
                copy.start()
        send = [1, 3, 4, 5] if half else [1, 2, 3, 4, 5]
        to = slice(half * part, 4 * rows)
        c = slice(g * HD, (g + 1) * HD)
        dv = dot(jnp.concatenate([pb[n] for n in send], axis=0), do2, NN)
        dk = dot(jnp.concatenate([db[n] for n in send], axis=0), q2, NN)
        if todo[ch - 1][0] == g and ch > 0:
            accv[to, :] += dv
            acck[to, :] += dk
        else:
            accv[...] = dv
            acck[...] = dk
        if ch + 1 == len(todo) or todo[ch + 1][0] > g:
            for w, acc in enumerate((acck, accv)):
                far_ref[w, :, c] = acc[0:rows, :]
                far_ref[2 + w, :, c] = acc[rows : 2 * rows, :]
                swap_ref[2 + w, :, c] = acc[2 * rows : 3 * rows, :].astype(BF)
                swap_ref[w, :, c] = acc[3 * rows : 4 * rows, :].astype(BF)
    for n in range(len(cuts) - 1):
        for copy in store(n):
            copy.wait()


def specs(rows):
    def wide(height):
        return pl.BlockSpec((height, PER * HD), lambda g, *_: (0, g))

    def heads(n):
        return pl.BlockSpec((n, rows, HD), lambda g, *_: (0, 0, g))

    return wide, pl.BlockSpec((rows, HD), lambda g, *_: (0, g)), heads


def in_hbm(*xs):
    return [pltpu.with_memory_space_constraint(x, pltpu.HBM) for x in xs]


def main_call(lengths, index, q, do, delta, ks, vs):
    rows = q.shape[0]
    vmem, hbm = pl.BlockSpec(memory_space=pltpu.VMEM), pl.BlockSpec(memory_space=pltpu.HBM)
    smem = pl.BlockSpec(memory_space=pltpu.SMEM)
    tall = 9 * rows // 2
    return pl.pallas_call(
        main_kernel,
        in_specs=[smem, smem, hbm, hbm, hbm] + [vmem] * 12,
        out_specs=[hbm, hbm, vmem, vmem],
        scratch_shapes=[
            pltpu.VMEM((2, tall, HK * HD), BF),
            pltpu.VMEM((2, tall, HK * HD), BF),
            pltpu.VMEM((2, 4 * rows, rows), F32),
            pltpu.VMEM((4 * rows, HD), F32),
            pltpu.VMEM((4 * rows, HD), F32),
            pltpu.VMEM((rows, HQ * HD), BF),
            pltpu.VMEM((rows, HQ * HD), BF),
            pltpu.VMEM((tall, HQ * HD), BF),
            pltpu.VMEM((rows, HQ * HD), BF),
            pltpu.VMEM((HQ, rows), F32),
            pltpu.SemaphoreType.DMA((2, 2)),
            pltpu.SemaphoreType.DMA((2, len(CUTS) - 1)),
            pltpu.SemaphoreType.DMA,
        ],
        out_shape=[
            pltpu.HBM((tall, HQ * HD), BF),
            pltpu.HBM((rows, HQ * HD), BF),
            jax.ShapeDtypeStruct((4, rows, HK * HD), F32),
            jax.ShapeDtypeStruct((4, rows, HK * HD), BF),
        ],
        compiler_params=pltpu.CompilerParams(vmem_limit_bytes=40 * MIB),
        cost_estimate=pl.CostEstimate(flops=16 * 10**9, bytes_accessed=16 * MIB, transcendentals=4 * 10**6),
        name="main",
    )(lengths, index, *in_hbm(q, do, delta), *ks, *vs)


def late_kernel(place_ref, q_ref, do_ref, d_ref, p_ref, *refs):
    k_refs = refs[0:6]
    dq_ref, own_ref, kt = refs[6:]
    rows = q_ref.shape[0]
    part = rows // 2
    core = place_ref[0] % 2
    for half in range(2):
        kt[half] = gathered(k_refs, core, half).astype(F32).T.astype(BF)
    own_ref[...] = jnp.zeros_like(own_ref)
    for ch, (half, hs) in enumerate(chunks()):
        at = slice(ch * GROUP * part, (ch + 1) * GROUP * part)
        dqt = dot(kt[half], d_ref[:, at], NN)
        for i in range(GROUP // 2):
            pair = dqt[:, i * rows : (i + 1) * rows].T.astype(BF)
            for j in range(2):
                h = hs[2 * i + j]
                dq_ref[half * part : (half + 1) * part, h * HD : (h + 1) * HD] = pair[j * part : (j + 1) * part, :]
        grads, probs = d_ref[0:part, at], p_ref[0:part, at]
        if half:
            grads = jnp.concatenate([d_ref[rows : rows + part, at], grads], axis=0)
            probs = jnp.concatenate([p_ref[part:, at], probs], axis=0)
        to = slice(0, part + half * part)
        own_ref[0, to, :] += dot(grads, stacked(q_ref, half, hs), NN)
        own_ref[1, to, :] += dot(probs, stacked(do_ref, half, hs), NN)


def late_call(index, q, do, grads, probs, ks):
    rows = q.shape[0]
    wide, head, heads = specs(rows)
    return pl.pallas_call(
        late_kernel,
        grid_spec=pltpu.PrefetchScalarGridSpec(
            num_scalar_prefetch=1,
            grid=(HK,),
            in_specs=[wide(rows), wide(rows), wide(9 * rows // 2), wide(rows)] + [head] * 6,
            out_specs=[wide(rows), heads(2)],
            scratch_shapes=[pltpu.VMEM((2, HD, 9 * rows // 2), BF)],
        ),
        out_shape=[jax.ShapeDtypeStruct((rows, HQ * HD), BF), jax.ShapeDtypeStruct((2, rows, HK * HD), F32)],
        compiler_params=pltpu.CompilerParams(vmem_limit_bytes=40 * MIB),
        cost_estimate=pl.CostEstimate(flops=8 * 10**9, bytes_accessed=20 * MIB, transcendentals=0),
        name="late",
    )(index, *in_hbm(q, do, grads, probs), *ks)


def delta_kernel(o_ref, do_ref, out_ref):
    ones = jnp.ones((8, 2 * HD), BF)
    for ch, (half, hs) in enumerate(chunks()):
        for i in range(GROUP // 2):
            pair = hs[2 * i : 2 * i + 2]
            x = stacked(o_ref, half, pair).astype(F32) * stacked(do_ref, half, pair).astype(F32)
            high = x.astype(BF)
            low = (x - high.astype(F32)).astype(BF)
            row = ch * (GROUP // 2) + i
            out_ref[row : row + 1, :] = dot(ones, jnp.concatenate([high, low], axis=1), NT)[0:1, :]


def delta_call(o, do):
    rows = o.shape[0]
    big = pl.BlockSpec((rows, PER * HD), lambda g: (0, g))
    return pl.pallas_call(
        delta_kernel,
        grid=(HK,),
        in_specs=[big, big],
        out_specs=pl.BlockSpec((PER, rows), lambda g: (g, 0)),
        out_shape=jax.ShapeDtypeStruct((HQ, rows), F32),
        cost_estimate=pl.CostEstimate(flops=10**8, bytes_accessed=4 * MIB, transcendentals=0),
        name="delta",
    )(o, do)


def moved(x, by):
    size = lax.axis_size("ctx")
    return lax.ppermute(x, "ctx", [(i, (i + by) % size) for i in range(size)])


def swapped(x):
    size = lax.axis_size("ctx")
    return lax.ppermute(x, "ctx", [(i, i ^ 1) for i in range(size)])


def moved(x, by):
    size = lax.axis_size("ctx")
    return lax.ppermute(x, "ctx", [(i, (i + by) % size) for i in range(size)])


def swapped(x):
    size = lax.axis_size("ctx")
    return lax.ppermute(x, "ctx", [(i, i ^ 1) for i in range(size)])


def on_device(queries, keys, values, outputs, d_out, lengths):
    place = lax.axis_index("ctx").astype(jnp.int32)
    even = place % 2 == 0
    index = place.reshape(1)
    k4 = moved(keys, 4)
    k2 = moved(keys, 2)
    v4 = moved(values, 4)
    v2 = moved(values, 2)
    km, vm = swapped(keys), swapped(values)
    delta = delta_call(outputs, d_out)
    k4, k2, delta = lax.optimization_barrier((k4, k2, delta))
    k2s, k4s = swapped(k2), swapped(k4)
    v4, v2, k2s, k4s = lax.optimization_barrier((v4, v2, k2s, k4s))
    ks = (keys, k4, k2, k2s, k4s, km)
    vs = (values, v4, v2, swapped(v2), swapped(v4), vm)
    grads, probs, far, swap = main_call(lengths, index, queries, d_out, delta, ks, vs)
    back = swapped(swap).astype(F32)
    near, mid = back[0:2], back[2:4]
    far4 = [(far[w] + jnp.where(even, 0.0, near[w])).astype(BF) for w in range(2)]
    far2 = [(far[2 + w] + mid[w]).astype(BF) for w in range(2)]
    index, *both = lax.optimization_barrier((index, *far4, *far2))
    got = [moved(x, -4 if i < 2 else -2).astype(F32) for i, x in enumerate(both)]
    d_queries, own = late_call(index, queries, d_out, grads, probs, ks)
    total = [(own[w] + jnp.where(even, near[w], 0.0) + got[w] + got[2 + w]).astype(BF) for w in range(2)]
    return d_queries, total[0], total[1]


def solution(mesh):
    spec = P(("group", "ctx"), None)
    return jax.shard_map(
        on_device,
        mesh=mesh,
        in_specs=(spec,) * 5 + (P("group"),),
        out_specs=(spec,) * 3,
        check_vma=False,
    )
```

time: 56.9 us -> 52.2 us (0.917)
  Pallas kernels: 31.9 us -> 29.3 us
  starting transfers between devices: 13.7 us -> 12.3 us
  local copies, waits for them, and re-layouts: 0.65 us -> 0.01 us
    pallas_call x1, Pallas kernels: 18.4 us -> 16.3 us  [main_call(): pl.pallas_call(main_kernel, in_specs=[smem, smem, hbm, hbm, hbm] + [vmem]...]
    ppermute x8, starting transfers between devices: 11.6 us -> 10.4 us  [moved(): return lax.ppermute(x, 'ctx', [(i, (i + by) % size) for i in range(size)])]
    unnamed x24 -> x6, local copies, waits for them, and re-layouts: 0.65 us -> 0.01 us
  transfers between devices with their start and end apart: 15 -> 15, of which waited for: 7 -> 6; matrix products, arithmetic and copies ran while one was open for 0% -> 0% of each run, Pallas kernels for 24% -> 25%
where the time goes in v5:
time: 52.2 us; the launch traced here: 51.3 us
  Pallas kernels  29.3 us (56%)
  starting transfers between devices  12.3 us (24%)
  waiting for transfers between devices  7.76 us (15%)
  other arithmetic  1.24 us (2%)
  between operations  0.72 us (1%)
    pallas_call x1, Pallas kernels, main_call(): pl.pallas_call(main_kernel, in_specs=[smem, smem, hbm, hbm, hbm] + [vmem]...  16.3 us
    ppermute x8, starting transfers between devices, moved(): return lax.ppermute(x, 'ctx', [(i, (i + by) % size) for i in range(size)])  10.4 us
    pallas_call x1, Pallas kernels, late_call(): pl.pallas_call(late_kernel, grid_spec=pltpu.PrefetchScalarGridSpec(num_sc...  8.5 us
    ppermute x8, waiting for transfers between devices, moved(): return lax.ppermute(x, 'ctx', [(i, (i + by) % size) for i in range(size)])  5.15 us
    pallas_call x1, Pallas kernels, delta_call(): pl.pallas_call(delta_kernel, grid=(HK,), in_specs=[big, big], out_specs=p...  4.46 us
    ppermute x7, waiting for transfers between devices, swapped(): return lax.ppermute(x, 'ctx', [(i, i ^ 1) for i in range(size)])  2.61 us
    ppermute x7, starting transfers between devices, swapped(): return lax.ppermute(x, 'ctx', [(i, i ^ 1) for i in range(size)])  1.91 us
  transfers between devices with their start and end apart: 15, of which 6 were waited for; matrix products, arithmetic and copies ran while one was open for 0% of the time, Pallas kernels for 25%

profile of v5, /device:TPU:6, one launch (start us, length us, event | category | flops | bytes accessed | tf_op | source)
XLA Modules:
  0.0 51.3 jit_solution(2576094490441323428)
XLA Ops:
  0.7 1.6 %collective-permute-start.1 = (bf16[128,512]{1,0:T(8,128)(2,1)}, bf16[128,512]{1,0:T(8,128)(2,1)S(1)}, u32[]{:S(2)}, u32[]{:S(2)}) collective-permute-start(bf16[128,512]{1,0:T(8,128)(2,1)} %refs_0_.3), channel_id=1, source_target_pairs={{0,2},{1,3},{2,4},{3,5},{4,6},{5,7},{6,8},{7,9},{8,10},{9,11},{10,... | collective-permute-start | bytes 393224 | tf_op jit(solution)/shard_map/ppermute | solution.py:316
  2.3 1.6 %collective-permute-start = (bf16[128,512]{1,0:T(8,128)(2,1)}, bf16[128,512]{1,0:T(8,128)(2,1)S(1)}, u32[]{:S(2)}, u32[]{:S(2)}) collective-permute-start(bf16[128,512]{1,0:T(8,128)(2,1)} %refs_0_.3), channel_id=1, source_target_pairs={{0,4},{1,5},{2,6},{3,7},{4,8},{5,9},{6,10},{7,11},{8,12},{9,13},{1... | collective-permute-start | bytes 393224 | tf_op jit(solution)/shard_map/ppermute | solution.py:316
  3.8 1.5 %collective-permute-start.3 = (bf16[128,512]{1,0:T(8,128)(2,1)}, bf16[128,512]{1,0:T(8,128)(2,1)S(1)}, u32[]{:S(2)}, u32[]{:S(2)}) collective-permute-start(bf16[128,512]{1,0:T(8,128)(2,1)} %refs_6_.1), channel_id=1, source_target_pairs={{0,2},{1,3},{2,4},{3,5},{4,6},{5,7},{6,8},{7,9},{8,10},{9,11},{10,... | collective-permute-start | bytes 393224 | tf_op jit(solution)/shard_map/ppermute | solution.py:316
  5.3 1.6 %collective-permute-start.2 = (bf16[128,512]{1,0:T(8,128)(2,1)}, bf16[128,512]{1,0:T(8,128)(2,1)S(1)}, u32[]{:S(2)}, u32[]{:S(2)}) collective-permute-start(bf16[128,512]{1,0:T(8,128)(2,1)} %refs_6_.1), channel_id=1, source_target_pairs={{0,4},{1,5},{2,6},{3,7},{4,8},{5,9},{6,10},{7,11},{8,12},{9,13},{1... | collective-permute-start | bytes 393224 | tf_op jit(solution)/shard_map/ppermute | solution.py:316
  6.9 4.5 %delta.1.delta_out_ref = f32[64,128]{1,0:T(8,128)} custom-call(bf16[128,8192]{1,0:T(8,128)(2,1)} %o_ref.1, bf16[128,8192]{1,0:T(8,128)(2,1)} %do_ref.5), custom_call_target="tpu_custom_call" | custom-call | flops 100000000 | bytes 4194304 | tf_op jit(solution)/shard_map/delta/pallas_call | solution.py:293
  11.4 0.0 collective-permute-done.1.refs_2_
  11.4 0.5 collective-permute-done.refs_1_
  11.9 0.0 collective-permute-start.5
  11.9 0.5 collective-permute-start.4
  12.4 0.0 collective-permute-start.9
  12.4 0.0 collective-permute-done.3.refs_8_
  12.4 0.5 collective-permute-start.6
  12.9 3.5 %collective-permute-done.2.refs_7_ = bf16[128,512]{1,0:T(8,128)(2,1)S(1)} collective-permute-done((bf16[128,512]{1,0:T(8,128)(2,1)}, bf16[128,512]{1,0:T(8,128)(2,1)S(1)}, u32[]{:S(2)}, u32[]{:S(2)}) %collective-permute-start.2) | collective-permute-done | bytes 131104 | tf_op jit(solution)/shard_map/ppermute | solution.py:316
  16.4 0.0 collective-permute-done.5.refs_4_
  16.5 0.0 collective-permute-done.4.refs_3_
  16.5 0.5 collective-permute-start.7
  17.0 0.8 %collective-permute-done.8.refs_10_ = bf16[128,512]{1,0:T(8,128)(2,1)S(1)} collective-permute-done((bf16[128,512]{1,0:T(8,128)(2,1)S(1)}, bf16[128,512]{1,0:T(8,128)(2,1)S(1)}, u32[]{:S(2)}, u32[]{:S(2)}) %collective-permute-start.8) | collective-permute-done | bytes 131104 | tf_op jit(solution)/shard_map/ppermute | solution.py:321
  17.8 0.2 collective-permute-done.7.refs_9_
  18.0 16.3 %main.1 = (bf16[576,8192]{1,0:T(8,128)(2,1)}, bf16[128,8192]{1,0:T(8,128)(2,1)}, f32[4,128,512]{2,1,0:T(8,128)S(1)}, bf16[4,128,512]{2,1,0:T(8,128)(2,1)S(1)}) custom-call(s32[8]{0:T(128)S(1)} %copy-done.2, s32[1]{0:T(128)} %bitcast.place_ref, bf16[128,8192]{1,0:T(8,128)(2,1)} %q_ref.3, bf16[128,8192]{1,0:T(8,128)(2,1)} %do_ref.5, ...), custom_call_target="tpu_custom_call" | custom-call | flops 16000000000 | bytes 16777216 | tf_op jit(solution)/shard_map/main/pallas_call | solution.py:202
  34.3 0.4 collective-permute-start.10
  34.7 1.6 %collective-permute-done.10 = bf16[4,128,512]{2,1,0:T(8,128)(2,1)S(1)} collective-permute-done((bf16[4,128,512]{2,1,0:T(8,128)(2,1)S(1)}, bf16[4,128,512]{2,1,0:T(8,128)(2,1)S(1)}, u32[]{:S(2)}, u32[]{:S(2)}) %collective-permute-start.10) | collective-permute-done | bytes 524320 | tf_op jit(solution)/shard_map/ppermute | solution.py:321
  36.3 0.1 convert_element_type.45
  36.4 0.3 fusion.9
  36.7 1.8 %collective-permute-start.11 = (bf16[128,512]{1,0:T(8,128)(2,1)S(1)}, bf16[128,512]{1,0:T(8,128)(2,1)S(1)}, u32[]{:S(2)}, u32[]{:S(2)}) collective-permute-start(bf16[128,512]{1,0:T(8,128)(2,1)S(1)} %get-tuple-element.35), channel_id=1, source_target_pairs={{0,12},{1,13},{2,14},{3,15},{4,0},{5,1},{6,2},{7,3},{8,4},{9,5},{1... | collective-permute-start | bytes 393224 | tf_op jit(solution)/shard_map/ppermute | solution.py:316
  38.4 0.2 collective-permute-start.12
  38.6 0.4 collective-permute-start.13
  39.1 1.7 %collective-permute-start.14 = (bf16[128,512]{1,0:T(8,128)(2,1)S(1)}, bf16[128,512]{1,0:T(8,128)(2,1)S(1)}, u32[]{:S(2)}, u32[]{:S(2)}) collective-permute-start(bf16[128,512]{1,0:T(8,128)(2,1)S(1)} %get-tuple-element.38), channel_id=1, source_target_pairs={{0,14},{1,15},{2,0},{3,1},{4,2},{5,3},{6,4},{7,5},{8,6},{9,7},{10,... | collective-permute-start | bytes 393224 | tf_op jit(solution)/shard_map/ppermute | solution.py:316
  40.8 8.5 %late.1 = (bf16[128,8192]{1,0:T(8,128)(2,1)}, f32[2,128,512]{2,1,0:T(8,128)S(1)}) custom-call(s32[1]{0:T(128)} %bitcast.place_ref, bf16[128,8192]{1,0:T(8,128)(2,1)} %q_ref.3, bf16[128,8192]{1,0:T(8,128)(2,1)} %do_ref.5, bf16[576,8192]{1,0:T(8,128)(2,1)} %get-tuple-element.31.d_ref, bf16[128,8192]{1,0:T(8,128)(2,1)} %get-tuple-element.32.p_ref, ...), custom_call_target="tpu_custom_call" | custom-call | flops 8000000000 | bytes 20971520 | tf_op jit(solution)/shard_map/late/pallas_call | solution.py:262
  49.3 0.0 collective-permute-done.11
  49.3 0.0 collective-permute-done.12
  49.3 1.1 %collective-permute-done.14 = bf16[128,512]{1,0:T(8,128)(2,1)S(1)} collective-permute-done((bf16[128,512]{1,0:T(8,128)(2,1)S(1)}, bf16[128,512]{1,0:T(8,128)(2,1)S(1)}, u32[]{:S(2)}, u32[]{:S(2)}) %collective-permute-start.14) | collective-permute-done | bytes 131104 | tf_op jit(solution)/shard_map/ppermute | solution.py:316
  50.4 0.9 %fusion.3 = (bf16[128,512]{1,0:T(8,128)(2,1)}, bf16[128,512]{1,0:T(8,128)(2,1)}) fusion(bf16[128,512]{1,0:T(8,128)(2,1)S(1)} %collective-permute-done.14, bf16[128,512]{1,0:T(8,128)(2,1)S(1)} %collective-permute-done.13, f32[2,128,512]{2,1,0:T(8,128)S(1)} %get-tuple-element.34, f32[4,128,512]{2,1,0:T(8,128)S(1)} %convert_element_type.45, pred[]{:T(512)S(6)} %eq.5, ...), kind=kLoop, calls=%fused_computation.6 | loop fusion | flops 917504 | bytes 1835009 | tf_op jit(solution)/shard_map/convert_element_type | solution.py:347
  (10 shorter events, 0.0 us)
Async XLA Ops:
  0.6 11.8 %copy-start.1 = (bf16[128,512]{1,0:T(8,128)(2,1)S(1)}, bf16[128,512]{1,0:T(8,128)(2,1)}, u32[]{:S(2)}) copy-start(bf16[128,512]{1,0:T(8,128)(2,1)} %refs_0_.3) | copy-start | bytes 393220
  0.6 11.8 %copy-start = (bf16[128,512]{1,0:T(8,128)(2,1)S(1)}, bf16[128,512]{1,0:T(8,128)(2,1)}, u32[]{:S(2)}) copy-start(bf16[128,512]{1,0:T(8,128)(2,1)} %refs_6_.1) | copy-start | bytes 393220
  0.7 17.3 %copy-start.2 = (s32[8]{0:T(128)S(1)}, s32[8]{0:T(128)}, u32[]{:S(2)}) copy-start(s32[8]{0:T(128)} %len_ref.1) | copy-start | bytes 100
  0.7 10.7 %collective-permute-start.1 = (bf16[128,512]{1,0:T(8,128)(2,1)}, bf16[128,512]{1,0:T(8,128)(2,1)S(1)}, u32[]{:S(2)}, u32[]{:S(2)}) collective-permute-start(bf16[128,512]{1,0:T(8,128)(2,1)} %refs_0_.3), channel_id=1, source_target_pairs={{0,2},{1,3},{2,4},{3,5},{4,6},{5,7},{6,8},{7,9},{8,10},{9,11},{10,... | collective-permute-start | bytes 393224 | tf_op jit(solution)/shard_map/ppermute | solution.py:316
  2.3 9.6 %collective-permute-start = (bf16[128,512]{1,0:T(8,128)(2,1)}, bf16[128,512]{1,0:T(8,128)(2,1)S(1)}, u32[]{:S(2)}, u32[]{:S(2)}) collective-permute-start(bf16[128,512]{1,0:T(8,128)(2,1)} %refs_0_.3), channel_id=1, source_target_pairs={{0,4},{1,5},{2,6},{3,7},{4,8},{5,9},{6,10},{7,11},{8,12},{9,13},{1... | collective-permute-start | bytes 393224 | tf_op jit(solution)/shard_map/ppermute | solution.py:316
  3.8 8.6 %collective-permute-start.3 = (bf16[128,512]{1,0:T(8,128)(2,1)}, bf16[128,512]{1,0:T(8,128)(2,1)S(1)}, u32[]{:S(2)}, u32[]{:S(2)}) collective-permute-start(bf16[128,512]{1,0:T(8,128)(2,1)} %refs_6_.1), channel_id=1, source_target_pairs={{0,2},{1,3},{2,4},{3,5},{4,6},{5,7},{6,8},{7,9},{8,10},{9,11},{10,... | collective-permute-start | bytes 393224 | tf_op jit(solution)/shard_map/ppermute | solution.py:316
  5.3 11.1 %collective-permute-start.2 = (bf16[128,512]{1,0:T(8,128)(2,1)}, bf16[128,512]{1,0:T(8,128)(2,1)S(1)}, u32[]{:S(2)}, u32[]{:S(2)}) collective-permute-start(bf16[128,512]{1,0:T(8,128)(2,1)} %refs_6_.1), channel_id=1, source_target_pairs={{0,4},{1,5},{2,6},{3,7},{4,8},{5,9},{6,10},{7,11},{8,12},{9,13},{1... | collective-permute-start | bytes 393224 | tf_op jit(solution)/shard_map/ppermute | solution.py:316
  11.9 4.6 %collective-permute-start.5 = (bf16[128,512]{1,0:T(8,128)(2,1)S(1)}, bf16[128,512]{1,0:T(8,128)(2,1)S(1)}, u32[]{:S(2)}, u32[]{:S(2)}) collective-permute-start(bf16[128,512]{1,0:T(8,128)(2,1)S(1)} %collective-permute-done.refs_1_), channel_id=1, source_target_pairs={{0,1},{1,0},{2,3},{3,2},{4,5},{5,4},{6,7},{7,6},{8,9},{9,8},{10,11... | collective-permute-start | bytes 393224 | tf_op jit(solution)/shard_map/ppermute | solution.py:321
  11.9 4.6 %collective-permute-start.4 = (bf16[128,512]{1,0:T(8,128)(2,1)S(1)}, bf16[128,512]{1,0:T(8,128)(2,1)S(1)}, u32[]{:S(2)}, u32[]{:S(2)}) collective-permute-start(bf16[128,512]{1,0:T(8,128)(2,1)S(1)} %collective-permute-done.1.refs_2_), channel_id=1, source_target_pairs={{0,1},{1,0},{2,3},{3,2},{4,5},{5,4},{6,7},{7,6},{8,9},{9,8},{10,11... | collective-permute-start | bytes 393224 | tf_op jit(solution)/shard_map/ppermute | solution.py:321
  12.4 4.6 %collective-permute-start.9 = (bf16[128,512]{1,0:T(8,128)(2,1)S(1)}, bf16[128,512]{1,0:T(8,128)(2,1)S(1)}, u32[]{:S(2)}, u32[]{:S(2)}) collective-permute-start(bf16[128,512]{1,0:T(8,128)(2,1)S(1)} %copy-done), channel_id=1, source_target_pairs={{0,1},{1,0},{2,3},{3,2},{4,5},{5,4},{6,7},{7,6},{8,9},{9,8},{10,11... | collective-permute-start | bytes 393224 | tf_op jit(solution)/shard_map/ppermute | solution.py:321
  12.4 4.6 %collective-permute-start.6 = (bf16[128,512]{1,0:T(8,128)(2,1)S(1)}, bf16[128,512]{1,0:T(8,128)(2,1)S(1)}, u32[]{:S(2)}, u32[]{:S(2)}) collective-permute-start(bf16[128,512]{1,0:T(8,128)(2,1)S(1)} %copy-done.1), channel_id=1, source_target_pairs={{0,1},{1,0},{2,3},{3,2},{4,5},{5,4},{6,7},{7,6},{8,9},{9,8},{10,11... | collective-permute-start | bytes 393224 | tf_op jit(solution)/shard_map/ppermute | solution.py:321
  16.5 1.4 %collective-permute-start.8 = (bf16[128,512]{1,0:T(8,128)(2,1)S(1)}, bf16[128,512]{1,0:T(8,128)(2,1)S(1)}, u32[]{:S(2)}, u32[]{:S(2)}) collective-permute-start(bf16[128,512]{1,0:T(8,128)(2,1)S(1)} %collective-permute-done.2.refs_7_), channel_id=1, source_target_pairs={{0,1},{1,0},{2,3},{3,2},{4,5},{5,4},{6,7},{7,6},{8,9},{9,8},{10,11... | collective-permute-start | bytes 393224 | tf_op jit(solution)/shard_map/ppermute | solution.py:321
  16.5 1.5 %collective-permute-start.7 = (bf16[128,512]{1,0:T(8,128)(2,1)S(1)}, bf16[128,512]{1,0:T(8,128)(2,1)S(1)}, u32[]{:S(2)}, u32[]{:S(2)}) collective-permute-start(bf16[128,512]{1,0:T(8,128)(2,1)S(1)} %collective-permute-done.3.refs_8_), channel_id=1, source_target_pairs={{0,1},{1,0},{2,3},{3,2},{4,5},{5,4},{6,7},{7,6},{8,9},{9,8},{10,11... | collective-permute-start | bytes 393224 | tf_op jit(solution)/shard_map/ppermute | solution.py:321
  34.3 2.0 %collective-permute-start.10 = (bf16[4,128,512]{2,1,0:T(8,128)(2,1)S(1)}, bf16[4,128,512]{2,1,0:T(8,128)(2,1)S(1)}, u32[]{:S(2)}, u32[]{:S(2)}) collective-permute-start(bf16[4,128,512]{2,1,0:T(8,128)(2,1)S(1)} %get-tuple-element.29), channel_id=1, source_target_pairs={{0,1},{1,0},{2,3},{3,2},{4,5},{5,4},{6,7},{7,6},{8,9},{9,8},{10,11... | collective-permute-start | bytes 1572872 | tf_op jit(solution)/shard_map/ppermute | solution.py:321
  36.7 12.6 %collective-permute-start.11 = (bf16[128,512]{1,0:T(8,128)(2,1)S(1)}, bf16[128,512]{1,0:T(8,128)(2,1)S(1)}, u32[]{:S(2)}, u32[]{:S(2)}) collective-permute-start(bf16[128,512]{1,0:T(8,128)(2,1)S(1)} %get-tuple-element.35), channel_id=1, source_target_pairs={{0,12},{1,13},{2,14},{3,15},{4,0},{5,1},{6,2},{7,3},{8,4},{9,5},{1... | collective-permute-start | bytes 393224 | tf_op jit(solution)/shard_map/ppermute | solution.py:316
  38.4 10.9 %collective-permute-start.12 = (bf16[128,512]{1,0:T(8,128)(2,1)S(1)}, bf16[128,512]{1,0:T(8,128)(2,1)S(1)}, u32[]{:S(2)}, u32[]{:S(2)}) collective-permute-start(bf16[128,512]{1,0:T(8,128)(2,1)S(1)} %get-tuple-element.36), channel_id=1, source_target_pairs={{0,14},{1,15},{2,0},{3,1},{4,2},{5,3},{6,4},{7,5},{8,6},{9,7},{10,... | collective-permute-start | bytes 393224 | tf_op jit(solution)/shard_map/ppermute | solution.py:316
  38.6 10.7 %collective-permute-start.13 = (bf16[128,512]{1,0:T(8,128)(2,1)S(1)}, bf16[128,512]{1,0:T(8,128)(2,1)S(1)}, u32[]{:S(2)}, u32[]{:S(2)}) collective-permute-start(bf16[128,512]{1,0:T(8,128)(2,1)S(1)} %get-tuple-element.37), channel_id=1, source_target_pairs={{0,12},{1,13},{2,14},{3,15},{4,0},{5,1},{6,2},{7,3},{8,4},{9,5},{1... | collective-permute-start | bytes 393224 | tf_op jit(solution)/shard_map/ppermute | solution.py:316
  39.1 11.3 %collective-permute-start.14 = (bf16[128,512]{1,0:T(8,128)(2,1)S(1)}, bf16[128,512]{1,0:T(8,128)(2,1)S(1)}, u32[]{:S(2)}, u32[]{:S(2)}) collective-permute-start(bf16[128,512]{1,0:T(8,128)(2,1)S(1)} %get-tuple-element.38), channel_id=1, source_target_pairs={{0,14},{1,15},{2,0},{3,1},{4,2},{5,3},{6,4},{7,5},{8,6},{9,7},{10,... | collective-permute-start | bytes 393224 | tf_op jit(solution)/shard_map/ppermute | solution.py:316

commit v6 on v5

--- a/solution.py
+++ b/solution.py
@@ -111,6 +111,27 @@
         q2 = stacked(q_all, half, hs)
         do2 = stacked(do_all, half, hs)
         return q2, do2, dot(kall[half, :, c], q2, NT), dot(vall[half, :, c], do2, NT)
+
+    behind = None
+
+    def spread(ch, g, half, pb, db, q2, do2):
+        send = [1, 3, 4, 5] if half else [1, 2, 3, 4, 5]
+        to = slice(half * part, 4 * rows)
+        c = slice(g * HD, (g + 1) * HD)
+        dv = dot(jnp.concatenate([pb[n] for n in send], axis=0), do2, NN)
+        dk = dot(jnp.concatenate([db[n] for n in send], axis=0), q2, NN)
+        if todo[ch - 1][0] == g and ch > 0:
+            accv[to, :] += dv
+            acck[to, :] += dk
+        else:
+            accv[...] = dv
+            acck[...] = dk
+        if ch + 1 == len(todo) or todo[ch + 1][0] > g:
+            for w, acc in enumerate((acck, accv)):
+                far_ref[w, :, c] = acc[0:rows, :]
+                far_ref[2 + w, :, c] = acc[rows : 2 * rows, :]
+                swap_ref[2 + w, :, c] = acc[2 * rows : 3 * rows, :].astype(BF)
+                swap_ref[w, :, c] = acc[3 * rows : 4 * rows, :].astype(BF)
 
     todo = [(g, *x) for g in range(HK) for x in chunks()]
     for copy in fetch(0):
@@ -158,23 +179,10 @@
         if ch + 1 in cuts:
             for copy in store(cuts.index(ch + 1) - 1):
                 copy.start()
-        send = [1, 3, 4, 5] if half else [1, 2, 3, 4, 5]
-        to = slice(half * part, 4 * rows)
-        c = slice(g * HD, (g + 1) * HD)
-        dv = dot(jnp.concatenate([pb[n] for n in send], axis=0), do2, NN)
-        dk = dot(jnp.concatenate([db[n] for n in send], axis=0), q2, NN)
-        if todo[ch - 1][0] == g and ch > 0:
-            accv[to, :] += dv
-            acck[to, :] += dk
-        else:
-            accv[...] = dv
-            acck[...] = dk
-        if ch + 1 == len(todo) or todo[ch + 1][0] > g:
-            for w, acc in enumerate((acck, accv)):
-                far_ref[w, :, c] = acc[0:rows, :]
-                far_ref[2 + w, :, c] = acc[rows : 2 * rows, :]
-                swap_ref[2 + w, :, c] = acc[2 * rows : 3 * rows, :].astype(BF)
-                swap_ref[w, :, c] = acc[3 * rows : 4 * rows, :].astype(BF)
+        if behind is not None:
+            spread(*behind)
+        behind = (ch, g, half, pb, db, q2, do2)
+    spread(*behind)
     for n in range(len(cuts) - 1):
         for copy in store(n):
             copy.wait()

time: 52.2 us -> 51.9 us (level)
  no operation moved by 1% of the time
where the time goes in v6:
time: 51.9 us; the launch traced here: 51 us
  Pallas kernels  29 us (56%)
  starting transfers between devices  12.3 us (24%)
  waiting for transfers between devices  7.77 us (15%)
  other arithmetic  1.24 us (2%)
  between operations  0.72 us (1%)
    pallas_call x1, Pallas kernels, main_call(): pl.pallas_call(main_kernel, in_specs=[smem, smem, hbm, hbm, hbm] + [vmem]...  16.1 us
    ppermute x8, starting transfers between devices, moved(): return lax.ppermute(x, 'ctx', [(i, (i + by) % size) for i in range(size)])  10.4 us
    pallas_call x1, Pallas kernels, late_call(): pl.pallas_call(late_kernel, grid_spec=pltpu.PrefetchScalarGridSpec(num_sc...  8.5 us
    ppermute x8, waiting for transfers between devices, moved(): return lax.ppermute(x, 'ctx', [(i, (i + by) % size) for i in range(size)])  5.16 us
    pallas_call x1, Pallas kernels, delta_call(): pl.pallas_call(delta_kernel, grid=(HK,), in_specs=[big, big], out_specs=p...  4.46 us
    ppermute x7, waiting for transfers between devices, swapped(): return lax.ppermute(x, 'ctx', [(i, i ^ 1) for i in range(size)])  2.61 us
    ppermute x7, starting transfers between devices, swapped(): return lax.ppermute(x, 'ctx', [(i, i ^ 1) for i in range(size)])  1.91 us
  transfers between devices with their start and end apart: 15, of which 6 were waited for; matrix products, arithmetic and copies ran while one was open for 0% of the time, Pallas kernels for 25%

profile of v6, /device:TPU:6, one launch (start us, length us, event | category | flops | bytes accessed | tf_op | source)
XLA Modules:
  0.0 51.0 jit_solution(5698614250493774457)
XLA Ops:
  0.7 1.6 %collective-permute-start.1 = (bf16[128,512]{1,0:T(8,128)(2,1)}, bf16[128,512]{1,0:T(8,128)(2,1)S(1)}, u32[]{:S(2)}, u32[]{:S(2)}) collective-permute-start(bf16[128,512]{1,0:T(8,128)(2,1)} %refs_0_.3), channel_id=1, source_target_pairs={{0,2},{1,3},{2,4},{3,5},{4,6},{5,7},{6,8},{7,9},{8,10},{9,11},{10,... | collective-permute-start | bytes 393224 | tf_op jit(solution)/shard_map/ppermute | solution.py:324
  2.3 1.6 %collective-permute-start = (bf16[128,512]{1,0:T(8,128)(2,1)}, bf16[128,512]{1,0:T(8,128)(2,1)S(1)}, u32[]{:S(2)}, u32[]{:S(2)}) collective-permute-start(bf16[128,512]{1,0:T(8,128)(2,1)} %refs_0_.3), channel_id=1, source_target_pairs={{0,4},{1,5},{2,6},{3,7},{4,8},{5,9},{6,10},{7,11},{8,12},{9,13},{1... | collective-permute-start | bytes 393224 | tf_op jit(solution)/shard_map/ppermute | solution.py:324
  3.8 1.5 %collective-permute-start.3 = (bf16[128,512]{1,0:T(8,128)(2,1)}, bf16[128,512]{1,0:T(8,128)(2,1)S(1)}, u32[]{:S(2)}, u32[]{:S(2)}) collective-permute-start(bf16[128,512]{1,0:T(8,128)(2,1)} %refs_6_.1), channel_id=1, source_target_pairs={{0,2},{1,3},{2,4},{3,5},{4,6},{5,7},{6,8},{7,9},{8,10},{9,11},{10,... | collective-permute-start | bytes 393224 | tf_op jit(solution)/shard_map/ppermute | solution.py:324
  5.3 1.6 %collective-permute-start.2 = (bf16[128,512]{1,0:T(8,128)(2,1)}, bf16[128,512]{1,0:T(8,128)(2,1)S(1)}, u32[]{:S(2)}, u32[]{:S(2)}) collective-permute-start(bf16[128,512]{1,0:T(8,128)(2,1)} %refs_6_.1), channel_id=1, source_target_pairs={{0,4},{1,5},{2,6},{3,7},{4,8},{5,9},{6,10},{7,11},{8,12},{9,13},{1... | collective-permute-start | bytes 393224 | tf_op jit(solution)/shard_map/ppermute | solution.py:324
  6.9 4.5 %delta.1.delta_out_ref = f32[64,128]{1,0:T(8,128)} custom-call(bf16[128,8192]{1,0:T(8,128)(2,1)} %o_ref.1, bf16[128,8192]{1,0:T(8,128)(2,1)} %do_ref.5), custom_call_target="tpu_custom_call" | custom-call | flops 100000000 | bytes 4194304 | tf_op jit(solution)/shard_map/delta/pallas_call | solution.py:301
  11.4 0.0 collective-permute-done.1.refs_2_
  11.4 0.5 collective-permute-done.refs_1_
  11.9 0.0 collective-permute-start.5
  11.9 0.5 collective-permute-start.4
  12.4 0.0 collective-permute-start.9
  12.4 0.5 collective-permute-start.6
  12.9 3.5 %collective-permute-done.2.refs_7_ = bf16[128,512]{1,0:T(8,128)(2,1)S(1)} collective-permute-done((bf16[128,512]{1,0:T(8,128)(2,1)}, bf16[128,512]{1,0:T(8,128)(2,1)S(1)}, u32[]{:S(2)}, u32[]{:S(2)}) %collective-permute-start.2) | collective-permute-done | bytes 131104 | tf_op jit(solution)/shard_map/ppermute | solution.py:324
  16.4 0.0 collective-permute-done.5.refs_4_
  16.5 0.0 collective-permute-done.4.refs_3_
  16.5 0.0 collective-permute-start.8
  16.5 0.5 collective-permute-start.7
  17.0 0.0 collective-permute-done.9.refs_11_
  17.0 0.8 %collective-permute-done.8.refs_10_ = bf16[128,512]{1,0:T(8,128)(2,1)S(1)} collective-permute-done((bf16[128,512]{1,0:T(8,128)(2,1)S(1)}, bf16[128,512]{1,0:T(8,128)(2,1)S(1)}, u32[]{:S(2)}, u32[]{:S(2)}) %collective-permute-start.8) | collective-permute-done | bytes 131104 | tf_op jit(solution)/shard_map/ppermute | solution.py:329
  17.8 0.2 collective-permute-done.7.refs_9_
  18.0 16.1 %main.1 = (bf16[576,8192]{1,0:T(8,128)(2,1)}, bf16[128,8192]{1,0:T(8,128)(2,1)}, f32[4,128,512]{2,1,0:T(8,128)S(1)}, bf16[4,128,512]{2,1,0:T(8,128)(2,1)S(1)}) custom-call(s32[8]{0:T(128)S(1)} %copy-done.2, s32[1]{0:T(128)} %bitcast.place_ref, bf16[128,8192]{1,0:T(8,128)(2,1)} %q_ref.3, bf16[128,8192]{1,0:T(8,128)(2,1)} %do_ref.5, ...), custom_call_target="tpu_custom_call" | custom-call | flops 16000000000 | bytes 16777216 | tf_op jit(solution)/shard_map/main/pallas_call | solution.py:210
  34.1 0.4 collective-permute-start.10
  34.4 1.6 %collective-permute-done.10 = bf16[4,128,512]{2,1,0:T(8,128)(2,1)S(1)} collective-permute-done((bf16[4,128,512]{2,1,0:T(8,128)(2,1)S(1)}, bf16[4,128,512]{2,1,0:T(8,128)(2,1)S(1)}, u32[]{:S(2)}, u32[]{:S(2)}) %collective-permute-start.10) | collective-permute-done | bytes 524320 | tf_op jit(solution)/shard_map/ppermute | solution.py:329
  36.0 0.1 convert_element_type.45
  36.2 0.3 fusion.9
  36.4 1.8 %collective-permute-start.11 = (bf16[128,512]{1,0:T(8,128)(2,1)S(1)}, bf16[128,512]{1,0:T(8,128)(2,1)S(1)}, u32[]{:S(2)}, u32[]{:S(2)}) collective-permute-start(bf16[128,512]{1,0:T(8,128)(2,1)S(1)} %get-tuple-element.35), channel_id=1, source_target_pairs={{0,12},{1,13},{2,14},{3,15},{4,0},{5,1},{6,2},{7,3},{8,4},{9,5},{1... | collective-permute-start | bytes 393224 | tf_op jit(solution)/shard_map/ppermute | solution.py:324
  38.2 0.2 collective-permute-start.12
  38.4 0.5 collective-permute-start.13
  38.8 1.7 %collective-permute-start.14 = (bf16[128,512]{1,0:T(8,128)(2,1)S(1)}, bf16[128,512]{1,0:T(8,128)(2,1)S(1)}, u32[]{:S(2)}, u32[]{:S(2)}) collective-permute-start(bf16[128,512]{1,0:T(8,128)(2,1)S(1)} %get-tuple-element.38), channel_id=1, source_target_pairs={{0,14},{1,15},{2,0},{3,1},{4,2},{5,3},{6,4},{7,5},{8,6},{9,7},{10,... | collective-permute-start | bytes 393224 | tf_op jit(solution)/shard_map/ppermute | solution.py:324
  40.5 8.5 %late.1 = (bf16[128,8192]{1,0:T(8,128)(2,1)}, f32[2,128,512]{2,1,0:T(8,128)S(1)}) custom-call(s32[1]{0:T(128)} %bitcast.place_ref, bf16[128,8192]{1,0:T(8,128)(2,1)} %q_ref.3, bf16[128,8192]{1,0:T(8,128)(2,1)} %do_ref.5, bf16[576,8192]{1,0:T(8,128)(2,1)} %get-tuple-element.31.d_ref, bf16[128,8192]{1,0:T(8,128)(2,1)} %get-tuple-element.32.p_ref, ...), custom_call_target="tpu_custom_call" | custom-call | flops 8000000000 | bytes 20971520 | tf_op jit(solution)/shard_map/late/pallas_call | solution.py:270
  49.0 0.0 collective-permute-done.12
  49.1 1.1 %collective-permute-done.14 = bf16[128,512]{1,0:T(8,128)(2,1)S(1)} collective-permute-done((bf16[128,512]{1,0:T(8,128)(2,1)S(1)}, bf16[128,512]{1,0:T(8,128)(2,1)S(1)}, u32[]{:S(2)}, u32[]{:S(2)}) %collective-permute-start.14) | collective-permute-done | bytes 131104 | tf_op jit(solution)/shard_map/ppermute | solution.py:324
  50.2 0.9 %fusion.3 = (bf16[128,512]{1,0:T(8,128)(2,1)}, bf16[128,512]{1,0:T(8,128)(2,1)}) fusion(bf16[128,512]{1,0:T(8,128)(2,1)S(1)} %collective-permute-done.14, bf16[128,512]{1,0:T(8,128)(2,1)S(1)} %collective-permute-done.13, f32[2,128,512]{2,1,0:T(8,128)S(1)} %get-tuple-element.34, f32[4,128,512]{2,1,0:T(8,128)S(1)} %convert_element_type.45, pred[]{:T(512)S(6)} %eq.5, ...), kind=kLoop, calls=%fused_computation.6 | loop fusion | flops 917504 | bytes 1835009 | tf_op jit(solution)/shard_map/convert_element_type | solution.py:355
  (10 shorter events, 0.0 us)
Async XLA Ops:
  0.6 11.8 %copy-start.1 = (bf16[128,512]{1,0:T(8,128)(2,1)S(1)}, bf16[128,512]{1,0:T(8,128)(2,1)}, u32[]{:S(2)}) copy-start(bf16[128,512]{1,0:T(8,128)(2,1)} %refs_0_.3) | copy-start | bytes 393220
  0.6 11.8 %copy-start = (bf16[128,512]{1,0:T(8,128)(2,1)S(1)}, bf16[128,512]{1,0:T(8,128)(2,1)}, u32[]{:S(2)}) copy-start(bf16[128,512]{1,0:T(8,128)(2,1)} %refs_6_.1) | copy-start | bytes 393220
  0.7 17.3 %copy-start.2 = (s32[8]{0:T(128)S(1)}, s32[8]{0:T(128)}, u32[]{:S(2)}) copy-start(s32[8]{0:T(128)} %len_ref.1) | copy-start | bytes 100
  0.7 10.7 %collective-permute-start.1 = (bf16[128,512]{1,0:T(8,128)(2,1)}, bf16[128,512]{1,0:T(8,128)(2,1)S(1)}, u32[]{:S(2)}, u32[]{:S(2)}) collective-permute-start(bf16[128,512]{1,0:T(8,128)(2,1)} %refs_0_.3), channel_id=1, source_target_pairs={{0,2},{1,3},{2,4},{3,5},{4,6},{5,7},{6,8},{7,9},{8,10},{9,11},{10,... | collective-permute-start | bytes 393224 | tf_op jit(solution)/shard_map/ppermute | solution.py:324
  2.3 9.6 %collective-permute-start = (bf16[128,512]{1,0:T(8,128)(2,1)}, bf16[128,512]{1,0:T(8,128)(2,1)S(1)}, u32[]{:S(2)}, u32[]{:S(2)}) collective-permute-start(bf16[128,512]{1,0:T(8,128)(2,1)} %refs_0_.3), channel_id=1, source_target_pairs={{0,4},{1,5},{2,6},{3,7},{4,8},{5,9},{6,10},{7,11},{8,12},{9,13},{1... | collective-permute-start | bytes 393224 | tf_op jit(solution)/shard_map/ppermute | solution.py:324
  3.8 8.6 %collective-permute-start.3 = (bf16[128,512]{1,0:T(8,128)(2,1)}, bf16[128,512]{1,0:T(8,128)(2,1)S(1)}, u32[]{:S(2)}, u32[]{:S(2)}) collective-permute-start(bf16[128,512]{1,0:T(8,128)(2,1)} %refs_6_.1), channel_id=1, source_target_pairs={{0,2},{1,3},{2,4},{3,5},{4,6},{5,7},{6,8},{7,9},{8,10},{9,11},{10,... | collective-permute-start | bytes 393224 | tf_op jit(solution)/shard_map/ppermute | solution.py:324
  5.3 11.1 %collective-permute-start.2 = (bf16[128,512]{1,0:T(8,128)(2,1)}, bf16[128,512]{1,0:T(8,128)(2,1)S(1)}, u32[]{:S(2)}, u32[]{:S(2)}) collective-permute-start(bf16[128,512]{1,0:T(8,128)(2,1)} %refs_6_.1), channel_id=1, source_target_pairs={{0,4},{1,5},{2,6},{3,7},{4,8},{5,9},{6,10},{7,11},{8,12},{9,13},{1... | collective-permute-start | bytes 393224 | tf_op jit(solution)/shard_map/ppermute | solution.py:324
  11.9 4.6 %collective-permute-start.5 = (bf16[128,512]{1,0:T(8,128)(2,1)S(1)}, bf16[128,512]{1,0:T(8,128)(2,1)S(1)}, u32[]{:S(2)}, u32[]{:S(2)}) collective-permute-start(bf16[128,512]{1,0:T(8,128)(2,1)S(1)} %collective-permute-done.refs_1_), channel_id=1, source_target_pairs={{0,1},{1,0},{2,3},{3,2},{4,5},{5,4},{6,7},{7,6},{8,9},{9,8},{10,11... | collective-permute-start | bytes 393224 | tf_op jit(solution)/shard_map/ppermute | solution.py:329
  11.9 4.6 %collective-permute-start.4 = (bf16[128,512]{1,0:T(8,128)(2,1)S(1)}, bf16[128,512]{1,0:T(8,128)(2,1)S(1)}, u32[]{:S(2)}, u32[]{:S(2)}) collective-permute-start(bf16[128,512]{1,0:T(8,128)(2,1)S(1)} %collective-permute-done.1.refs_2_), channel_id=1, source_target_pairs={{0,1},{1,0},{2,3},{3,2},{4,5},{5,4},{6,7},{7,6},{8,9},{9,8},{10,11... | collective-permute-start | bytes 393224 | tf_op jit(solution)/shard_map/ppermute | solution.py:329
  12.4 4.6 %collective-permute-start.9 = (bf16[128,512]{1,0:T(8,128)(2,1)S(1)}, bf16[128,512]{1,0:T(8,128)(2,1)S(1)}, u32[]{:S(2)}, u32[]{:S(2)}) collective-permute-start(bf16[128,512]{1,0:T(8,128)(2,1)S(1)} %copy-done), channel_id=1, source_target_pairs={{0,1},{1,0},{2,3},{3,2},{4,5},{5,4},{6,7},{7,6},{8,9},{9,8},{10,11... | collective-permute-start | bytes 393224 | tf_op jit(solution)/shard_map/ppermute | solution.py:329
  12.4 4.6 %collective-permute-start.6 = (bf16[128,512]{1,0:T(8,128)(2,1)S(1)}, bf16[128,512]{1,0:T(8,128)(2,1)S(1)}, u32[]{:S(2)}, u32[]{:S(2)}) collective-permute-start(bf16[128,512]{1,0:T(8,128)(2,1)S(1)} %copy-done.1), channel_id=1, source_target_pairs={{0,1},{1,0},{2,3},{3,2},{4,5},{5,4},{6,7},{7,6},{8,9},{9,8},{10,11... | collective-permute-start | bytes 393224 | tf_op jit(solution)/shard_map/ppermute | solution.py:329
  16.5 1.4 %collective-permute-start.8 = (bf16[128,512]{1,0:T(8,128)(2,1)S(1)}, bf16[128,512]{1,0:T(8,128)(2,1)S(1)}, u32[]{:S(2)}, u32[]{:S(2)}) collective-permute-start(bf16[128,512]{1,0:T(8,128)(2,1)S(1)} %collective-permute-done.2.refs_7_), channel_id=1, source_target_pairs={{0,1},{1,0},{2,3},{3,2},{4,5},{5,4},{6,7},{7,6},{8,9},{9,8},{10,11... | collective-permute-start | bytes 393224 | tf_op jit(solution)/shard_map/ppermute | solution.py:329
  16.5 1.5 %collective-permute-start.7 = (bf16[128,512]{1,0:T(8,128)(2,1)S(1)}, bf16[128,512]{1,0:T(8,128)(2,1)S(1)}, u32[]{:S(2)}, u32[]{:S(2)}) collective-permute-start(bf16[128,512]{1,0:T(8,128)(2,1)S(1)} %collective-permute-done.3.refs_8_), channel_id=1, source_target_pairs={{0,1},{1,0},{2,3},{3,2},{4,5},{5,4},{6,7},{7,6},{8,9},{9,8},{10,11... | collective-permute-start | bytes 393224 | tf_op jit(solution)/shard_map/ppermute | solution.py:329
  34.1 2.0 %collective-permute-start.10 = (bf16[4,128,512]{2,1,0:T(8,128)(2,1)S(1)}, bf16[4,128,512]{2,1,0:T(8,128)(2,1)S(1)}, u32[]{:S(2)}, u32[]{:S(2)}) collective-permute-start(bf16[4,128,512]{2,1,0:T(8,128)(2,1)S(1)} %get-tuple-element.29), channel_id=1, source_target_pairs={{0,1},{1,0},{2,3},{3,2},{4,5},{5,4},{6,7},{7,6},{8,9},{9,8},{10,11... | collective-permute-start | bytes 1572872 | tf_op jit(solution)/shard_map/ppermute | solution.py:329
  36.4 12.6 %collective-permute-start.11 = (bf16[128,512]{1,0:T(8,128)(2,1)S(1)}, bf16[128,512]{1,0:T(8,128)(2,1)S(1)}, u32[]{:S(2)}, u32[]{:S(2)}) collective-permute-start(bf16[128,512]{1,0:T(8,128)(2,1)S(1)} %get-tuple-element.35), channel_id=1, source_target_pairs={{0,12},{1,13},{2,14},{3,15},{4,0},{5,1},{6,2},{7,3},{8,4},{9,5},{1... | collective-permute-start | bytes 393224 | tf_op jit(solution)/shard_map/ppermute | solution.py:324
  38.2 10.9 %collective-permute-start.12 = (bf16[128,512]{1,0:T(8,128)(2,1)S(1)}, bf16[128,512]{1,0:T(8,128)(2,1)S(1)}, u32[]{:S(2)}, u32[]{:S(2)}) collective-permute-start(bf16[128,512]{1,0:T(8,128)(2,1)S(1)} %get-tuple-element.36), channel_id=1, source_target_pairs={{0,14},{1,15},{2,0},{3,1},{4,2},{5,3},{6,4},{7,5},{8,6},{9,7},{10,... | collective-permute-start | bytes 393224 | tf_op jit(solution)/shard_map/ppermute | solution.py:324
  38.4 10.7 %collective-permute-start.13 = (bf16[128,512]{1,0:T(8,128)(2,1)S(1)}, bf16[128,512]{1,0:T(8,128)(2,1)S(1)}, u32[]{:S(2)}, u32[]{:S(2)}) collective-permute-start(bf16[128,512]{1,0:T(8,128)(2,1)S(1)} %get-tuple-element.37), channel_id=1, source_target_pairs={{0,12},{1,13},{2,14},{3,15},{4,0},{5,1},{6,2},{7,3},{8,4},{9,5},{1... | collective-permute-start | bytes 393224 | tf_op jit(solution)/shard_map/ppermute | solution.py:324
  38.8 11.3 %collective-permute-start.14 = (bf16[128,512]{1,0:T(8,128)(2,1)S(1)}, bf16[128,512]{1,0:T(8,128)(2,1)S(1)}, u32[]{:S(2)}, u32[]{:S(2)}) collective-permute-start(bf16[128,512]{1,0:T(8,128)(2,1)S(1)} %get-tuple-element.38), channel_id=1, source_target_pairs={{0,14},{1,15},{2,0},{3,1},{4,2},{5,3},{6,4},{7,5},{8,6},{9,7},{10,... | collective-permute-start | bytes 393224 | tf_op jit(solution)/shard_map/ppermute | solution.py:324

commit v7 on v6

--- a/solution.py
+++ b/solution.py
@@ -345,14 +345,14 @@
     ks = (keys, k4, k2, k2s, k4s, km)
     vs = (values, v4, v2, swapped(v2), swapped(v4), vm)
     grads, probs, far, swap = main_call(lengths, index, queries, d_out, delta, ks, vs)
-    back = swapped(swap).astype(F32)
+    back = swapped(swap)
     near, mid = back[0:2], back[2:4]
-    far4 = [(far[w] + jnp.where(even, 0.0, near[w])).astype(BF) for w in range(2)]
-    far2 = [(far[2 + w] + mid[w]).astype(BF) for w in range(2)]
+    far4 = [(far[w] + jnp.where(even, 0.0, near[w].astype(F32))).astype(BF) for w in range(2)]
+    far2 = [(far[2 + w] + mid[w].astype(F32)).astype(BF) for w in range(2)]
     index, *both = lax.optimization_barrier((index, *far4, *far2))
     got = [moved(x, -4 if i < 2 else -2).astype(F32) for i, x in enumerate(both)]
     d_queries, own = late_call(index, queries, d_out, grads, probs, ks)
-    total = [(own[w] + jnp.where(even, near[w], 0.0) + got[w] + got[2 + w]).astype(BF) for w in range(2)]
+    total = [(own[w] + jnp.where(even, near[w].astype(F32), 0.0) + got[w] + got[2 + w]).astype(BF) for w in range(2)]
     return d_queries, total[0], total[1]
 
 

time: 51.9 us -> 51.7 us (level)
    convert_element_type x3 -> x2, other arithmetic: 1.24 us -> 1.02 us  [the longest x1 0.86 us: on_device(): (own[w] + jnp.where(even, near[w].astype(F32), 0.0) + got[w] + got[2 + w]...]
  transfers between devices with their start and end apart: 15 -> 15, of which waited for: 6 -> 6; matrix products, arithmetic and copies ran while one was open for 0% -> 0% of each run, Pallas kernels for 25% -> 26%
where the time goes in v7:
time: 51.7 us; the launch traced here: 50.8 us
  Pallas kernels  29 us (56%)
  starting transfers between devices  12.3 us (24%)
  waiting for transfers between devices  7.77 us (15%)
  other arithmetic  1.02 us (2%)
  between operations  0.71 us (1%)
    pallas_call x1, Pallas kernels, main_call(): pl.pallas_call(main_kernel, in_specs=[smem, smem, hbm, hbm, hbm] + [vmem]...  16.1 us
    ppermute x8, starting transfers between devices, moved(): return lax.ppermute(x, 'ctx', [(i, (i + by) % size) for i in range(size)])  10.4 us
    pallas_call x1, Pallas kernels, late_call(): pl.pallas_call(late_kernel, grid_spec=pltpu.PrefetchScalarGridSpec(num_sc...  8.5 us
    ppermute x8, waiting for transfers between devices, moved(): return lax.ppermute(x, 'ctx', [(i, (i + by) % size) for i in range(size)])  5.15 us
    pallas_call x1, Pallas kernels, delta_call(): pl.pallas_call(delta_kernel, grid=(HK,), in_specs=[big, big], out_specs=p...  4.46 us
    ppermute x7, waiting for transfers between devices, swapped(): return lax.ppermute(x, 'ctx', [(i, i ^ 1) for i in range(size)])  2.61 us
    ppermute x7, starting transfers between devices, swapped(): return lax.ppermute(x, 'ctx', [(i, i ^ 1) for i in range(size)])  1.91 us
  transfers between devices with their start and end apart: 15, of which 6 were waited for; matrix products, arithmetic and copies ran while one was open for 0% of the time, Pallas kernels for 26%

profile of v7, /device:TPU:6, one launch (start us, length us, event | category | flops | bytes accessed | tf_op | source)
XLA Modules:
  0.0 50.8 jit_solution(13415079828109941020)
XLA Ops:
  0.7 1.6 %collective-permute-start.1 = (bf16[128,512]{1,0:T(8,128)(2,1)}, bf16[128,512]{1,0:T(8,128)(2,1)S(1)}, u32[]{:S(2)}, u32[]{:S(2)}) collective-permute-start(bf16[128,512]{1,0:T(8,128)(2,1)} %refs_0_.3), channel_id=1, source_target_pairs={{0,2},{1,3},{2,4},{3,5},{4,6},{5,7},{6,8},{7,9},{8,10},{9,11},{10,... | collective-permute-start | bytes 393224 | tf_op jit(solution)/shard_map/ppermute | solution.py:324
  2.3 1.6 %collective-permute-start = (bf16[128,512]{1,0:T(8,128)(2,1)}, bf16[128,512]{1,0:T(8,128)(2,1)S(1)}, u32[]{:S(2)}, u32[]{:S(2)}) collective-permute-start(bf16[128,512]{1,0:T(8,128)(2,1)} %refs_0_.3), channel_id=1, source_target_pairs={{0,4},{1,5},{2,6},{3,7},{4,8},{5,9},{6,10},{7,11},{8,12},{9,13},{1... | collective-permute-start | bytes 393224 | tf_op jit(solution)/shard_map/ppermute | solution.py:324
  3.8 1.5 %collective-permute-start.3 = (bf16[128,512]{1,0:T(8,128)(2,1)}, bf16[128,512]{1,0:T(8,128)(2,1)S(1)}, u32[]{:S(2)}, u32[]{:S(2)}) collective-permute-start(bf16[128,512]{1,0:T(8,128)(2,1)} %refs_6_.1), channel_id=1, source_target_pairs={{0,2},{1,3},{2,4},{3,5},{4,6},{5,7},{6,8},{7,9},{8,10},{9,11},{10,... | collective-permute-start | bytes 393224 | tf_op jit(solution)/shard_map/ppermute | solution.py:324
  5.3 1.6 %collective-permute-start.2 = (bf16[128,512]{1,0:T(8,128)(2,1)}, bf16[128,512]{1,0:T(8,128)(2,1)S(1)}, u32[]{:S(2)}, u32[]{:S(2)}) collective-permute-start(bf16[128,512]{1,0:T(8,128)(2,1)} %refs_6_.1), channel_id=1, source_target_pairs={{0,4},{1,5},{2,6},{3,7},{4,8},{5,9},{6,10},{7,11},{8,12},{9,13},{1... | collective-permute-start | bytes 393224 | tf_op jit(solution)/shard_map/ppermute | solution.py:324
  6.9 4.5 %delta.1.delta_out_ref = f32[64,128]{1,0:T(8,128)} custom-call(bf16[128,8192]{1,0:T(8,128)(2,1)} %o_ref.1, bf16[128,8192]{1,0:T(8,128)(2,1)} %do_ref.5), custom_call_target="tpu_custom_call" | custom-call | flops 100000000 | bytes 4194304 | tf_op jit(solution)/shard_map/delta/pallas_call | solution.py:301
  11.4 0.0 collective-permute-done.1.refs_2_
  11.4 0.5 collective-permute-done.refs_1_
  11.9 0.0 collective-permute-start.5
  11.9 0.5 collective-permute-start.4
  12.4 0.0 collective-permute-start.9
  12.4 0.5 collective-permute-start.6
  12.9 3.5 %collective-permute-done.2.refs_7_ = bf16[128,512]{1,0:T(8,128)(2,1)S(1)} collective-permute-done((bf16[128,512]{1,0:T(8,128)(2,1)}, bf16[128,512]{1,0:T(8,128)(2,1)S(1)}, u32[]{:S(2)}, u32[]{:S(2)}) %collective-permute-start.2) | collective-permute-done | bytes 131104 | tf_op jit(solution)/shard_map/ppermute | solution.py:324
  16.4 0.0 collective-permute-done.5.refs_4_
  16.5 0.0 collective-permute-done.4.refs_3_
  16.5 0.0 collective-permute-start.8
  16.5 0.5 collective-permute-start.7
  17.0 0.0 collective-permute-done.9.refs_11_
  17.0 0.8 %collective-permute-done.8.refs_10_ = bf16[128,512]{1,0:T(8,128)(2,1)S(1)} collective-permute-done((bf16[128,512]{1,0:T(8,128)(2,1)S(1)}, bf16[128,512]{1,0:T(8,128)(2,1)S(1)}, u32[]{:S(2)}, u32[]{:S(2)}) %collective-permute-start.8) | collective-permute-done | bytes 131104 | tf_op jit(solution)/shard_map/ppermute | solution.py:329
  17.8 0.2 collective-permute-done.7.refs_9_
  18.0 16.1 %main.1 = (bf16[576,8192]{1,0:T(8,128)(2,1)}, bf16[128,8192]{1,0:T(8,128)(2,1)}, f32[4,128,512]{2,1,0:T(8,128)S(1)}, bf16[4,128,512]{2,1,0:T(8,128)(2,1)S(1)}) custom-call(s32[8]{0:T(128)S(1)} %copy-done.2, s32[1]{0:T(128)} %bitcast.place_ref, bf16[128,8192]{1,0:T(8,128)(2,1)} %q_ref.3, bf16[128,8192]{1,0:T(8,128)(2,1)} %do_ref.5, ...), custom_call_target="tpu_custom_call" | custom-call | flops 16000000000 | bytes 16777216 | tf_op jit(solution)/shard_map/main/pallas_call | solution.py:210
  34.1 0.4 collective-permute-start.10
  34.4 1.6 %collective-permute-done.10 = bf16[4,128,512]{2,1,0:T(8,128)(2,1)S(1)} collective-permute-done((bf16[4,128,512]{2,1,0:T(8,128)(2,1)S(1)}, bf16[4,128,512]{2,1,0:T(8,128)(2,1)S(1)}, u32[]{:S(2)}, u32[]{:S(2)}) %collective-permute-start.10) | collective-permute-done | bytes 524320 | tf_op jit(solution)/shard_map/ppermute | solution.py:329
  36.0 0.2 fusion.15
  36.2 1.8 %collective-permute-start.11 = (bf16[128,512]{1,0:T(8,128)(2,1)S(1)}, bf16[128,512]{1,0:T(8,128)(2,1)S(1)}, u32[]{:S(2)}, u32[]{:S(2)}) collective-permute-start(bf16[128,512]{1,0:T(8,128)(2,1)S(1)} %get-tuple-element.35), channel_id=1, source_target_pairs={{0,12},{1,13},{2,14},{3,15},{4,0},{5,1},{6,2},{7,3},{8,4},{9,5},{1... | collective-permute-start | bytes 393224 | tf_op jit(solution)/shard_map/ppermute | solution.py:324
  38.0 0.2 collective-permute-start.12
  38.2 0.5 collective-permute-start.13
  38.6 1.7 %collective-permute-start.14 = (bf16[128,512]{1,0:T(8,128)(2,1)S(1)}, bf16[128,512]{1,0:T(8,128)(2,1)S(1)}, u32[]{:S(2)}, u32[]{:S(2)}) collective-permute-start(bf16[128,512]{1,0:T(8,128)(2,1)S(1)} %get-tuple-element.38), channel_id=1, source_target_pairs={{0,14},{1,15},{2,0},{3,1},{4,2},{5,3},{6,4},{7,5},{8,6},{9,7},{10,... | collective-permute-start | bytes 393224 | tf_op jit(solution)/shard_map/ppermute | solution.py:324
  40.3 8.5 %late.1 = (bf16[128,8192]{1,0:T(8,128)(2,1)}, f32[2,128,512]{2,1,0:T(8,128)S(1)}) custom-call(s32[1]{0:T(128)} %bitcast.place_ref, bf16[128,8192]{1,0:T(8,128)(2,1)} %q_ref.3, bf16[128,8192]{1,0:T(8,128)(2,1)} %do_ref.5, bf16[576,8192]{1,0:T(8,128)(2,1)} %get-tuple-element.31.d_ref, bf16[128,8192]{1,0:T(8,128)(2,1)} %get-tuple-element.32.p_ref, ...), custom_call_target="tpu_custom_call" | custom-call | flops 8000000000 | bytes 20971520 | tf_op jit(solution)/shard_map/late/pallas_call | solution.py:270
  48.8 0.0 collective-permute-done.11
  48.8 0.0 collective-permute-done.12
  48.8 1.1 %collective-permute-done.14 = bf16[128,512]{1,0:T(8,128)(2,1)S(1)} collective-permute-done((bf16[128,512]{1,0:T(8,128)(2,1)S(1)}, bf16[128,512]{1,0:T(8,128)(2,1)S(1)}, u32[]{:S(2)}, u32[]{:S(2)}) %collective-permute-start.14) | collective-permute-done | bytes 131104 | tf_op jit(solution)/shard_map/ppermute | solution.py:324
  49.9 0.9 %fusion.13 = (bf16[128,512]{1,0:T(8,128)(2,1)}, bf16[128,512]{1,0:T(8,128)(2,1)}) fusion(bf16[128,512]{1,0:T(8,128)(2,1)S(1)} %collective-permute-done.14, bf16[128,512]{1,0:T(8,128)(2,1)S(1)} %collective-permute-done.13, f32[2,128,512]{2,1,0:T(8,128)S(1)} %get-tuple-element.34, pred[]{:T(512)S(6)} %eq.5, ...), kind=kLoop, calls=%fused_computation.17 | loop fusion | flops 1048576 | bytes 1572865 | tf_op jit(solution)/shard_map/convert_element_type | solution.py:355
  (9 shorter events, 0.0 us)
Async XLA Ops:
  0.6 11.8 %copy-start.1 = (bf16[128,512]{1,0:T(8,128)(2,1)S(1)}, bf16[128,512]{1,0:T(8,128)(2,1)}, u32[]{:S(2)}) copy-start(bf16[128,512]{1,0:T(8,128)(2,1)} %refs_0_.3) | copy-start | bytes 393220
  0.6 11.8 %copy-start = (bf16[128,512]{1,0:T(8,128)(2,1)S(1)}, bf16[128,512]{1,0:T(8,128)(2,1)}, u32[]{:S(2)}) copy-start(bf16[128,512]{1,0:T(8,128)(2,1)} %refs_6_.1) | copy-start | bytes 393220
  0.7 17.3 %copy-start.2 = (s32[8]{0:T(128)S(1)}, s32[8]{0:T(128)}, u32[]{:S(2)}) copy-start(s32[8]{0:T(128)} %len_ref.1) | copy-start | bytes 100
  0.7 10.7 %collective-permute-start.1 = (bf16[128,512]{1,0:T(8,128)(2,1)}, bf16[128,512]{1,0:T(8,128)(2,1)S(1)}, u32[]{:S(2)}, u32[]{:S(2)}) collective-permute-start(bf16[128,512]{1,0:T(8,128)(2,1)} %refs_0_.3), channel_id=1, source_target_pairs={{0,2},{1,3},{2,4},{3,5},{4,6},{5,7},{6,8},{7,9},{8,10},{9,11},{10,... | collective-permute-start | bytes 393224 | tf_op jit(solution)/shard_map/ppermute | solution.py:324
  2.3 9.6 %collective-permute-start = (bf16[128,512]{1,0:T(8,128)(2,1)}, bf16[128,512]{1,0:T(8,128)(2,1)S(1)}, u32[]{:S(2)}, u32[]{:S(2)}) collective-permute-start(bf16[128,512]{1,0:T(8,128)(2,1)} %refs_0_.3), channel_id=1, source_target_pairs={{0,4},{1,5},{2,6},{3,7},{4,8},{5,9},{6,10},{7,11},{8,12},{9,13},{1... | collective-permute-start | bytes 393224 | tf_op jit(solution)/shard_map/ppermute | solution.py:324
  3.8 8.6 %collective-permute-start.3 = (bf16[128,512]{1,0:T(8,128)(2,1)}, bf16[128,512]{1,0:T(8,128)(2,1)S(1)}, u32[]{:S(2)}, u32[]{:S(2)}) collective-permute-start(bf16[128,512]{1,0:T(8,128)(2,1)} %refs_6_.1), channel_id=1, source_target_pairs={{0,2},{1,3},{2,4},{3,5},{4,6},{5,7},{6,8},{7,9},{8,10},{9,11},{10,... | collective-permute-start | bytes 393224 | tf_op jit(solution)/shard_map/ppermute | solution.py:324
  5.3 11.1 %collective-permute-start.2 = (bf16[128,512]{1,0:T(8,128)(2,1)}, bf16[128,512]{1,0:T(8,128)(2,1)S(1)}, u32[]{:S(2)}, u32[]{:S(2)}) collective-permute-start(bf16[128,512]{1,0:T(8,128)(2,1)} %refs_6_.1), channel_id=1, source_target_pairs={{0,4},{1,5},{2,6},{3,7},{4,8},{5,9},{6,10},{7,11},{8,12},{9,13},{1... | collective-permute-start | bytes 393224 | tf_op jit(solution)/shard_map/ppermute | solution.py:324
  11.9 4.6 %collective-permute-start.5 = (bf16[128,512]{1,0:T(8,128)(2,1)S(1)}, bf16[128,512]{1,0:T(8,128)(2,1)S(1)}, u32[]{:S(2)}, u32[]{:S(2)}) collective-permute-start(bf16[128,512]{1,0:T(8,128)(2,1)S(1)} %collective-permute-done.refs_1_), channel_id=1, source_target_pairs={{0,1},{1,0},{2,3},{3,2},{4,5},{5,4},{6,7},{7,6},{8,9},{9,8},{10,11... | collective-permute-start | bytes 393224 | tf_op jit(solution)/shard_map/ppermute | solution.py:329
  11.9 4.6 %collective-permute-start.4 = (bf16[128,512]{1,0:T(8,128)(2,1)S(1)}, bf16[128,512]{1,0:T(8,128)(2,1)S(1)}, u32[]{:S(2)}, u32[]{:S(2)}) collective-permute-start(bf16[128,512]{1,0:T(8,128)(2,1)S(1)} %collective-permute-done.1.refs_2_), channel_id=1, source_target_pairs={{0,1},{1,0},{2,3},{3,2},{4,5},{5,4},{6,7},{7,6},{8,9},{9,8},{10,11... | collective-permute-start | bytes 393224 | tf_op jit(solution)/shard_map/ppermute | solution.py:329
  12.4 4.6 %collective-permute-start.9 = (bf16[128,512]{1,0:T(8,128)(2,1)S(1)}, bf16[128,512]{1,0:T(8,128)(2,1)S(1)}, u32[]{:S(2)}, u32[]{:S(2)}) collective-permute-start(bf16[128,512]{1,0:T(8,128)(2,1)S(1)} %copy-done), channel_id=1, source_target_pairs={{0,1},{1,0},{2,3},{3,2},{4,5},{5,4},{6,7},{7,6},{8,9},{9,8},{10,11... | collective-permute-start | bytes 393224 | tf_op jit(solution)/shard_map/ppermute | solution.py:329
  12.4 4.6 %collective-permute-start.6 = (bf16[128,512]{1,0:T(8,128)(2,1)S(1)}, bf16[128,512]{1,0:T(8,128)(2,1)S(1)}, u32[]{:S(2)}, u32[]{:S(2)}) collective-permute-start(bf16[128,512]{1,0:T(8,128)(2,1)S(1)} %copy-done.1), channel_id=1, source_target_pairs={{0,1},{1,0},{2,3},{3,2},{4,5},{5,4},{6,7},{7,6},{8,9},{9,8},{10,11... | collective-permute-start | bytes 393224 | tf_op jit(solution)/shard_map/ppermute | solution.py:329
  16.5 1.4 %collective-permute-start.8 = (bf16[128,512]{1,0:T(8,128)(2,1)S(1)}, bf16[128,512]{1,0:T(8,128)(2,1)S(1)}, u32[]{:S(2)}, u32[]{:S(2)}) collective-permute-start(bf16[128,512]{1,0:T(8,128)(2,1)S(1)} %collective-permute-done.2.refs_7_), channel_id=1, source_target_pairs={{0,1},{1,0},{2,3},{3,2},{4,5},{5,4},{6,7},{7,6},{8,9},{9,8},{10,11... | collective-permute-start | bytes 393224 | tf_op jit(solution)/shard_map/ppermute | solution.py:329
  16.5 1.5 %collective-permute-start.7 = (bf16[128,512]{1,0:T(8,128)(2,1)S(1)}, bf16[128,512]{1,0:T(8,128)(2,1)S(1)}, u32[]{:S(2)}, u32[]{:S(2)}) collective-permute-start(bf16[128,512]{1,0:T(8,128)(2,1)S(1)} %collective-permute-done.3.refs_8_), channel_id=1, source_target_pairs={{0,1},{1,0},{2,3},{3,2},{4,5},{5,4},{6,7},{7,6},{8,9},{9,8},{10,11... | collective-permute-start | bytes 393224 | tf_op jit(solution)/shard_map/ppermute | solution.py:329
  34.1 2.0 %collective-permute-start.10 = (bf16[4,128,512]{2,1,0:T(8,128)(2,1)S(1)}, bf16[4,128,512]{2,1,0:T(8,128)(2,1)S(1)}, u32[]{:S(2)}, u32[]{:S(2)}) collective-permute-start(bf16[4,128,512]{2,1,0:T(8,128)(2,1)S(1)} %get-tuple-element.29), channel_id=1, source_target_pairs={{0,1},{1,0},{2,3},{3,2},{4,5},{5,4},{6,7},{7,6},{8,9},{9,8},{10,11... | collective-permute-start | bytes 1572872 | tf_op jit(solution)/shard_map/ppermute | solution.py:329
  36.2 12.6 %collective-permute-start.11 = (bf16[128,512]{1,0:T(8,128)(2,1)S(1)}, bf16[128,512]{1,0:T(8,128)(2,1)S(1)}, u32[]{:S(2)}, u32[]{:S(2)}) collective-permute-start(bf16[128,512]{1,0:T(8,128)(2,1)S(1)} %get-tuple-element.35), channel_id=1, source_target_pairs={{0,12},{1,13},{2,14},{3,15},{4,0},{5,1},{6,2},{7,3},{8,4},{9,5},{1... | collective-permute-start | bytes 393224 | tf_op jit(solution)/shard_map/ppermute | solution.py:324
  38.0 10.9 %collective-permute-start.12 = (bf16[128,512]{1,0:T(8,128)(2,1)S(1)}, bf16[128,512]{1,0:T(8,128)(2,1)S(1)}, u32[]{:S(2)}, u32[]{:S(2)}) collective-permute-start(bf16[128,512]{1,0:T(8,128)(2,1)S(1)} %get-tuple-element.36), channel_id=1, source_target_pairs={{0,14},{1,15},{2,0},{3,1},{4,2},{5,3},{6,4},{7,5},{8,6},{9,7},{10,... | collective-permute-start | bytes 393224 | tf_op jit(solution)/shard_map/ppermute | solution.py:324
  38.2 10.7 %collective-permute-start.13 = (bf16[128,512]{1,0:T(8,128)(2,1)S(1)}, bf16[128,512]{1,0:T(8,128)(2,1)S(1)}, u32[]{:S(2)}, u32[]{:S(2)}) collective-permute-start(bf16[128,512]{1,0:T(8,128)(2,1)S(1)} %get-tuple-element.37), channel_id=1, source_target_pairs={{0,12},{1,13},{2,14},{3,15},{4,0},{5,1},{6,2},{7,3},{8,4},{9,5},{1... | collective-permute-start | bytes 393224 | tf_op jit(solution)/shard_map/ppermute | solution.py:324
  38.6 11.3 %collective-permute-start.14 = (bf16[128,512]{1,0:T(8,128)(2,1)S(1)}, bf16[128,512]{1,0:T(8,128)(2,1)S(1)}, u32[]{:S(2)}, u32[]{:S(2)}) collective-permute-start(bf16[128,512]{1,0:T(8,128)(2,1)S(1)} %get-tuple-element.38), channel_id=1, source_target_pairs={{0,14},{1,15},{2,0},{3,1},{4,2},{5,3},{6,4},{7,5},{8,6},{9,7},{10,... | collective-permute-start | bytes 393224 | tf_op jit(solution)/shard_map/ppermute | solution.py:324
